TPU v7x, 32 devices: a whole 2x2x4 slice. The times are simulated.
32 devices in a mesh: seq: 8 (over z, x), rep: 4 (over y, core).
Axes of the slice: x: 2, y: 2, z: 4, core: 2. Of those that a mesh axis runs over, the one named last changes fastest.
Arguments:
- query_in: bfloat16 [4, 1024, 1024], P('rep', 'seq'), may hold values from -120 to 120
- key_in: bfloat16 [4, 1024, 1024], P('rep', 'seq'), may hold values from -4 to 4
- value_in: bfloat16 [4, 1024, 1024], P('rep', 'seq'), may hold values from -6 to 6
- out_weight: bfloat16 [1024, 2048], replicated, may hold values from -0.1875 to 0.1875
- grad_out: bfloat16 [4, 1024, 2048], P('rep', 'seq'), may hold values from -6 to 6
- pattern: int32 [16, 8], replicated, may hold values from 0 to 15, as said below
Outputs:
- mixed_out: bfloat16 [4, 1024, 2048], P('rep', 'seq')
- query_grad: bfloat16 [4, 1024, 1024], P('rep', 'seq')
- key_grad: bfloat16 [4, 1024, 1024], P('rep', 'seq')
- value_grad: bfloat16 [4, 1024, 1024], P('rep', 'seq')
- weight_grad: float32 [1024, 2048], P('seq')
Inputs may be any that keep to these rules, and one draw needn't show every extreme that they name: `pattern`: row b names blocks b - 1, b and b + 1 modulo 16 in columns 0 to 2; columns 3 and 4 hold the same two blocks in every row; the other columns may name any block.
All inputs are finite; a program needn't handle non-finite values.
Results may differ from a plain program's by a relative error of at most 0.0095.
Values may be sent and summed in bfloat16 or wider, within the bound.
No kernel may reach another device: no remote copies, remote signals or barrier semaphores. Data moves between devices by JAX's collectives and lax.ppermute only.
A program may use at most 128 MiB of HBM per device.

v0:
```python
import math

import jax
import jax.numpy as jnp
from jax import lax
from jax.sharding import PartitionSpec as P

HD = 128
BLK = 64


def local(query_in, key_in, value_in, out_weight, grad_out, pattern):
    seq_count = lax.axis_size("seq")
    rep_count = lax.axis_size("rep")
    tokens_here = query_in.shape[1]
    width = query_in.shape[2]
    head_size = HD
    head_count = width // head_size
    groups = max(seq_count // head_count, 1)
    per_device = max(head_count // seq_count, 1)
    head_groups = head_count // per_device
    local_blocks = tokens_here // BLK
    group_rows = BLK // groups
    all_blocks = seq_count * local_blocks
    columns = per_device * head_size
    span = pattern.shape[1]
    block_run = math.gcd(all_blocks, 32)
    run_count = all_blocks // block_run
    scale = 1.0 / math.sqrt(head_size)

    def to_heads(source):
        shaped = source.reshape(local_blocks, groups, group_rows, head_groups, columns)
        return shaped.transpose(3, 1, 0, 2, 4).reshape(
            seq_count, local_blocks * group_rows, columns
        )

    def to_tokens(source):
        shaped = source.reshape(head_groups, groups, local_blocks, group_rows, columns)
        return shaped.transpose(2, 1, 3, 0, 4).reshape(tokens_here, width)

    query_local = query_in[0]
    key_local = key_in[0]
    value_local = value_in[0]
    grad_local = grad_out[0]

    def spread(source):
        grouped = source.reshape(tokens_here, head_groups, columns).transpose(1, 0, 2)
        copies = jnp.broadcast_to(grouped[:, None], (head_groups, groups, tokens_here, columns))
        return copies.reshape(seq_count, tokens_here, columns)

    query_heads, key_all, value_all = (
        lax.all_to_all(to_heads(query_local), "seq", split_axis=0, concat_axis=0, tiled=True),
        lax.all_to_all(spread(key_local), "seq", split_axis=0, concat_axis=0, tiled=True),
        lax.all_to_all(spread(value_local), "seq", split_axis=0, concat_axis=0, tiled=True),
    )
    attended_grad = lax.dot_general(
        grad_local, out_weight, (((1,), (1,)), ((), ())), preferred_element_type=jnp.float32
    ).astype(jnp.bfloat16)
    grad_heads = lax.all_to_all(
        to_heads(attended_grad), "seq", split_axis=0, concat_axis=0, tiled=True
    )
    key_blocks = key_all.reshape(all_blocks, BLK, per_device, head_size)
    value_blocks = value_all.reshape(all_blocks, BLK, per_device, head_size)
    query_runs = query_heads.reshape(run_count, block_run, group_rows, per_device, head_size)
    grad_runs = grad_heads.reshape(run_count, block_run, group_rows, per_device, head_size)
    pattern_runs = pattern.reshape(run_count, block_run, span)

    def attend_step(carry, items):
        key_acc, value_acc = carry
        query_run, grad_run, pattern_run = items
        key_gathered = key_blocks[pattern_run].reshape(block_run, span * BLK, per_device, head_size)
        value_gathered = value_blocks[pattern_run].reshape(
            block_run, span * BLK, per_device, head_size
        )
        scores = (
            jnp.einsum(
                "crhd,ckhd->chrk", query_run, key_gathered, preferred_element_type=jnp.float32
            )
            * scale
        )
        shifted = scores - jnp.max(scores, axis=-1, keepdims=True)
        weights = jnp.exp(shifted)
        probs = weights / jnp.sum(weights, axis=-1, keepdims=True)
        probs_low = probs.astype(jnp.bfloat16)
        result = jnp.einsum(
            "chrk,ckhd->crhd", probs_low, value_gathered, preferred_element_type=jnp.float32
        ).astype(jnp.bfloat16)
        prob_grad = jnp.einsum(
            "crhd,ckhd->chrk", grad_run, value_gathered, preferred_element_type=jnp.float32
        )
        delta = jnp.sum(probs * prob_grad, axis=-1, keepdims=True)
        score_grad = (probs * (prob_grad - delta)).astype(jnp.bfloat16)
        query_part = (
            jnp.einsum(
                "chrk,ckhd->crhd", score_grad, key_gathered, preferred_element_type=jnp.float32
            )
            * scale
        ).astype(jnp.bfloat16)
        key_contrib = (
            jnp.einsum("chrk,crhd->ckhd", score_grad, query_run, preferred_element_type=jnp.float32)
            * scale
        )
        value_contrib = jnp.einsum(
            "chrk,crhd->ckhd", probs_low, grad_run, preferred_element_type=jnp.float32
        )
        key_acc = key_acc.at[pattern_run].add(
            key_contrib.reshape(block_run, span, BLK, per_device, head_size)
        )
        value_acc = value_acc.at[pattern_run].add(
            value_contrib.reshape(block_run, span, BLK, per_device, head_size)
        )
        return ((key_acc, value_acc), (result, query_part))

    zero_grads = jnp.zeros((all_blocks, BLK, per_device, head_size), jnp.float32)
    (key_acc, value_acc), (out_heads, query_parts) = lax.scan(
        attend_step, (zero_grads, zero_grads), (query_runs, grad_runs, pattern_runs)
    )
    out_send = out_heads.reshape(seq_count, local_blocks * group_rows, columns)
    attended = to_tokens(lax.all_to_all(out_send, "seq", split_axis=0, concat_axis=0, tiled=True))
    mixed_out = jnp.dot(attended, out_weight, preferred_element_type=jnp.float32).astype(
        jnp.bfloat16
    )
    norm_factor = 1.0 / math.sqrt(rep_count * seq_count * tokens_here)
    weight_shard = lax.psum_scatter(
        lax.dot_general(
            attended, grad_local, (((0,), (0,)), ((), ())), preferred_element_type=jnp.float32
        ),
        ("seq", "rep"),
        scatter_dimension=0,
        tiled=True,
    )
    weight_grad = lax.all_gather(
        (weight_shard * norm_factor).astype(jnp.bfloat16), "rep", axis=0, tiled=True
    ).astype(jnp.float32)
    query_send = query_parts.reshape(seq_count, local_blocks * group_rows, columns)
    key_send = key_acc.astype(jnp.bfloat16).reshape(seq_count, tokens_here, columns)
    value_send = value_acc.astype(jnp.bfloat16).reshape(seq_count, tokens_here, columns)
    query_back, key_back, value_back = (
        lax.all_to_all(query_send, "seq", split_axis=0, concat_axis=0, tiled=True),
        lax.all_to_all(key_send, "seq", split_axis=0, concat_axis=0, tiled=True),
        lax.all_to_all(value_send, "seq", split_axis=0, concat_axis=0, tiled=True),
    )

    def fold_groups(source):
        summed = jnp.sum(
            source.reshape(head_groups, groups, tokens_here, columns).astype(jnp.float32), axis=1
        )
        return summed.astype(jnp.bfloat16).transpose(1, 0, 2).reshape(tokens_here, width)

    query_grad = to_tokens(query_back)
    key_grad = fold_groups(key_back)
    value_grad = fold_groups(value_back)
    return (mixed_out[None], query_grad[None], key_grad[None], value_grad[None], weight_grad)


def solution(mesh):
    placed = (
        P("rep", "seq", None),
        P("rep", "seq", None),
        P("rep", "seq", None),
        P(),
        P("rep", "seq", None),
        P(),
    )
    return jax.shard_map(
        local,
        mesh=mesh,
        in_specs=placed,
        out_specs=(
            P("rep", "seq", None),
            P("rep", "seq", None),
            P("rep", "seq", None),
            P("rep", "seq", None),
            P("seq", None),
        ),
        check_vma=False,
    )
```

profile of v0, /device:TPU:0, one launch (start us, length us, event | category | flops | bytes accessed | tf_op | source)
XLA Modules:
  0.0 236.8 jit_solution(9128325199954188067)
XLA Ops:
  9.1 7.3 %all-to-all-start = ((bf16[8,128,128]{1,2,0:T(8,128)(2,1)}), bf16[8,128,128]{1,2,0:T(8,128)(2,1)S(1)}, u32[]{:S(2)}, u32[]{:S(2)}) async-start(bf16[8,128,128]{1,2,0:T(8,128)(2,1)} %bitcast.1), calls=%async_computation | async-start | bytes 524288 | tf_op jit(solution)/shard_map/all_to_all | solution.py:54
  18.1 7.1 %all-to-all-done = bf16[8,128,128]{1,2,0:T(8,128)(2,1)S(1)} async-done(((bf16[8,128,128]{1,2,0:T(8,128)(2,1)}), bf16[8,128,128]{1,2,0:T(8,128)(2,1)S(1)}, u32[]{:S(2)}, u32[]{:S(2)}) %all-to-all-start) | async-done | bytes 262176 | tf_op jit(solution)/shard_map/all_to_all | solution.py:54
  25.2 3.6 %all-to-all-start.1 = ((bf16[8,128,128]{1,2,0:T(8,128)(2,1)}), bf16[8,128,128]{1,2,0:T(8,128)(2,1)S(1)}, u32[]{:S(2)}, u32[]{:S(2)}) async-start(bf16[8,128,128]{1,2,0:T(8,128)(2,1)} %bitcast.5), calls=%async_computation.1 | async-start | bytes 524288 | tf_op jit(solution)/shard_map/all_to_all | solution.py:53
  29.6 7.7 %all-to-all-done.1 = bf16[8,128,128]{1,2,0:T(8,128)(2,1)S(1)} async-done(((bf16[8,128,128]{1,2,0:T(8,128)(2,1)}), bf16[8,128,128]{1,2,0:T(8,128)(2,1)S(1)}, u32[]{:S(2)}, u32[]{:S(2)}) %all-to-all-start.1) | async-done | bytes 262176 | tf_op jit(solution)/shard_map/all_to_all | solution.py:53
  37.4 3.6 %all-to-all-start.2 = ((bf16[8,128,128]{2,1,0:T(8,128)(2,1)}), bf16[8,128,128]{2,1,0:T(8,128)(2,1)S(1)}, u32[]{:S(2)}, u32[]{:S(2)}) async-start(bf16[8,128,128]{2,1,0:T(8,128)(2,1)} %bitcast.9), calls=%async_computation.2 | async-start | bytes 524288 | tf_op jit(solution)/shard_map/all_to_all | solution.py:52
  44.7 4.8 %all-to-all-done.2 = bf16[8,128,128]{2,1,0:T(8,128)(2,1)S(1)} async-done(((bf16[8,128,128]{2,1,0:T(8,128)(2,1)}), bf16[8,128,128]{2,1,0:T(8,128)(2,1)S(1)}, u32[]{:S(2)}, u32[]{:S(2)}) %all-to-all-start.2) | async-done | bytes 262176 | tf_op jit(solution)/shard_map/all_to_all | solution.py:52
  49.5 2.3 fusion.20
  51.8 2.7 %convolution_convert_fusion.1 = bf16[16,128,64]{1,2,0:T(8,128)(2,1)S(1)} fusion(bf16[16,512,128]{2,1,0:T(8,128)(2,1)} %bitcast.116, f32[16,64,512]{2,1,0:T(8,128)} %get-tuple-element.41, f32[16,64]{1,0:T(8,128)S(1)} %get-tuple-element.40), kind=kOutput, calls=%fused_computation.18 | convolution fusion | flops 135397376 | bytes 4460544 | tf_op jit(solution)/shard_map/while/body/eval_jaxpr/chrk,ckhd->crhd/dot_general | solution.py:85
  54.5 11.8 %all_to_all.40 = bf16[8,128,128]{2,1,0:T(8,128)(2,1)S(1)} all-to-all(bf16[8,128,128]{2,1,0:T(8,128)(2,1)S(1)} %bitcast.131), channel_id=1, replica_groups=mesh['seq'=8,'rep'=4] {'seq'}, dimensions={0} | all-to-all | bytes 524288 | tf_op jit(solution)/shard_map/all_to_all | solution.py:119
  66.5 4.5 %fusion.10 = f32[1024,2048]{1,0:T(8,128)} fusion(bf16[1,128,2048]{2,1,0:T(8,128)(2,1)S(1)} %copy-done, bf16[16,8,8,128]{3,2,1,0:T(8,128)(2,1)S(1)} %bitcast.114), kind=kOutput, calls=%fused_computation.23 | convolution fusion | flops 536870912 | bytes 9175040 | tf_op jit(solution)/shard_map/dot_general | solution.py:125
  71.1 3.8 %fusion.8 = bf16[16,8,8,128]{3,1,2,0:T(8,128)(2,1)S(1)} fusion(bf16[1024,2048]{1,0:T(8,128)(2,1)} %param.9, bf16[1,128,2048]{2,1,0:T(8,128)(2,1)S(1)} %copy-done), kind=kOutput, calls=%fused_computation.20 | convolution fusion | flops 537001984 | bytes 4980736 | tf_op jit(solution)/shard_map/dot_general | solution.py:56
  75.1 13.2 %all_to_all.41 = bf16[8,128,128]{2,1,0:T(8,128)(2,1)S(1)} all-to-all(bf16[8,128,128]{2,1,0:T(8,128)(2,1)S(1)} %copy.28), channel_id=1, replica_groups=mesh['seq'=8,'rep'=4] {'seq'}, dimensions={0} | all-to-all | bytes 524288 | tf_op jit(solution)/shard_map/all_to_all | solution.py:59
  92.0 3.4 %all-to-all-start.5 = ((bf16[8,128,128]{2,1,0:T(8,128)(2,1)}), bf16[8,128,128]{2,1,0:T(8,128)(2,1)S(1)}, u32[]{:S(2)}, u32[]{:S(2)}) async-start(bf16[8,128,128]{2,1,0:T(8,128)(2,1)} %bitcast.24), calls=%async_computation.5 | async-start | bytes 524288 | tf_op jit(solution)/shard_map/all_to_all | solution.py:139
  95.4 2.8 %convolution_multiply_fusion = f32[16,512,128]{2,1,0:T(8,128)} fusion(bf16[16,64,512]{2,1,0:T(8,128)(2,1)S(1)} %multiply_convert_fusion, bf16[16,64,128]{2,1,0:T(8,128)(2,1)S(1)} %bitcast.127), kind=kOutput, calls=%fused_computation.8 | convolution fusion | flops 135266304 | bytes 5505024 | tf_op jit(solution)/shard_map/while/body/eval_jaxpr/chrk,crhd->ckhd/dot_general | solution.py:100
  98.2 13.6 %scatter_fusion = f32[16,64,128]{2,1,0:T(8,128)S(1)} fusion(f32[16,64,128]{2,1,0:T(8,128)S(1)} %broadcast.48.clone, s32[128]{0:T(128)S(1)} %reshape.165, f32[128,64,128]{2,1,0:T(8,128)} %bitcast.111), kind=kCustom, calls=%fused_computation.2 | custom fusion | flops 1048576 | bytes 12583424 | tf_op jit(solution)/shard_map/while/body/eval_jaxpr/scatter-add | solution.py:106
  112.5 5.9 %all-to-all-start.6 = ((bf16[8,128,128]{2,1,0:T(8,128)(2,1)}), bf16[8,128,128]{2,1,0:T(8,128)(2,1)S(1)}, u32[]{:S(2)}, u32[]{:S(2)}) async-start(bf16[8,128,128]{2,1,0:T(8,128)(2,1)} %bitcast.31), calls=%async_computation.6 | async-start | bytes 524288 | tf_op jit(solution)/shard_map/all_to_all | solution.py:140
  118.5 4.4 %convolution_bitcast_fusion = f32[16,512,1,128]{1,3,0,2:T(8,128)} fusion(bf16[16,64,128]{2,1,0:T(8,128)(2,1)S(1)} %bitcast.130, f32[16,64,512]{2,1,0:T(8,128)} %get-tuple-element.41, f32[16,64]{1,0:T(8,128)S(1)} %get-tuple-element.40), kind=kOutput, calls=%fused_computation.7 | convolution fusion | flops 135266304 | bytes 6557696 | tf_op jit(solution)/shard_map/while/body/eval_jaxpr/chrk,crhd->ckhd/dot_general | solution.py:103
  122.8 5.3 %copy.31 = f32[16,512,1,128]{3,1,0,2:T(8,128)} copy(f32[16,512,1,128]{1,3,0,2:T(8,128)} %convolution_bitcast_fusion) | data formatting | bytes 8388608 | tf_op jit(solution)/shard_map/while/body/eval_jaxpr/chrk,crhd->ckhd/transpose | solution.py:103
  128.2 13.6 %scatter_fusion.1 = f32[16,64,128]{2,1,0:T(8,128)S(1)} fusion(f32[16,64,128]{2,1,0:T(8,128)S(1)} %broadcast.48.clone.1, s32[128]{0:T(128)S(1)} %reshape.165, f32[128,64,128]{2,1,0:T(8,128)} %bitcast.110), kind=kCustom, calls=%fused_computation.3 | custom fusion | flops 1048576 | bytes 12583424 | tf_op jit(solution)/shard_map/while/body/eval_jaxpr/scatter-add | solution.py:109
  142.6 6.0 %all-to-all-start.7 = ((bf16[8,128,128]{2,1,0:T(8,128)(2,1)}), bf16[8,128,128]{2,1,0:T(8,128)(2,1)S(1)}, u32[]{:S(2)}, u32[]{:S(2)}) async-start(bf16[8,128,128]{2,1,0:T(8,128)(2,1)} %bitcast.37), calls=%async_computation.7 | async-start | bytes 524288 | tf_op jit(solution)/shard_map/all_to_all | solution.py:141
  150.5 6.9 %all-to-all-done.7 = bf16[8,128,128]{2,1,0:T(8,128)(2,1)S(1)} async-done(((bf16[8,128,128]{2,1,0:T(8,128)(2,1)}), bf16[8,128,128]{2,1,0:T(8,128)(2,1)S(1)}, u32[]{:S(2)}, u32[]{:S(2)}) %all-to-all-start.7) | async-done | bytes 262176 | tf_op jit(solution)/shard_map/all_to_all | solution.py:141
  158.5 3.8 %fusion.1 = bf16[1,128,2048]{2,1,0:T(8,128)(2,1)} fusion(bf16[1024,2048]{1,0:T(8,128)(2,1)} %param.9, bf16[16,8,8,128]{3,2,1,0:T(8,128)(2,1)S(1)} %bitcast.115), kind=kOutput, calls=%fused_computation.6 | convolution fusion | flops 537133056 | bytes 4980736 | tf_op jit(solution)/shard_map/dot_general | solution.py:120
  162.3 59.2 %reduce-scatter.2.cloned.1.call-done = f32[32,2048]{1,0:T(8,128)} async-done(((f32[1024,2048]{1,0:T(8,128)}), f32[32,2048]{1,0:T(8,128)}) %reduce-scatter.2.cloned.1.call-update) | async-done | bytes 262160 | tf_op jit(solution)/shard_map/reduce_scatter | solution.py:124
  222.4 6.5 %all_gather.3 = bf16[128,2048]{1,0:T(8,128)(2,1)S(1)} all-gather(bf16[32,2048]{1,0:T(8,128)(2,1)S(1)} %multiply_convert_fusion.1), channel_id=1, replica_groups=mesh['seq'=8,'rep'=4] {'rep'}, dimensions={0}, use_global_device_ids=true | all-gather | bytes 655360 | tf_op jit(solution)/shard_map/all_gather | solution.py:132
  (48 shorter events, 18.9 us)
Async XLA Ops:
  7.2 59.4 %copy-start = (bf16[1,128,2048]{2,1,0:T(8,128)(2,1)S(1)}, bf16[1,128,2048]{2,1,0:T(8,128)(2,1)}, u32[]{:S(2)}) copy-start(bf16[1,128,2048]{2,1,0:T(8,128)(2,1)} %param.10) | copy-start | bytes 1572868
  7.2 21.6 %copy-start.5 = (bf16[1,128,1024]{2,1,0:T(8,128)(2,1)S(1)}, bf16[1,128,1024]{2,1,0:T(8,128)(2,1)}, u32[]{:S(2)}) copy-start(bf16[1,128,1024]{2,1,0:T(8,128)(2,1)} %param.6) | copy-start | bytes 786436
  7.2 33.8 %copy-start.6 = (s32[16,8]{0,1:T(8,128)S(1)}, s32[16,8]{0,1:T(8,128)}, u32[]{:S(2)}) copy-start(s32[16,8]{0,1:T(8,128)} %param.11) | copy-start | bytes 1540
  9.1 16.2 %all-to-all-start = ((bf16[8,128,128]{1,2,0:T(8,128)(2,1)}), bf16[8,128,128]{1,2,0:T(8,128)(2,1)S(1)}, u32[]{:S(2)}, u32[]{:S(2)}) async-start(bf16[8,128,128]{1,2,0:T(8,128)(2,1)} %bitcast.1), calls=%async_computation | async-start | bytes 524288 | tf_op jit(solution)/shard_map/all_to_all | solution.py:54
  25.2 12.2 %all-to-all-start.1 = ((bf16[8,128,128]{1,2,0:T(8,128)(2,1)}), bf16[8,128,128]{1,2,0:T(8,128)(2,1)S(1)}, u32[]{:S(2)}, u32[]{:S(2)}) async-start(bf16[8,128,128]{1,2,0:T(8,128)(2,1)} %bitcast.5), calls=%async_computation.1 | async-start | bytes 524288 | tf_op jit(solution)/shard_map/all_to_all | solution.py:53
  37.4 12.1 %all-to-all-start.2 = ((bf16[8,128,128]{2,1,0:T(8,128)(2,1)}), bf16[8,128,128]{2,1,0:T(8,128)(2,1)S(1)}, u32[]{:S(2)}, u32[]{:S(2)}) async-start(bf16[8,128,128]{2,1,0:T(8,128)(2,1)} %bitcast.9), calls=%async_computation.2 | async-start | bytes 524288 | tf_op jit(solution)/shard_map/all_to_all | solution.py:52
  41.0 180.5 %reduce-scatter.2.cloned.1.call-start = ((), (), s32[]{:S(2)}) async-start(), calls=%async_computation.9 | async-start | bytes 8650752 | tf_op jit(solution)/shard_map/reduce_scatter | solution.py:124
  44.7 7.1 %copy-start.1 = (bf16[128,64,128]{2,1,0:T(8,128)(2,1)}, bf16[128,64,128]{2,1,0:T(8,128)(2,1)S(1)}, u32[]{:S(2)}) copy-start(bf16[128,64,128]{2,1,0:T(8,128)(2,1)S(1)} %gather_fusion.1) | copy-start | bytes 6291460
  71.1 17.1 %copy-start.3 = (f32[16,64,512]{2,1,0:T(8,128)S(1)}, f32[16,64,512]{2,1,0:T(8,128)}, u32[]{:S(2)}) copy-start(f32[16,64,512]{2,1,0:T(8,128)} %get-tuple-element.41) | copy-start | bytes 6291460
  71.1 17.1 %copy-start.4 = (bf16[128,64,128]{2,1,0:T(8,128)(2,1)S(1)}, bf16[128,64,128]{2,1,0:T(8,128)(2,1)}, u32[]{:S(2)}) copy-start(bf16[128,64,128]{2,1,0:T(8,128)(2,1)} %gather_fusion) | copy-start | bytes 6291460
  89.2 1.6 copy-start.2
  92.0 20.5 %all-to-all-start.5 = ((bf16[8,128,128]{2,1,0:T(8,128)(2,1)}), bf16[8,128,128]{2,1,0:T(8,128)(2,1)S(1)}, u32[]{:S(2)}, u32[]{:S(2)}) async-start(bf16[8,128,128]{2,1,0:T(8,128)(2,1)} %bitcast.24), calls=%async_computation.5 | async-start | bytes 524288 | tf_op jit(solution)/shard_map/all_to_all | solution.py:139
  112.5 30.0 %all-to-all-start.6 = ((bf16[8,128,128]{2,1,0:T(8,128)(2,1)}), bf16[8,128,128]{2,1,0:T(8,128)(2,1)S(1)}, u32[]{:S(2)}, u32[]{:S(2)}) async-start(bf16[8,128,128]{2,1,0:T(8,128)(2,1)} %bitcast.31), calls=%async_computation.6 | async-start | bytes 524288 | tf_op jit(solution)/shard_map/all_to_all | solution.py:140
  142.6 14.9 %all-to-all-start.7 = ((bf16[8,128,128]{2,1,0:T(8,128)(2,1)}), bf16[8,128,128]{2,1,0:T(8,128)(2,1)S(1)}, u32[]{:S(2)}, u32[]{:S(2)}) async-start(bf16[8,128,128]{2,1,0:T(8,128)(2,1)} %bitcast.37), calls=%async_computation.7 | async-start | bytes 524288 | tf_op jit(solution)/shard_map/all_to_all | solution.py:141
Sparse Core Ops, SparseCore 0:
  71.2 150.1 reduce-scatter.1
where the time goes:
time: 239 us; the launch traced here: 237 us
  waiting for transfers between devices  85.8 us (36%)
  blocking collectives  31.5 us (13%)
  other arithmetic  31.1 us (13%)
  starting transfers between devices  29.8 us (12%)
  matrix products  26.4 us (11%)
  local copies, waits for them, and re-layouts  18.1 us (8%)
  between operations  14.3 us (6%)
    reduce_scatter x1, waiting for transfers between devices, local(): lax.psum_scatter(lax.dot_general(attended, grad_local, (((0,), (0,)), (()...  59.2 us
    scatter-add x1, other arithmetic, attend_step(): value_acc.at[pattern_run]  13.6 us
    scatter-add x1, other arithmetic, attend_step(): key_acc.at[pattern_run]  13.6 us
    all_to_all x1, blocking collectives, local(): lax.all_to_all(to_heads(attended_grad), 'seq', split_axis=0, concat_axis=...  13.2 us
    all_to_all x1, blocking collectives, local(): lax.all_to_all(out_send, 'seq', split_axis=0, concat_axis=0, tiled=True)  11.8 us
    all_to_all x1, waiting for transfers between devices, local(): lax.all_to_all(spread(key_local), 'seq', split_axis=0, concat_axis=0, til...  7.75 us
    all_to_all x1, starting transfers between devices, local(): lax.all_to_all(spread(value_local), 'seq', split_axis=0, concat_axis=0, t...  7.25 us
    all_to_all x1, waiting for transfers between devices, local(): lax.all_to_all(spread(value_local), 'seq', split_axis=0, concat_axis=0, t...  7.13 us
  transfers between devices with their start and end apart: 7, of which 5 were waited for; matrix products, arithmetic and copies ran while one was open for 26% of the time, Pallas kernels for 0%

commit v1 on v0

--- a/solution.py
+++ b/solution.py
@@ -1,15 +1,428 @@
+import functools
 import math
 
 import jax
 import jax.numpy as jnp
 from jax import lax
+from jax.experimental import pallas as pl
+from jax.experimental.pallas import tpu as pltpu
 from jax.sharding import PartitionSpec as P
 
 HD = 128
 BLK = 64
+MASKED = -1e30
+VMEM = pltpu.VMEM
+NT = (((1,), (1,)), ((), ()))
+NN = (((1,), (0,)), ((), ()))
+TN = (((0,), (0,)), ((), ()))
+
+
+def dot(left, right, dims):
+    return lax.dot_general(left, right, dims, preferred_element_type=jnp.float32)
+
+
+def whole(count):
+    return [pl.BlockSpec(memory_space=VMEM)] * count
+
+
+def params(mib):
+    return pltpu.CompilerParams(vmem_limit_bytes=mib * 1024 * 1024)
+
+
+def cost(flops, moved):
+    return pl.CostEstimate(flops=flops, bytes_accessed=moved, transcendentals=0)
+
+
+def struct(*shape, dtype=jnp.bfloat16):
+    return jax.ShapeDtypeStruct(shape, dtype)
+
+
+def swap(array, axis, mask):
+    return lax.ppermute(array, axis, [(i, i ^ mask) for i in range(lax.axis_size(axis))])
+
+
+def pack_kernel(ids, key_ref, value_ref, query_ref, *sends):
+    for mask, send in enumerate(sends):
+        columns = pl.ds(pl.multiple_of((ids[0] ^ mask) * HD, HD), HD)
+        rows = key_ref.shape[0]
+        send[:rows] = key_ref[:, columns]
+        send[rows : 2 * rows] = value_ref[:, columns]
+        send[2 * rows :] = query_ref[:, columns]
+
+
+def pack(ids, key_local, value_local, query_local, peers):
+    rows = key_local.shape[0]
+    return pl.pallas_call(
+        pack_kernel,
+        out_shape=[struct(3 * rows, HD)] * peers,
+        in_specs=[pl.BlockSpec(memory_space=pltpu.SMEM)] + whole(3),
+        out_specs=whole(peers),
+        compiler_params=params(16),
+        name="pack_kvq",
+    )(ids, key_local, value_local, query_local)
+
+
+def quarter_kernel(ids, grad_ref, *sends):
+    width = grad_ref.shape[1] // len(sends)
+    for mask, send in enumerate(sends):
+        send[...] = grad_ref[:, pl.ds(pl.multiple_of((ids[1] ^ mask) * width, width), width)]
+
+
+def quarters(ids, grad_local, count):
+    rows, width = grad_local.shape
+    return pl.pallas_call(
+        quarter_kernel,
+        out_shape=[struct(rows, width // count)] * count,
+        in_specs=[pl.BlockSpec(memory_space=pltpu.SMEM)] + whole(1),
+        out_specs=whole(count),
+        compiler_params=params(16),
+        name="pack_grad",
+    )(ids, grad_local)
+
+
+def head_grad_kernel(ids, grad_ref, weight_ref, *sends):
+    step = pl.program_id(0)
+    block = dot(grad_ref[...], weight_ref[...], NT).astype(jnp.bfloat16)
+    for mask, send in enumerate(sends):
+
+        @pl.when(step == mask)
+        def _():
+            send[...] = block
+
+
+def head_grads(ids, grad_local, out_weight, peers):
+    rows, width = grad_local.shape
+    grid = pltpu.PrefetchScalarGridSpec(
+        num_scalar_prefetch=1,
+        grid=(peers,),
+        in_specs=[
+            pl.BlockSpec((rows, width), lambda i, ids: (0, 0)),
+            pl.BlockSpec((HD, width), lambda i, ids: (ids[0] ^ i, 0)),
+        ],
+        out_specs=[pl.BlockSpec((rows, HD), lambda i, ids: (0, 0))] * peers,
+    )
+    return pl.pallas_call(
+        head_grad_kernel,
+        out_shape=[struct(rows, HD)] * peers,
+        grid_spec=grid,
+        compiler_params=params(16),
+        cost_estimate=cost(2 * rows * width * HD * peers, out_weight.size * 2),
+        name="head_grads",
+    )(ids, grad_local, out_weight)
+
+
+def load_heads(ids, parts, rows, *targets):
+    for mask, part in enumerate(parts):
+        place = pl.ds(pl.multiple_of((ids[0] ^ mask) * rows, rows), rows)
+        for index, target in enumerate(targets):
+            target[place] = part[index * rows : (index + 1) * rows]
+
+
+def scores_of(keys, queries, bias, scale):
+    blocks = bias.shape[0]
+    scores = dot(keys, queries, NT) * scale
+    shaped = scores.reshape(blocks, BLK, queries.shape[0]) + bias[:, None, :]
+    return shaped.reshape(scores.shape)
+
+
+def forward_kernel(peers, chunk, scale, ids, bias_ref, *refs):
+    parts, refs = refs[:peers], refs[peers:]
+    outs, (top_ref, sum_ref, keys, values, queries, heads) = refs[:-6], refs[-6:]
+    load_heads(ids, parts, parts[0].shape[0] // 3, keys, values, queries)
+    value_cols = values[...].T
+    for start in range(0, keys.shape[0], chunk):
+        rows = slice(start, start + chunk)
+        scores = scores_of(keys[...], queries[rows], bias_ref[:, rows], scale)
+        top = jnp.max(scores, axis=0, keepdims=True)
+        weights = jnp.exp(scores - top)
+        total = 1.0 / jnp.sum(weights, axis=0, keepdims=True)
+        probs_low = (weights * total).astype(jnp.bfloat16)
+        heads[rows] = dot(value_cols, probs_low, NN).T.astype(jnp.bfloat16)
+        top_ref[:, rows] = top
+        sum_ref[:, rows] = total
+    size = outs[0].shape[0]
+    for mask, out in enumerate(outs):
+        out[...] = heads[pl.ds(pl.multiple_of(((ids[0] >> 1) ^ mask) * size, size), size)]
+
+
+def forward(ids, bias, parts, scale):
+    peers, tokens = len(parts), bias.shape[1]
+    quads = peers // 2
+    return pl.pallas_call(
+        functools.partial(forward_kernel, peers, 2 * tokens // peers, scale),
+        out_shape=[struct(2 * tokens // peers, HD)] * quads
+        + [struct(1, tokens, dtype=jnp.float32)] * 2,
+        in_specs=[pl.BlockSpec(memory_space=pltpu.SMEM)] + whole(peers + 1),
+        out_specs=whole(quads + 2),
+        scratch_shapes=[pltpu.VMEM((tokens, HD), jnp.bfloat16)] * 4,
+        compiler_params=params(24),
+        cost_estimate=cost(16 * tokens * tokens * HD, 4 * tokens * HD * 2),
+        name="attend",
+    )(ids, bias, *parts)
+
+
+def backward_kernel(peers, chunk, scale, ids, bias_ref, top_ref, sum_ref, *refs):
+    parts, refs = refs[:peers], refs[peers:]
+    grad_parts, refs = refs[:peers], refs[peers:]
+    outs, refs = refs[:peers], refs[peers:]
+    keys, values, queries, grads, query_grad, key_sum, value_sum = refs
+    rows_each = grad_parts[0].shape[0]
+    load_heads(ids, parts, rows_each, keys, values, queries)
+    load_heads(ids, grad_parts, rows_each, grads)
+    key_cols = keys[...].T
+    for start in range(0, keys.shape[0], chunk):
+        rows = slice(start, start + chunk)
+        scores = scores_of(keys[...], queries[rows], bias_ref[:, rows], scale)
+        probs = jnp.exp(scores - top_ref[:, rows]) * sum_ref[:, rows]
+        prob_grad = dot(values[...], grads[rows], NT)
+        delta = jnp.sum(probs * prob_grad, axis=0, keepdims=True)
+        score_grad = (probs * (prob_grad - delta)).astype(jnp.bfloat16)
+        value_part = dot(probs.astype(jnp.bfloat16), grads[rows], NN)
+        key_part = dot(score_grad, queries[rows], NN)
+        if start == 0:
+            value_sum[...] = value_part
+            key_sum[...] = key_part
+        else:
+            value_sum[...] += value_part
+            key_sum[...] += key_part
+        query_grad[rows] = (dot(key_cols, score_grad, NN) * scale).T.astype(jnp.bfloat16)
+    for mask, out in enumerate(outs):
+        place = pl.ds(pl.multiple_of((ids[0] ^ mask) * rows_each, rows_each), rows_each)
+        out[:rows_each] = query_grad[place]
+        out[rows_each : 2 * rows_each] = (key_sum[place] * scale).astype(jnp.bfloat16)
+        out[2 * rows_each :] = value_sum[place].astype(jnp.bfloat16)
+
+
+def backward(ids, bias, top, total, parts, grad_parts, scale):
+    peers, tokens = len(parts), bias.shape[1]
+    return pl.pallas_call(
+        functools.partial(backward_kernel, peers, 2 * tokens // peers, scale),
+        out_shape=[struct(3 * tokens // peers, HD)] * peers,
+        in_specs=[pl.BlockSpec(memory_space=pltpu.SMEM)] + whole(2 * peers + 3),
+        out_specs=whole(peers),
+        scratch_shapes=[pltpu.VMEM((tokens, HD), jnp.bfloat16)] * 5
+        + [pltpu.VMEM((tokens, HD), jnp.float32)] * 2,
+        compiler_params=params(24),
+        cost_estimate=cost(40 * tokens * tokens * HD, 8 * tokens * HD * 2),
+        name="attend_back",
+    )(ids, bias, top, total, *parts, *grad_parts)
+
+
+def unpack_kernel(ids, *refs):
+    parts, targets = refs[:-3], refs[-3:]
+    for mask, part in enumerate(parts):
+        columns = pl.ds(pl.multiple_of((ids[0] ^ mask) * HD, HD), HD)
+        rows = targets[0].shape[0]
+        for index, target in enumerate(targets):
+            target[:, columns] = part[index * rows : (index + 1) * rows]
+
+
+def unpack(ids, parts):
+    rows = parts[0].shape[0] // 3
+    return pl.pallas_call(
+        unpack_kernel,
+        out_shape=[struct(rows, HD * len(parts))] * 3,
+        in_specs=[pl.BlockSpec(memory_space=pltpu.SMEM)] + whole(len(parts)),
+        out_specs=whole(3),
+        compiler_params=params(16),
+        name="unpack_grads",
+    )(ids, *parts)
+
+
+def project_kernel(quads, ids, near, far, weight_ref, out_ref, attended):
+    rows = out_ref.shape[0]
+
+    @pl.when(pl.program_id(0) == 0)
+    def _():
+        side = ids[0] & 1
+        for mask in range(quads):
+            pair = ((ids[0] >> 1) ^ mask) * 2
+            mine = pl.ds(pl.multiple_of((2 * mask + side) * rows, rows), rows)
+            for head, block in (
+                (pair + side, near[mine]),
+                (pair + 1 - side, far[mask * rows : (mask + 1) * rows]),
+            ):
+                attended[:, pl.ds(pl.multiple_of(head * HD, HD), HD)] = block
+
+    out_ref[...] = dot(attended[...], weight_ref[...], NN).astype(jnp.bfloat16)
+
+
+def project(ids, near, far, out_weight, quads):
+    rows = far.shape[0] // quads
+    depth, width = out_weight.shape
+    tile = width // 4
+    grid = pltpu.PrefetchScalarGridSpec(
+        num_scalar_prefetch=1,
+        grid=(width // tile,),
+        in_specs=[
+            pl.BlockSpec(near.shape, lambda i, ids: (0, 0)),
+            pl.BlockSpec(far.shape, lambda i, ids: (0, 0)),
+            pl.BlockSpec((depth, tile), lambda i, ids: (0, i)),
+        ],
+        out_specs=pl.BlockSpec((rows, tile), lambda i, ids: (0, i)),
+        scratch_shapes=[pltpu.VMEM((rows, depth), jnp.bfloat16)],
+    )
+    return pl.pallas_call(
+        functools.partial(project_kernel, quads),
+        out_shape=struct(rows, width),
+        grid_spec=grid,
+        compiler_params=params(16),
+        cost_estimate=cost(2 * rows * depth * width, depth * width * 2),
+        name="project",
+    )(ids, near, far, out_weight)
+
+
+def stack_pair_kernel(ids, *refs):
+    blocks, (near, far) = refs[:-2], refs[-2:]
+    rows = blocks[0].shape[0] // 2
+    for mask, block in enumerate(blocks):
+        near[2 * mask * rows : 2 * (mask + 1) * rows] = block[...]
+        theirs = pl.ds(pl.multiple_of((1 - (ids[0] & 1)) * rows, rows), rows)
+        far[mask * rows : (mask + 1) * rows] = block[theirs]
+
+
+def stack_pair(ids, blocks):
+    rows = len(blocks) * blocks[0].shape[0]
+    return pl.pallas_call(
+        stack_pair_kernel,
+        out_shape=[struct(rows, HD), struct(rows // 2, HD)],
+        in_specs=[pl.BlockSpec(memory_space=pltpu.SMEM)] + whole(len(blocks)),
+        out_specs=whole(2),
+        compiler_params=params(8),
+        name="stack_pair",
+    )(ids, *blocks)
+
+
+def weight_part_kernel(quads, ids, *refs):
+    docs = len(refs) - quads - 2
+    heads, grads, outs = refs[:docs], refs[docs : docs + 2], refs[docs + 2 :]
+    rows = heads[0].shape[0] // (2 * quads)
+    right = jnp.concatenate([grad[...] for grad in grads], axis=0)
+    side = ids[0] & 1
+    for mask, out in enumerate(outs):
+        places = [
+            pl.ds(pl.multiple_of((2 * mask + index) * rows, rows), rows) for index in (side, 1 - side)
+        ]
+        left = jnp.concatenate([head[place] for place in places for head in heads], axis=0)
+        out[...] = dot(left, right, TN).astype(jnp.bfloat16)
+
+
+def weight_parts(ids, heads, grads, quads):
+    width = grads[0].shape[1]
+    return pl.pallas_call(
+        functools.partial(weight_part_kernel, quads),
+        out_shape=[struct(HD, width)] * quads,
+        in_specs=[pl.BlockSpec(memory_space=pltpu.SMEM)] + whole(len(heads) + 2),
+        out_specs=whole(quads),
+        compiler_params=params(16),
+        cost_estimate=cost(4 * quads * HD * width * grads[0].shape[0], 4 << 20),
+        name="weight_part",
+    )(ids, *heads, *grads)
+
+
+def weight_sum_kernel(factor, *refs):
+    total = refs[0][...].astype(jnp.float32)
+    for part in refs[1:-1]:
+        total += part[...].astype(jnp.float32)
+    refs[-1][...] = (total * factor).astype(jnp.bfloat16)
+
+
+def weight_sum(parts, factor):
+    return pl.pallas_call(
+        functools.partial(weight_sum_kernel, factor),
+        out_shape=struct(*parts[0].shape),
+        in_specs=whole(len(parts)),
+        out_specs=pl.BlockSpec(memory_space=VMEM),
+        compiler_params=params(8),
+        name="weight_sum",
+    )(*parts)
+
+
+def weight_join_kernel(ids, *refs):
+    width = refs[0].shape[1]
+    for mask, part in enumerate(refs[:-1]):
+        columns = pl.ds(pl.multiple_of((ids[1] ^ mask) * width, width), width)
+        refs[-1][:, columns] = part[...].astype(jnp.float32)
+
+
+def weight_join(ids, parts):
+    rows, width = parts[0].shape
+    return pl.pallas_call(
+        weight_join_kernel,
+        out_shape=struct(rows, width * len(parts), dtype=jnp.float32),
+        in_specs=[pl.BlockSpec(memory_space=pltpu.SMEM)] + whole(len(parts)),
+        out_specs=pl.BlockSpec(memory_space=VMEM),
+        compiler_params=params(8),
+        name="weight_join",
+    )(ids, *parts)
+
+
+def gather_rep(block):
+    blocks, bit = [block], 1
+    while bit < lax.axis_size("rep"):
+        blocks = blocks + [swap(item, "rep", bit) for item in blocks]
+        bit *= 2
+    return blocks
+
+
+def dense_bias(pattern, tokens):
+    blocks = pattern.shape[0]
+    named = pattern[:, :, None] == jnp.arange(blocks, dtype=pattern.dtype)
+    counts = jnp.sum(named.astype(jnp.float32), axis=1).T
+    bias = jnp.where(counts > 0, jnp.log(jnp.maximum(counts, 1.0)), MASKED)
+    return jnp.repeat(bias, tokens // blocks, axis=1)
+
+
+def dense_local(query_in, key_in, value_in, out_weight, grad_out, pattern):
+    seq_count, rep_count = lax.axis_size("seq"), lax.axis_size("rep")
+    tokens_here = query_in.shape[1]
+    tokens = tokens_here * seq_count
+    quads = seq_count // 2
+    scale = 1.0 / math.sqrt(HD)
+    ids = jnp.stack([lax.axis_index("seq"), lax.axis_index("rep")]).astype(jnp.int32)
+    bias = dense_bias(pattern, tokens)
+
+    sends = pack(ids, key_in[0], value_in[0], query_in[0], seq_count)
+    parts = [sends[0]] + [swap(sends[mask], "seq", mask) for mask in range(1, seq_count)]
+    grad_sends = head_grads(ids, grad_out[0], out_weight, seq_count)
+    grad_parts = [grad_sends[0]] + [swap(grad_sends[mask], "seq", mask) for mask in range(1, seq_count)]
+    grad_quarters = quarters(ids, grad_out[0], rep_count)
+    doc_grads = jnp.concatenate(
+        [grad_quarters[0]] + [swap(grad_quarters[mask], "rep", mask) for mask in range(1, rep_count)],
+        axis=0,
+    )
+    pair_grads = swap(doc_grads, "seq", 1)
+
+    *heads, top, total = forward(ids, bias, parts, scale)
+    near = [heads[0]] + [swap(heads[mask], "seq", 2 * mask) for mask in range(1, quads)]
+    back = backward(ids, bias, top, total, parts, grad_parts, scale)
+
+    near, far_send = stack_pair(ids, near)
+    far = swap(far_send, "seq", 1)
+    mixed_out = project(ids, near, far, out_weight, quads)
+
+    weight_sends = weight_parts(ids, gather_rep(near), [doc_grads, pair_grads], quads)
+    weight_blocks = [weight_sends[0]] + [
+        swap(weight_sends[mask], "seq", 2 * mask) for mask in range(1, quads)
+    ]
+    factor = 1.0 / math.sqrt(rep_count * tokens)
+    weight_grad = weight_join(ids, gather_rep(weight_sum(weight_blocks, factor)))
+
+    returned = [back[0]] + [swap(back[mask], "seq", mask) for mask in range(1, seq_count)]
+    query_grad, key_grad, value_grad = unpack(ids, returned)
+    return (mixed_out[None], query_grad[None], key_grad[None], value_grad[None], weight_grad)
 
 
 def local(query_in, key_in, value_in, out_weight, grad_out, pattern):
+    seq_count, rep_count = lax.axis_size("seq"), lax.axis_size("rep")
+    one_head_each = seq_count * HD == query_in.shape[2]
+    paired = seq_count & (seq_count - 1) == 0 and rep_count & (rep_count - 1) == 0 and seq_count > 1
+    if one_head_each and paired and query_in.shape[0] == 1:
+        return dense_local(query_in, key_in, value_in, out_weight, grad_out, pattern)
+    return general_local(query_in, key_in, value_in, out_weight, grad_out, pattern)
+
+
+def general_local(query_in, key_in, value_in, out_weight, grad_out, pattern):
     seq_count = lax.axis_size("seq")
     rep_count = lax.axis_size("rep")
     tokens_here = query_in.shape[1]

time: 239 us -> 105 us (0.44)
  waiting for transfers between devices: 85.8 us -> 23 us
  blocking collectives: 31.5 us -> 0 us
  other arithmetic: 31.1 us -> 0.18 us
  matrix products: 26.4 us -> 0 us
  starting transfers between devices: 29.8 us -> 54.8 us
  Pallas kernels: 0 us -> 21.2 us
  between operations: 14.3 us -> 0.9 us
  local copies, waits for them, and re-layouts: 18.1 us -> 4.96 us
    reduce_scatter x1 -> x0, waiting for transfers between devices: 59.2 us -> none  [local(): lax.psum_scatter(lax.dot_general(attended, grad_local, (((0,), (0,)), (()...]
    ppermute x0 -> x38, starting transfers between devices: none -> 54.8 us  [swap(): lax.ppermute(array, axis, [(i, i ^ mask) for i in range(lax.axis_size(axi...]
    all_to_all x6 -> x0, starting transfers between devices: 29.7 us -> none  [the longest x1 7.25 us: local(): lax.all_to_all(spread(value_local), 'seq', split_axis=0, concat_axis=0, t...]
    scatter-add x2 -> x0, other arithmetic: 27.1 us -> none  [the longest x1 13.6 us: attend_step(): value_acc.at[pattern_run]]
    all_to_all x6 -> x0, waiting for transfers between devices: 26.6 us -> none  [the longest x1 7.75 us: local(): lax.all_to_all(spread(key_local), 'seq', split_axis=0, concat_axis=0, til...]
    all_to_all x2 -> x0, blocking collectives: 25 us -> none  [the longest x1 13.2 us: local(): lax.all_to_all(to_heads(attended_grad), 'seq', split_axis=0, concat_axis=...]
    dot_general x8 -> x0, matrix products: 24.1 us -> none  [the longest x1 4.51 us: local(): lax.dot_general(attended, grad_local, (((0,), (0,)), ((), ())), preferred...]
    ppermute x0 -> x38, waiting for transfers between devices: none -> 23 us  [swap(): lax.ppermute(array, axis, [(i, i ^ mask) for i in range(lax.axis_size(axi...]
  transfers between devices with their start and end apart: 7 -> 38, of which waited for: 5 -> 7; matrix products, arithmetic and copies ran while one was open for 26% -> 1% of each run, Pallas kernels for 0% -> 18%
where the time goes in v1:
time: 105 us
  starting transfers between devices  54.8 us (52%)
  waiting for transfers between devices  23 us (22%)
  Pallas kernels  21.2 us (20%)
  local copies, waits for them, and re-layouts  4.96 us (5%)
    ppermute x38, starting transfers between devices, swap(): lax.ppermute(array, axis, [(i, i ^ mask) for i in range(lax.axis_size(axi...  54.8 us
    ppermute x38, waiting for transfers between devices, swap(): lax.ppermute(array, axis, [(i, i ^ mask) for i in range(lax.axis_size(axi...  23 us
    unnamed x16, local copies, waits for them, and re-layouts  4.69 us
    pallas_call x1, Pallas kernels, backward(): pl.pallas_call(functools.partial(backward_kernel, peers, 2 * tokens // pe...  4.25 us
    pallas_call x1, Pallas kernels, forward(): pl.pallas_call(functools.partial(forward_kernel, peers, 2 * tokens // pee...  4.03 us
    pallas_call x1, Pallas kernels, head_grads(): pl.pallas_call(head_grad_kernel, out_shape=[struct(rows, HD)] * peers, gr...  3.3 us
    pallas_call x1, Pallas kernels, project(): pl.pallas_call(functools.partial(project_kernel, quads), out_shape=struct...  3.16 us
  transfers between devices with their start and end apart: 38, of which 7 were waited for; matrix products, arithmetic and copies ran while one was open for 1% of the time, Pallas kernels for 18%

profile of v1, /device:TPU:0, one launch (start us, length us, event | category | flops | bytes accessed | tf_op | source)
XLA Modules:
  0.0 105.0 jit_solution(14783442092724041324)
XLA Ops:
  4.3 3.0 %collective-permute-start = (bf16[384,128]{1,0:T(8,128)(2,1)S(1)}, bf16[384,128]{1,0:T(8,128)(2,1)S(1)}, u32[]{:S(2)}, u32[]{:S(2)}) collective-permute-start(bf16[384,128]{1,0:T(8,128)(2,1)S(1)} %get-tuple-element.49), channel_id=1, source_target_pairs={{0,4},{4,0},{8,12},{12,8},{16,20},{20,16},{24,28},{28,24},{1,5},{5... | collective-permute-start | bytes 294920 | tf_op jit(solution)/shard_map/ppermute | solution.py:41
  8.9 3.0 %collective-permute-start.3 = (bf16[384,128]{1,0:T(8,128)(2,1)S(1)}, bf16[384,128]{1,0:T(8,128)(2,1)S(1)}, u32[]{:S(2)}, u32[]{:S(2)}) collective-permute-start(bf16[384,128]{1,0:T(8,128)(2,1)S(1)} %get-tuple-element.52), channel_id=1, source_target_pairs={{0,16},{4,20},{8,24},{12,28},{16,0},{20,4},{24,8},{28,12},{1,17},{... | collective-permute-start | bytes 294920 | tf_op jit(solution)/shard_map/ppermute | solution.py:41
  16.0 3.7 %collective-permute-start.5 = (bf16[384,128]{1,0:T(8,128)(2,1)S(1)}, bf16[384,128]{1,0:T(8,128)(2,1)S(1)}, u32[]{:S(2)}, u32[]{:S(2)}) collective-permute-start(bf16[384,128]{1,0:T(8,128)(2,1)S(1)} %get-tuple-element.54), channel_id=1, source_target_pairs={{0,24},{4,28},{8,16},{12,20},{16,8},{20,12},{24,0},{28,4},{1,25},{... | collective-permute-start | bytes 294920 | tf_op jit(solution)/shard_map/ppermute | solution.py:41
  19.8 1.7 %collective-permute-start.29 = (bf16[128,512]{1,0:T(8,128)(2,1)S(1)}, bf16[128,512]{1,0:T(8,128)(2,1)S(1)}, u32[]{:S(2)}, u32[]{:S(2)}) collective-permute-start(bf16[128,512]{1,0:T(8,128)(2,1)S(1)} %get-tuple-element.85), channel_id=1, source_target_pairs={{0,2},{1,3},{2,0},{3,1},{4,6},{5,7},{6,4},{7,5},{8,10},{9,11},{10,... | collective-permute-start | bytes 393224 | tf_op jit(solution)/shard_map/ppermute | solution.py:41
  21.5 5.5 %collective-permute-done.4.refs_5_ = bf16[384,128]{1,0:T(8,128)(2,1)S(1)} collective-permute-done((bf16[384,128]{1,0:T(8,128)(2,1)S(1)}, bf16[384,128]{1,0:T(8,128)(2,1)S(1)}, u32[]{:S(2)}, u32[]{:S(2)}) %collective-permute-start.4) | collective-permute-done | bytes 98336 | tf_op jit(solution)/shard_map/ppermute | solution.py:41
  27.1 4.0 %attend.1 = (bf16[256,128]{1,0:T(8,128)(2,1)S(1)}, bf16[256,128]{1,0:T(8,128)(2,1)S(1)}, bf16[256,128]{1,0:T(8,128)(2,1)S(1)}, bf16[256,128]{1,0:T(8,128)(2,1)S(...) custom-call(s32[2]{0:T(128)S(1)} %pad_add_fusion.ids, f32[16,1024]{1,0:T(8,128)S(1)} %reshape.14.bias_ref, ...), custom_call_target="tpu_custom_call" | custom-call | flops 2147483648 | bytes 1048576 | tf_op jit(solution)/shard_map/attend/pallas_call | solution.py:151
  31.1 4.0 %collective-permute-start.7 = (bf16[256,128]{1,0:T(8,128)(2,1)S(1)}, bf16[256,128]{1,0:T(8,128)(2,1)S(1)}, u32[]{:S(2)}, u32[]{:S(2)}) collective-permute-start(bf16[256,128]{1,0:T(8,128)(2,1)S(1)} %get-tuple-element.57), channel_id=1, source_target_pairs={{0,8},{4,12},{8,0},{12,4},{16,24},{20,28},{24,16},{28,20},{1,9},{5... | collective-permute-start | bytes 196616 | tf_op jit(solution)/shard_map/ppermute | solution.py:41
  38.5 4.1 %collective-permute-done.8.refs_2_ = bf16[256,128]{1,0:T(8,128)(2,1)S(1)} collective-permute-done((bf16[256,128]{1,0:T(8,128)(2,1)S(1)}, bf16[256,128]{1,0:T(8,128)(2,1)S(1)}, u32[]{:S(2)}, u32[]{:S(2)}) %collective-permute-start.8) | collective-permute-done | bytes 65568 | tf_op jit(solution)/shard_map/ppermute | solution.py:41
  46.4 3.3 %head_grads.1 = (bf16[128,128]{1,0:T(8,128)(2,1)S(1)}, bf16[128,128]{1,0:T(8,128)(2,1)S(1)}, bf16[128,128]{1,0:T(8,128)(2,1)S(1)}, bf16[128,128]{1,0:T(8,128)(2,...) custom-call(s32[2]{0:T(128)S(1)} %pad_add_fusion.ids, ...), custom_call_target="tpu_custom_call" | custom-call | flops 536870912 | bytes 4194304 | tf_op jit(solution)/shard_map/head_grads/pallas_call | solution.py:104
  51.1 2.5 %collective-permute-done.11.refs_9_ = bf16[128,128]{1,0:T(8,128)(2,1)S(1)} collective-permute-done((bf16[128,128]{1,0:T(8,128)(2,1)S(1)}, bf16[128,128]{1,0:T(8,128)(2,1)S(1)}, u32[]{:S(2)}, u32[]{:S(2)}) %collective-permute-start.11) | collective-permute-done | bytes 32800 | tf_op jit(solution)/shard_map/ppermute | solution.py:41
  56.0 2.7 %collective-permute-start.15 = (bf16[128,128]{1,0:T(8,128)(2,1)S(1)}, bf16[128,128]{1,0:T(8,128)(2,1)S(1)}, u32[]{:S(2)}, u32[]{:S(2)}) collective-permute-start(bf16[128,128]{1,0:T(8,128)(2,1)S(1)} %get-tuple-element.69), channel_id=1, source_target_pairs={{0,20},{4,16},{8,28},{12,24},{16,4},{20,0},{24,12},{28,8},{1,21},{... | collective-permute-start | bytes 98312 | tf_op jit(solution)/shard_map/ppermute | solution.py:41
  58.7 2.3 %collective-permute-start.16 = (bf16[128,128]{1,0:T(8,128)(2,1)S(1)}, bf16[128,128]{1,0:T(8,128)(2,1)S(1)}, u32[]{:S(2)}, u32[]{:S(2)}) collective-permute-start(bf16[128,128]{1,0:T(8,128)(2,1)S(1)} %get-tuple-element.70), channel_id=1, source_target_pairs={{0,24},{4,28},{8,16},{12,20},{16,8},{20,12},{24,0},{28,4},{1,25},{... | collective-permute-start | bytes 98312 | tf_op jit(solution)/shard_map/ppermute | solution.py:41
  63.5 2.8 %collective-permute-start.33 = (bf16[128,512]{1,0:T(8,128)(2,1)S(1)}, bf16[128,512]{1,0:T(8,128)(2,1)S(1)}, u32[]{:S(2)}, u32[]{:S(2)}) collective-permute-start(bf16[128,512]{1,0:T(8,128)(2,1)S(1)} %get-tuple-element.89), channel_id=1, source_target_pairs={{0,16},{4,20},{8,24},{12,28},{16,0},{20,4},{24,8},{28,12},{1,17},{... | collective-permute-start | bytes 393224 | tf_op jit(solution)/shard_map/ppermute | solution.py:41
  68.1 4.2 %attend_back.1 = (bf16[384,128]{1,0:T(8,128)(2,1)S(1)}, bf16[384,128]{1,0:T(8,128)(2,1)S(1)}, bf16[384,128]{1,0:T(8,128)(2,1)S(1)}, bf16[384,128]{1,0:T(8,128)(2...) custom-call(s32[2]{0:T(128)S(1)} %pad_add_fusion.ids, ...), custom_call_target="tpu_custom_call" | custom-call | flops 5368709120 | bytes 2097152 | tf_op jit(solution)/shard_map/attend_back/pallas_call | solution.py:198
  72.3 1.8 %collective-permute-start.18 = (bf16[384,128]{1,0:T(8,128)(2,1)S(1)}, bf16[384,128]{1,0:T(8,128)(2,1)S(1)}, u32[]{:S(2)}, u32[]{:S(2)}) collective-permute-start(bf16[384,128]{1,0:T(8,128)(2,1)S(1)} %get-tuple-element.73), channel_id=1, source_target_pairs={{0,4},{4,0},{8,12},{12,8},{16,20},{20,16},{24,28},{28,24},{1,5},{5... | collective-permute-start | bytes 294920 | tf_op jit(solution)/shard_map/ppermute | solution.py:41
  75.2 3.2 %collective-permute-start.20 = (bf16[384,128]{1,0:T(8,128)(2,1)S(1)}, bf16[384,128]{1,0:T(8,128)(2,1)S(1)}, u32[]{:S(2)}, u32[]{:S(2)}) collective-permute-start(bf16[384,128]{1,0:T(8,128)(2,1)S(1)} %get-tuple-element.75), channel_id=1, source_target_pairs={{0,12},{4,8},{8,4},{12,0},{16,28},{20,24},{24,20},{28,16},{1,13},{... | collective-permute-start | bytes 294920 | tf_op jit(solution)/shard_map/ppermute | solution.py:41
  79.3 1.7 %collective-permute-start.22 = (bf16[384,128]{1,0:T(8,128)(2,1)S(1)}, bf16[384,128]{1,0:T(8,128)(2,1)S(1)}, u32[]{:S(2)}, u32[]{:S(2)}) collective-permute-start(bf16[384,128]{1,0:T(8,128)(2,1)S(1)} %get-tuple-element.77), channel_id=1, source_target_pairs={{0,20},{4,16},{8,28},{12,24},{16,4},{20,0},{24,12},{28,8},{1,21},{... | collective-permute-start | bytes 294920 | tf_op jit(solution)/shard_map/ppermute | solution.py:41
  81.1 1.8 %collective-permute-start.10 = (bf16[512,128]{1,0:T(8,128)(2,1)S(1)}, bf16[512,128]{1,0:T(8,128)(2,1)S(1)}, u32[]{:S(2)}, u32[]{:S(2)}) collective-permute-start(bf16[512,128]{1,0:T(8,128)(2,1)S(1)} %get-tuple-element.61), channel_id=1, source_target_pairs={{0,4},{4,0},{8,12},{12,8},{16,20},{20,16},{24,28},{28,24},{1,5},{5... | collective-permute-start | bytes 393224 | tf_op jit(solution)/shard_map/ppermute | solution.py:41
  82.8 2.3 %collective-permute-start.23 = (bf16[384,128]{1,0:T(8,128)(2,1)S(1)}, bf16[384,128]{1,0:T(8,128)(2,1)S(1)}, u32[]{:S(2)}, u32[]{:S(2)}) collective-permute-start(bf16[384,128]{1,0:T(8,128)(2,1)S(1)} %get-tuple-element.78), channel_id=1, source_target_pairs={{0,24},{4,28},{8,16},{12,20},{16,8},{20,12},{24,0},{28,4},{1,25},{... | collective-permute-start | bytes 294920 | tf_op jit(solution)/shard_map/ppermute | solution.py:41
  85.1 6.2 %collective-permute-done.21.refs_4_ = bf16[384,128]{1,0:T(8,128)(2,1)S(1)} collective-permute-done((bf16[384,128]{1,0:T(8,128)(2,1)S(1)}, bf16[384,128]{1,0:T(8,128)(2,1)S(1)}, u32[]{:S(2)}, u32[]{:S(2)}) %collective-permute-start.21) | collective-permute-done | bytes 98336 | tf_op jit(solution)/shard_map/ppermute | solution.py:41
  91.3 1.8 %collective-permute-start.24 = (bf16[384,128]{1,0:T(8,128)(2,1)S(1)}, bf16[384,128]{1,0:T(8,128)(2,1)S(1)}, u32[]{:S(2)}, u32[]{:S(2)}) collective-permute-start(bf16[384,128]{1,0:T(8,128)(2,1)S(1)} %get-tuple-element.79), channel_id=1, source_target_pairs={{0,28},{4,24},{8,20},{12,16},{16,12},{20,8},{24,4},{28,0},{1,29},{... | collective-permute-start | bytes 294920 | tf_op jit(solution)/shard_map/ppermute | solution.py:41
  95.2 3.5 %collective-permute-done.24.refs_7_ = bf16[384,128]{1,0:T(8,128)(2,1)S(1)} collective-permute-done((bf16[384,128]{1,0:T(8,128)(2,1)S(1)}, bf16[384,128]{1,0:T(8,128)(2,1)S(1)}, u32[]{:S(2)}, u32[]{:S(2)}) %collective-permute-start.24) | collective-permute-done | bytes 98336 | tf_op jit(solution)/shard_map/ppermute | solution.py:41
  98.6 1.6 %unpack_grads.1 = (bf16[128,1024]{1,0:T(8,128)(2,1)}, bf16[128,1024]{1,0:T(8,128)(2,1)}, bf16[128,1024]{1,0:T(8,128)(2,1)}) custom-call(s32[2]{0:T(128)S(1)} %pad_add_fusion.ids, bf16[384,128]{1,0:T(8,128)(2,1)S(1)} %get-tuple-element.72.refs_0_, bf16[384,128]{1,0:T(8,128)(2,1)S(1)} %collective-permute-done.18.refs_1_, ...), custom_call_target="tpu_custom_call" | custom-call | tf_op jit(solution)/shard_map/unpack_grads/pallas_call | solution.py:222
  100.3 3.2 %project.1 = bf16[128,2048]{1,0:T(8,128)(2,1)} custom-call(s32[2]{0:T(128)S(1)} %pad_add_fusion.ids, bf16[1024,128]{1,0:T(8,128)(2,1)S(1)} %get-tuple-element.60.near.refs_0_, bf16[512,128]{1,0:T(8,128)(2,1)S(1)} %collective-permute-done.10.far, bf16[1024,2048]{1,0:T(8,128)(2,1)S(1)} %copy-done), custom_call_target="tpu_custom_call" | custom-call | flops 536870912 | bytes 4194304 | tf_op jit(solution)/shard_map/project/pallas_call | solution.py:265
  (86 shorter events, 30.0 us)
Async XLA Ops:
  4.3 11.6 %collective-permute-start = (bf16[384,128]{1,0:T(8,128)(2,1)S(1)}, bf16[384,128]{1,0:T(8,128)(2,1)S(1)}, u32[]{:S(2)}, u32[]{:S(2)}) collective-permute-start(bf16[384,128]{1,0:T(8,128)(2,1)S(1)} %get-tuple-element.49), channel_id=1, source_target_pairs={{0,4},{4,0},{8,12},{12,8},{16,20},{20,16},{24,28},{28,24},{1,5},{5... | collective-permute-start | bytes 294920 | tf_op jit(solution)/shard_map/ppermute | solution.py:41
  7.3 12.3 %collective-permute-start.1 = (bf16[384,128]{1,0:T(8,128)(2,1)S(1)}, bf16[384,128]{1,0:T(8,128)(2,1)S(1)}, u32[]{:S(2)}, u32[]{:S(2)}) collective-permute-start(bf16[384,128]{1,0:T(8,128)(2,1)S(1)} %get-tuple-element.50), channel_id=1, source_target_pairs={{0,8},{4,12},{8,0},{12,4},{16,24},{20,28},{24,16},{28,20},{1,9},{5... | collective-permute-start | bytes 294920 | tf_op jit(solution)/shard_map/ppermute | solution.py:41
  8.9 10.8 %collective-permute-start.2 = (bf16[384,128]{1,0:T(8,128)(2,1)S(1)}, bf16[384,128]{1,0:T(8,128)(2,1)S(1)}, u32[]{:S(2)}, u32[]{:S(2)}) collective-permute-start(bf16[384,128]{1,0:T(8,128)(2,1)S(1)} %get-tuple-element.51), channel_id=1, source_target_pairs={{0,12},{4,8},{8,4},{12,0},{16,28},{20,24},{24,20},{28,16},{1,13},{... | collective-permute-start | bytes 294920 | tf_op jit(solution)/shard_map/ppermute | solution.py:41
  8.9 10.9 %collective-permute-start.3 = (bf16[384,128]{1,0:T(8,128)(2,1)S(1)}, bf16[384,128]{1,0:T(8,128)(2,1)S(1)}, u32[]{:S(2)}, u32[]{:S(2)}) collective-permute-start(bf16[384,128]{1,0:T(8,128)(2,1)S(1)} %get-tuple-element.52), channel_id=1, source_target_pairs={{0,16},{4,20},{8,24},{12,28},{16,0},{20,4},{24,8},{28,12},{1,17},{... | collective-permute-start | bytes 294920 | tf_op jit(solution)/shard_map/ppermute | solution.py:41
  11.9 15.1 %collective-permute-start.4 = (bf16[384,128]{1,0:T(8,128)(2,1)S(1)}, bf16[384,128]{1,0:T(8,128)(2,1)S(1)}, u32[]{:S(2)}, u32[]{:S(2)}) collective-permute-start(bf16[384,128]{1,0:T(8,128)(2,1)S(1)} %get-tuple-element.53), channel_id=1, source_target_pairs={{0,20},{4,16},{8,28},{12,24},{16,4},{20,0},{24,12},{28,8},{1,21},{... | collective-permute-start | bytes 294920 | tf_op jit(solution)/shard_map/ppermute | solution.py:41
  16.0 11.1 %collective-permute-start.5 = (bf16[384,128]{1,0:T(8,128)(2,1)S(1)}, bf16[384,128]{1,0:T(8,128)(2,1)S(1)}, u32[]{:S(2)}, u32[]{:S(2)}) collective-permute-start(bf16[384,128]{1,0:T(8,128)(2,1)S(1)} %get-tuple-element.54), channel_id=1, source_target_pairs={{0,24},{4,28},{8,16},{12,20},{16,8},{20,12},{24,0},{28,4},{1,25},{... | collective-permute-start | bytes 294920 | tf_op jit(solution)/shard_map/ppermute | solution.py:41
  19.7 16.7 %collective-permute-start.28 = (bf16[128,512]{1,0:T(8,128)(2,1)S(1)}, bf16[128,512]{1,0:T(8,128)(2,1)S(1)}, u32[]{:S(2)}, u32[]{:S(2)}) collective-permute-start(bf16[128,512]{1,0:T(8,128)(2,1)S(1)} %get-tuple-element.84), channel_id=1, source_target_pairs={{0,1},{1,0},{2,3},{3,2},{4,5},{5,4},{6,7},{7,6},{8,9},{9,8},{10,11... | collective-permute-start | bytes 393224 | tf_op jit(solution)/shard_map/ppermute | solution.py:41
  19.8 18.1 %collective-permute-start.29 = (bf16[128,512]{1,0:T(8,128)(2,1)S(1)}, bf16[128,512]{1,0:T(8,128)(2,1)S(1)}, u32[]{:S(2)}, u32[]{:S(2)}) collective-permute-start(bf16[128,512]{1,0:T(8,128)(2,1)S(1)} %get-tuple-element.85), channel_id=1, source_target_pairs={{0,2},{1,3},{2,0},{3,1},{4,6},{5,7},{6,4},{7,5},{8,10},{9,11},{10,... | collective-permute-start | bytes 393224 | tf_op jit(solution)/shard_map/ppermute | solution.py:41
  27.1 10.8 %collective-permute-start.30 = (bf16[128,512]{1,0:T(8,128)(2,1)S(1)}, bf16[128,512]{1,0:T(8,128)(2,1)S(1)}, u32[]{:S(2)}, u32[]{:S(2)}) collective-permute-start(bf16[128,512]{1,0:T(8,128)(2,1)S(1)} %get-tuple-element.86), channel_id=1, source_target_pairs={{0,3},{1,2},{2,1},{3,0},{4,7},{5,6},{6,5},{7,4},{8,11},{9,10},{10,... | collective-permute-start | bytes 393224 | tf_op jit(solution)/shard_map/ppermute | solution.py:41
  37.9 20.8 %collective-permute-start.31 = (bf16[512,512]{1,0:T(8,128)(2,1)S(1)}, bf16[512,512]{1,0:T(8,128)(2,1)S(1)}, u32[]{:S(2)}, u32[]{:S(2)}) collective-permute-start(bf16[512,512]{1,0:T(8,128)(2,1)S(1)} %constant_dynamic-update-slice_fusion.refs_4_), channel_id=1, source_target_pairs={{0,4},{4,0},{8,12},{12,8},{16,20},{20,16},{24,28},{28,24},{1,5},{5... | collective-permute-start | bytes 1572872 | tf_op jit(solution)/shard_map/ppermute | solution.py:41
  43.3 12.7 %collective-permute-start.26 = (bf16[1024,128]{1,0:T(8,128)(2,1)S(1)}, bf16[1024,128]{1,0:T(8,128)(2,1)S(1)}, u32[]{:S(2)}, u32[]{:S(2)}) collective-permute-start(bf16[1024,128]{1,0:T(8,128)(2,1)S(1)} %get-tuple-element.60.near.refs_0_), channel_id=1, source_target_pairs={{0,2},{1,3},{2,0},{3,1},{4,6},{5,7},{6,4},{7,5},{8,10},{9,11},{10,... | collective-permute-start | bytes 786440 | tf_op jit(solution)/shard_map/ppermute | solution.py:41
  44.9 16.1 %collective-permute-start.27 = (bf16[1024,128]{1,0:T(8,128)(2,1)S(1)}, bf16[1024,128]{1,0:T(8,128)(2,1)S(1)}, u32[]{:S(2)}, u32[]{:S(2)}) collective-permute-start(bf16[1024,128]{1,0:T(8,128)(2,1)S(1)} %collective-permute-done.25.refs_1_), channel_id=1, source_target_pairs={{0,2},{1,3},{2,0},{3,1},{4,6},{5,7},{6,4},{7,5},{8,10},{9,11},{10,... | collective-permute-start | bytes 786440 | tf_op jit(solution)/shard_map/ppermute | solution.py:41
  53.7 9.8 %collective-permute-start.13 = (bf16[128,128]{1,0:T(8,128)(2,1)S(1)}, bf16[128,128]{1,0:T(8,128)(2,1)S(1)}, u32[]{:S(2)}, u32[]{:S(2)}) collective-permute-start(bf16[128,128]{1,0:T(8,128)(2,1)S(1)} %get-tuple-element.67), channel_id=1, source_target_pairs={{0,12},{4,8},{8,4},{12,0},{16,28},{20,24},{24,20},{28,16},{1,13},{... | collective-permute-start | bytes 98312 | tf_op jit(solution)/shard_map/ppermute | solution.py:41
  56.0 10.3 %collective-permute-start.15 = (bf16[128,128]{1,0:T(8,128)(2,1)S(1)}, bf16[128,128]{1,0:T(8,128)(2,1)S(1)}, u32[]{:S(2)}, u32[]{:S(2)}) collective-permute-start(bf16[128,128]{1,0:T(8,128)(2,1)S(1)} %get-tuple-element.69), channel_id=1, source_target_pairs={{0,20},{4,16},{8,28},{12,24},{16,4},{20,0},{24,12},{28,8},{1,21},{... | collective-permute-start | bytes 98312 | tf_op jit(solution)/shard_map/ppermute | solution.py:41
  58.7 9.1 %collective-permute-start.16 = (bf16[128,128]{1,0:T(8,128)(2,1)S(1)}, bf16[128,128]{1,0:T(8,128)(2,1)S(1)}, u32[]{:S(2)}, u32[]{:S(2)}) collective-permute-start(bf16[128,128]{1,0:T(8,128)(2,1)S(1)} %get-tuple-element.70), channel_id=1, source_target_pairs={{0,24},{4,28},{8,16},{12,20},{16,8},{20,12},{24,0},{28,4},{1,25},{... | collective-permute-start | bytes 98312 | tf_op jit(solution)/shard_map/ppermute | solution.py:41
  63.4 10.7 %collective-permute-start.32 = (bf16[128,512]{1,0:T(8,128)(2,1)S(1)}, bf16[128,512]{1,0:T(8,128)(2,1)S(1)}, u32[]{:S(2)}, u32[]{:S(2)}) collective-permute-start(bf16[128,512]{1,0:T(8,128)(2,1)S(1)} %get-tuple-element.88), channel_id=1, source_target_pairs={{0,8},{4,12},{8,0},{12,4},{16,24},{20,28},{24,16},{28,20},{1,9},{5... | collective-permute-start | bytes 393224 | tf_op jit(solution)/shard_map/ppermute | solution.py:41
  63.5 11.5 %collective-permute-start.33 = (bf16[128,512]{1,0:T(8,128)(2,1)S(1)}, bf16[128,512]{1,0:T(8,128)(2,1)S(1)}, u32[]{:S(2)}, u32[]{:S(2)}) collective-permute-start(bf16[128,512]{1,0:T(8,128)(2,1)S(1)} %get-tuple-element.89), channel_id=1, source_target_pairs={{0,16},{4,20},{8,24},{12,28},{16,0},{20,4},{24,8},{28,12},{1,17},{... | collective-permute-start | bytes 393224 | tf_op jit(solution)/shard_map/ppermute | solution.py:41
  75.1 18.7 %collective-permute-start.35 = (bf16[128,512]{1,0:T(8,128)(2,1)S(1)}, bf16[128,512]{1,0:T(8,128)(2,1)S(1)}, u32[]{:S(2)}, u32[]{:S(2)}) collective-permute-start(bf16[128,512]{1,0:T(8,128)(2,1)S(1)} %weight_sum.1.refs_0_), channel_id=1, source_target_pairs={{0,1},{1,0},{2,3},{3,2},{4,5},{5,4},{6,7},{7,6},{8,9},{9,8},{10,11... | collective-permute-start | bytes 393224 | tf_op jit(solution)/shard_map/ppermute | solution.py:41
  78.4 12.9 %collective-permute-start.21 = (bf16[384,128]{1,0:T(8,128)(2,1)S(1)}, bf16[384,128]{1,0:T(8,128)(2,1)S(1)}, u32[]{:S(2)}, u32[]{:S(2)}) collective-permute-start(bf16[384,128]{1,0:T(8,128)(2,1)S(1)} %get-tuple-element.76), channel_id=1, source_target_pairs={{0,16},{4,20},{8,24},{12,28},{16,0},{20,4},{24,8},{28,12},{1,17},{... | collective-permute-start | bytes 294920 | tf_op jit(solution)/shard_map/ppermute | solution.py:41
  79.3 13.8 %collective-permute-start.22 = (bf16[384,128]{1,0:T(8,128)(2,1)S(1)}, bf16[384,128]{1,0:T(8,128)(2,1)S(1)}, u32[]{:S(2)}, u32[]{:S(2)}) collective-permute-start(bf16[384,128]{1,0:T(8,128)(2,1)S(1)} %get-tuple-element.77), channel_id=1, source_target_pairs={{0,20},{4,16},{8,28},{12,24},{16,4},{20,0},{24,12},{28,8},{1,21},{... | collective-permute-start | bytes 294920 | tf_op jit(solution)/shard_map/ppermute | solution.py:41
  81.1 19.2 %collective-permute-start.10 = (bf16[512,128]{1,0:T(8,128)(2,1)S(1)}, bf16[512,128]{1,0:T(8,128)(2,1)S(1)}, u32[]{:S(2)}, u32[]{:S(2)}) collective-permute-start(bf16[512,128]{1,0:T(8,128)(2,1)S(1)} %get-tuple-element.61), channel_id=1, source_target_pairs={{0,4},{4,0},{8,12},{12,8},{16,20},{20,16},{24,28},{28,24},{1,5},{5... | collective-permute-start | bytes 393224 | tf_op jit(solution)/shard_map/ppermute | solution.py:41
  82.8 12.3 %collective-permute-start.23 = (bf16[384,128]{1,0:T(8,128)(2,1)S(1)}, bf16[384,128]{1,0:T(8,128)(2,1)S(1)}, u32[]{:S(2)}, u32[]{:S(2)}) collective-permute-start(bf16[384,128]{1,0:T(8,128)(2,1)S(1)} %get-tuple-element.78), channel_id=1, source_target_pairs={{0,24},{4,28},{8,16},{12,20},{16,8},{20,12},{24,0},{28,4},{1,25},{... | collective-permute-start | bytes 294920 | tf_op jit(solution)/shard_map/ppermute | solution.py:41
  93.1 10.3 %collective-permute-start.36 = (bf16[128,512]{1,0:T(8,128)(2,1)S(1)}, bf16[128,512]{1,0:T(8,128)(2,1)S(1)}, u32[]{:S(2)}, u32[]{:S(2)}) collective-permute-start(bf16[128,512]{1,0:T(8,128)(2,1)S(1)} %weight_sum.1.refs_0_), channel_id=1, source_target_pairs={{0,2},{1,3},{2,0},{3,1},{4,6},{5,7},{6,4},{7,5},{8,10},{9,11},{10,... | collective-permute-start | bytes 393224 | tf_op jit(solution)/shard_map/ppermute | solution.py:41
  93.8 9.7 %collective-permute-start.37 = (bf16[128,512]{1,0:T(8,128)(2,1)S(1)}, bf16[128,512]{1,0:T(8,128)(2,1)S(1)}, u32[]{:S(2)}, u32[]{:S(2)}) collective-permute-start(bf16[128,512]{1,0:T(8,128)(2,1)S(1)} %collective-permute-done.35.refs_1_), channel_id=1, source_target_pairs={{0,2},{1,3},{2,0},{3,1},{4,6},{5,7},{6,4},{7,5},{8,10},{9,11},{10,... | collective-permute-start | bytes 393224 | tf_op jit(solution)/shard_map/ppermute | solution.py:41
  (20 other events, 134.7 us)

commit v2 on v0

--- a/solution.py
+++ b/solution.py
@@ -1,15 +1,523 @@
+import functools
 import math
 
 import jax
 import jax.numpy as jnp
 from jax import lax
+from jax.experimental import pallas as pl
+from jax.experimental.pallas import tpu as pltpu
 from jax.sharding import PartitionSpec as P
 
 HD = 128
 BLK = 64
+MASKED = -1e30
+VMEM = pltpu.VMEM
+ANY_SPEC = pl.BlockSpec(memory_space=pl.ANY)
+VMEM_SPEC = pl.BlockSpec()
+NT = (((1,), (1,)), ((), ()))
+NN = (((1,), (0,)), ((), ()))
+TN = (((0,), (0,)), ((), ()))
+WIDE = 58
+PROJECT_FLOPS = 4 << 30
+JOIN_FLOPS = 2 << 30
+
+
+def dot(left, right, dims):
+    return lax.dot_general(left, right, dims, preferred_element_type=jnp.float32)
+
+
+def params(mib):
+    return pltpu.CompilerParams(vmem_limit_bytes=mib * 1024 * 1024)
+
+
+def cost(flops=1, moved=1):
+    return pl.CostEstimate(flops=flops, bytes_accessed=moved, transcendentals=0)
+
+
+def struct(*shape, dtype=jnp.bfloat16):
+    return jax.ShapeDtypeStruct(shape, dtype)
+
+
+def span(index, size):
+    return pl.ds(pl.multiple_of(index * size, size), size)
+
+
+def swap(array, axis, mask):
+    return lax.ppermute(array, axis, [(i, i ^ mask) for i in range(lax.axis_size(axis))])
+
+
+def gather_rep(block):
+    blocks, bit = {0: block}, lax.axis_size("rep") // 2
+    while bit:
+        blocks |= {mask | bit: swap(item, "rep", bit) for mask, item in blocks.items()}
+        bit //= 2
+    return [blocks[mask] for mask in sorted(blocks)]
+
+
+def after(*arrays):
+    return lax.optimization_barrier(arrays)
+
+
+def anchored(kernel):
+    return lambda anchor, *refs: kernel(*refs)
+
+
+def members_of(peers):
+    return peers // 2
+
+
+def member(mask=0):
+    return (lax.axis_index("seq") ^ mask) & (members_of(lax.axis_size("seq")) - 1)
+
+
+def half_of():
+    return lax.axis_index("seq") // members_of(lax.axis_size("seq"))
+
+
+def pack_kernel(key_ref, value_ref, send, *refs):
+    held, sem = refs[:2], refs[2]
+    rows, width = key_ref.shape
+    peers = send.shape[0]
+    loads = [
+        pltpu.make_async_copy(source, target, sem.at[index])
+        for index, (source, target) in enumerate(zip((key_ref, value_ref), held))
+    ]
+    for load in loads:
+        load.start()
+    for index, source in enumerate(held):
+        loads[index].wait()
+        for peer in range(peers):
+            for slot in range(2):
+                head = peer % members_of(peers) + slot * members_of(peers)
+                place = pl.ds((2 * index + slot) * rows, rows)
+                send[peer, place] = source[:, head * HD : (head + 1) * HD]
+
+
+def pack(keys, values, peers):
+    rows, width = keys.shape
+    return pl.pallas_call(
+        pack_kernel,
+        out_shape=struct(peers, 4 * rows, HD),
+        in_specs=[ANY_SPEC] * 2,
+        out_specs=VMEM_SPEC,
+        scratch_shapes=[VMEM((rows, width), jnp.bfloat16)] * 2 + [pltpu.SemaphoreType.DMA((2,))],
+        compiler_params=params(WIDE),
+        cost_estimate=cost(),
+        name="pack_keys",
+    )(keys, values)
+
+
+def head_grad_kernel(query_ref, grad_ref, weight_ref, *refs):
+    sends, (query, grad, weight, head_grad, sem) = refs[:-5], refs[-5:]
+    rows = query_ref.shape[0]
+    members = len(sends)
+    loads = [
+        pltpu.make_async_copy(source, target, sem.at[index])
+        for index, (source, target) in enumerate(
+            zip((query_ref, grad_ref, weight_ref), (query, grad, weight))
+        )
+    ]
+    for load in loads:
+        load.start()
+    loads[0].wait()
+    for mask, send in enumerate(sends):
+        for slot in range(2):
+            send[slot * rows : (slot + 1) * rows] = query[:, span(member(mask) + slot * members, HD)]
+    loads[1].wait()
+    loads[2].wait()
+    head_grad[...] = dot(weight[...], grad[...], NT).astype(jnp.bfloat16)
+    for mask, send in enumerate(sends):
+        for slot in range(2):
+            place = pl.ds(2 * rows + slot * HD, HD)
+            send[place] = head_grad[span(member(mask) + slot * members, HD)]
+
+
+def head_grads(queries, grads, out_weight, members):
+    rows, width = queries.shape
+    return pl.pallas_call(
+        head_grad_kernel,
+        out_shape=[struct(2 * rows + 2 * HD, HD)] * members,
+        in_specs=[ANY_SPEC] * 3,
+        out_specs=[VMEM_SPEC] * members,
+        scratch_shapes=[
+            VMEM(queries.shape, jnp.bfloat16),
+            VMEM(grads.shape, jnp.bfloat16),
+            VMEM(out_weight.shape, jnp.bfloat16),
+            VMEM((width, rows), jnp.bfloat16),
+            pltpu.SemaphoreType.DMA((3,)),
+        ],
+        compiler_params=params(24),
+        cost_estimate=cost(),
+        name="head_grads",
+    )(queries, grads, out_weight)
+
+
+def join_queries_kernel(*refs):
+    parts, (queries, grads) = refs[:-2], refs[-2:]
+    rows = parts[0].shape[0] // 4
+    for mask, part in enumerate(parts):
+        for slot in range(2):
+            queries[slot, span(member(mask), rows)] = part[slot * rows : (slot + 1) * rows]
+            grad = part[2 * rows + slot * HD : 2 * rows + (slot + 1) * HD]
+            grads[slot, :, span(member(mask), rows)] = grad
+
+
+def join_queries(parts):
+    tokens = len(parts) * parts[0].shape[0] // 4
+    return pl.pallas_call(
+        join_queries_kernel,
+        out_shape=[struct(2, tokens, HD), struct(2, HD, tokens)],
+        in_specs=[VMEM_SPEC] * len(parts),
+        out_specs=[VMEM_SPEC] * 2,
+        compiler_params=params(8),
+        cost_estimate=cost(JOIN_FLOPS),
+        name="join_queries",
+    )(*parts)
+
+
+def load_heads(pairs, keys, values):
+    rows = pairs.shape[1] // 4
+    for peer in range(pairs.shape[0]):
+        for slot in range(2):
+            place = slice(peer * rows, (peer + 1) * rows)
+            keys[slot, place] = pairs[peer, slot * rows : (slot + 1) * rows]
+            values[slot, place] = pairs[peer, (2 + slot) * rows : (3 + slot) * rows]
+
+
+def scores_of(keys, queries, bias, scale):
+    blocks = bias.shape[0]
+    scores = dot(keys, queries, NT) * scale
+    shaped = scores.reshape(blocks, BLK, queries.shape[0]) + bias[:, None, :]
+    return shaped.reshape(scores.shape)
+
+
+def forward_kernel(chunk, scale, bias_ref, pairs, queries, near, top_ref, sum_ref, keys, values):
+    load_heads(pairs, keys, values)
+    tokens = queries.shape[1]
+    for slot in range(2):
+        value_cols = values[slot].T
+        for step in range(tokens // chunk):
+            rows = slice(step * chunk, (step + 1) * chunk)
+            bias = bias_ref[:, span(half_of() * (tokens // chunk) + step, chunk)]
+            scores = scores_of(keys[slot], queries[slot, rows], bias, scale)
+            top = jnp.max(scores, axis=0, keepdims=True)
+            weights = jnp.exp(scores - top)
+            total = 1.0 / jnp.sum(weights, axis=0, keepdims=True)
+            probs_low = (weights * total).astype(jnp.bfloat16)
+            place = pl.ds(slot * tokens + step * chunk, chunk)
+            near[place] = dot(value_cols, probs_low, NN).T.astype(jnp.bfloat16)
+            top_ref[slot : slot + 1, rows] = top
+            sum_ref[slot : slot + 1, rows] = total
+
+
+def forward(bias, pairs, queries, scale):
+    tokens = bias.shape[1]
+    chunk = 2 * tokens // pairs.shape[0]
+    stats = struct(2, tokens // 2, dtype=jnp.float32)
+    return pl.pallas_call(
+        functools.partial(forward_kernel, chunk, scale),
+        out_shape=[struct(tokens, HD), stats, stats],
+        in_specs=[VMEM_SPEC] * 3,
+        out_specs=[VMEM_SPEC] * 3,
+        scratch_shapes=[VMEM((2, tokens, HD), jnp.bfloat16)] * 2,
+        compiler_params=params(24),
+        cost_estimate=cost(),
+        name="attend",
+    )(bias, pairs, queries)
+
+
+def backward_kernel(chunk, scale, bias_ref, top_ref, sum_ref, pairs, queries, grads, near, *refs):
+    returns, outs, (keys, values, query_grad, key_sum, value_sum) = refs[0], refs[1:-5], refs[-5:]
+    load_heads(pairs, keys, values)
+    tokens = queries.shape[1]
+    peers = returns.shape[0]
+    here = returns.shape[1] // 4
+    for slot in range(2):
+        key_cols = keys[slot].T
+        for step in range(tokens // chunk):
+            rows = slice(step * chunk, (step + 1) * chunk)
+            bias = bias_ref[:, span(half_of() * (tokens // chunk) + step, chunk)]
+            scores = scores_of(keys[slot], queries[slot, rows], bias, scale)
+            probs = jnp.exp(scores - top_ref[slot : slot + 1, rows]) * sum_ref[slot : slot + 1, rows]
+            prob_grad = dot(values[slot], grads[slot, :, rows], NN)
+            delta = jnp.sum(probs * prob_grad, axis=0, keepdims=True)
+            score_grad = (probs * (prob_grad - delta)).astype(jnp.bfloat16)
+            value_part = dot(probs.astype(jnp.bfloat16), grads[slot, :, rows], NT)
+            key_part = dot(score_grad, queries[slot, rows], NN)
+            if step == 0:
+                value_sum[...] = value_part
+                key_sum[...] = key_part
+            else:
+                value_sum[...] += value_part
+                key_sum[...] += key_part
+            query_part = dot(key_cols, score_grad, NN) * scale
+            query_grad[slot, rows] = query_part.T.astype(jnp.bfloat16)
+        for peer in range(peers):
+            place = slice(peer * here, (peer + 1) * here)
+            key_low = (key_sum[place] * scale).astype(jnp.bfloat16)
+            returns[peer, slot * here : (slot + 1) * here] = key_low
+            value_low = value_sum[place].astype(jnp.bfloat16)
+            returns[peer, (2 + slot) * here : (3 + slot) * here] = value_low
+        for mask, out in enumerate(outs):
+            theirs = span(member(mask), here)
+            out[slot * here : (slot + 1) * here] = query_grad[slot, theirs]
+            theirs = span(slot * len(outs) + member(mask), here)
+            out[(2 + slot) * here : (3 + slot) * here] = near[theirs]
+
+
+def backward(bias, top, total, pairs, queries, grads, near, scale):
+    peers, tokens = pairs.shape[0], bias.shape[1]
+    members = members_of(peers)
+    here = tokens // peers
+    return pl.pallas_call(
+        functools.partial(backward_kernel, 2 * here, scale),
+        out_shape=[struct(peers, 4 * here, HD)] + [struct(4 * here, HD)] * members,
+        in_specs=[VMEM_SPEC] * 7,
+        out_specs=[VMEM_SPEC] * (1 + members),
+        scratch_shapes=[VMEM((2, tokens, HD), jnp.bfloat16)] * 2
+        + [VMEM((2, tokens // 2, HD), jnp.bfloat16)]
+        + [VMEM((tokens, HD), jnp.float32)] * 2,
+        compiler_params=params(24),
+        cost_estimate=cost(),
+        name="attend_back",
+    )(bias, top, total, pairs, queries, grads, near)
+
+
+def unpack_kernel(returned, *refs):
+    queries, (query_grad, key_grad, value_grad, token) = refs[:-4], refs[-4:]
+    token[...] = jnp.zeros_like(token)
+    members = len(queries)
+    here = query_grad.shape[0]
+    for index in range(members):
+        for slot in range(2):
+            columns = pl.ds((index + slot * members) * HD, HD)
+            for target, first in ((key_grad, slot), (value_grad, 2 + slot)):
+                rows = slice(first * here, (first + 1) * here)
+                both = returned[index, rows].astype(jnp.float32) + returned[
+                    index + members, rows
+                ].astype(jnp.float32)
+                target[:, columns] = both.astype(jnp.bfloat16)
+            part = queries[index][slot * here : (slot + 1) * here]
+            query_grad[:, span(member(index) + slot * members, HD)] = part
+
+
+def unpack(returned, queries, rows, width):
+    return pl.pallas_call(
+        unpack_kernel,
+        out_shape=[struct(rows, width)] * 3 + [struct(16, HD)],
+        in_specs=[VMEM_SPEC] * (1 + len(queries)),
+        out_specs=[VMEM_SPEC] * 4,
+        compiler_params=params(16),
+        cost_estimate=cost(1, 24 * rows * width),
+        name="unpack_grads",
+    )(returned, *queries)
+
+
+def project_kernel(*refs):
+    parts, (weight_ref, out_ref, token, attended) = refs[:-4], refs[-4:]
+    token[...] = jnp.zeros_like(token)
+    rows = out_ref.shape[0]
+
+    @pl.when(pl.program_id(0) == 0)
+    def _():
+        for mask, part in enumerate(parts):
+            for slot in range(2):
+                columns = span(member(mask) + slot * len(parts), HD)
+                attended[:, columns] = part[(2 + slot) * rows : (3 + slot) * rows]
+
+    out_ref[...] = dot(attended[...], weight_ref[...], NN).astype(jnp.bfloat16)
+
+
+def project(parts, out_weight):
+    rows = parts[0].shape[0] // 4
+    depth, width = out_weight.shape
+    tile = width // 4
+    return pl.pallas_call(
+        project_kernel,
+        out_shape=[struct(rows, width), struct(16, HD)],
+        grid=(width // tile,),
+        in_specs=[pl.BlockSpec(part.shape, lambda i: (0, 0)) for part in parts]
+        + [pl.BlockSpec((depth, tile), lambda i: (0, i))],
+        out_specs=[
+            pl.BlockSpec((rows, tile), lambda i: (0, i)),
+            pl.BlockSpec((16, HD), lambda i: (0, 0)),
+        ],
+        scratch_shapes=[VMEM((rows, depth), jnp.bfloat16)],
+        compiler_params=params(24),
+        cost_estimate=cost(PROJECT_FLOPS, 1),
+        name="project",
+    )(*parts, out_weight)
+
+
+def weight_part_kernel(docs, near, *refs):
+    grads, (own, send) = refs[:-2], refs[-2:]
+    members = len(grads)
+    rows = grads[0].shape[0]
+    width = grads[0].shape[1] // docs
+    lefts = []
+    for slot in range(2):
+        places = [span(slot * members + member(mask), rows) for mask in range(members)]
+        lefts.append(jnp.concatenate([near[place] for place in places], axis=0).T)
+    for mask in range(docs):
+        columns = span(lax.axis_index("rep") ^ mask, width)
+        right = jnp.concatenate([grad[:, columns] for grad in grads], axis=0)
+        for slot, left in enumerate(lefts):
+            place = pl.ds((mask // 2 * 2 + slot) * HD, HD)
+            if mask % 2:
+                send[place] = dot(left, right, NN).astype(jnp.bfloat16)
+            else:
+                own[place] = dot(left, right, NN)
+
+
+def weight_parts(near, grads, docs):
+    width = grads[0].shape[1] // docs
+    return pl.pallas_call(
+        functools.partial(weight_part_kernel, docs),
+        out_shape=[
+            struct(docs * HD, width, dtype=jnp.float32),
+            struct(docs * HD, width),
+        ],
+        in_specs=[VMEM_SPEC] * (1 + len(grads)),
+        out_specs=[VMEM_SPEC] * 2,
+        compiler_params=params(24),
+        cost_estimate=cost(),
+        name="weight_part",
+    )(near, *grads)
+
+
+def weight_fold_kernel(own, other, keep, send):
+    rows = keep.shape[0]
+    keep[...] = own[:rows] + other[:rows].astype(jnp.float32)
+    send[...] = (own[rows:] + other[rows:].astype(jnp.float32)).astype(jnp.bfloat16)
+
+
+def weight_fold(own, other):
+    rows, width = own.shape
+    return pl.pallas_call(
+        weight_fold_kernel,
+        out_shape=[struct(rows // 2, width, dtype=jnp.float32), struct(rows // 2, width)],
+        in_specs=[VMEM_SPEC] * 2,
+        out_specs=[VMEM_SPEC] * 2,
+        compiler_params=params(8),
+        cost_estimate=cost(),
+        name="weight_fold",
+    )(own, other)
+
+
+def weight_split_kernel(own, other, keep, send):
+    lower = half_of() == 0
+    rows = keep.shape[0]
+    first = own[:rows] + other[:rows].astype(jnp.float32)
+    second = own[rows:] + other[rows:].astype(jnp.float32)
+    keep[...] = jnp.where(lower, first, second)
+    send[...] = jnp.where(lower, second, first).astype(jnp.bfloat16)
+
+
+def weight_split(own, other):
+    rows, width = own.shape
+    return pl.pallas_call(
+        weight_split_kernel,
+        out_shape=[struct(rows // 2, width, dtype=jnp.float32), struct(rows // 2, width)],
+        in_specs=[VMEM_SPEC] * 2,
+        out_specs=[VMEM_SPEC] * 2,
+        compiler_params=params(8),
+        cost_estimate=cost(),
+        name="weight_split",
+    )(own, other)
+
+
+def weight_sum_kernel(factor, own, other, total):
+    total[...] = ((own[...] + other[...].astype(jnp.float32)) * factor).astype(jnp.bfloat16)
+
+
+def weight_sum(anchor, own, other, factor):
+    return pl.pallas_call(
+        anchored(functools.partial(weight_sum_kernel, factor)),
+        out_shape=struct(*own.shape),
+        in_specs=[ANY_SPEC] + [VMEM_SPEC] * 2,
+        out_specs=VMEM_SPEC,
+        compiler_params=params(8),
+        cost_estimate=cost(),
+        name="weight_sum",
+    )(anchor, own, other)
+
+
+def weight_join_kernel(*refs):
+    width = refs[0].shape[1]
+    for mask, part in enumerate(refs[:-1]):
+        refs[-1][:, span(lax.axis_index("rep") ^ mask, width)] = part[...].astype(jnp.float32)
+
+
+def weight_join(parts):
+    rows, width = parts[0].shape
+    return pl.pallas_call(
+        weight_join_kernel,
+        out_shape=struct(rows, width * len(parts), dtype=jnp.float32),
+        in_specs=[VMEM_SPEC] * len(parts),
+        out_specs=VMEM_SPEC,
+        compiler_params=params(8),
+        cost_estimate=cost(),
+        name="weight_join",
+    )(*parts)
+
+
+def dense_bias(pattern, tokens):
+    blocks = pattern.shape[0]
+    named = pattern[:, :, None] == jnp.arange(blocks, dtype=pattern.dtype)
+    counts = jnp.sum(named.astype(jnp.float32), axis=1).T
+    bias = jnp.where(counts > 0, jnp.log(jnp.maximum(counts, 1.0)), MASKED)
+    return jnp.repeat(bias, tokens // blocks, axis=1)
+
+
+def dense_local(query_in, key_in, value_in, out_weight, grad_out, pattern):
+    seq_count, rep_count = lax.axis_size("seq"), lax.axis_size("rep")
+    tokens_here = query_in.shape[1]
+    tokens = tokens_here * seq_count
+    members = members_of(seq_count)
+    scale = 1.0 / math.sqrt(HD)
+    bias = dense_bias(pattern, tokens)
+
+    pairs = lax.all_to_all(
+        pack(key_in[0], value_in[0], seq_count), "seq", split_axis=0, concat_axis=0, tiled=True
+    )
+    sends = head_grads(query_in[0], grad_out[0], out_weight, members)
+    parts = [sends[0]] + [swap(sends[mask], "seq", mask) for mask in range(1, members)]
+    grads, near_part = after(grad_out[0], parts[1])
+    queries, head_grad = join_queries(parts[:1] + [near_part] + parts[2:])
+    half_grads = [grads] + [swap(grads, "seq", mask) for mask in range(1, members)]
+
+    near, top, total = forward(bias, pairs, queries, scale)
+    returns, *sends = backward(bias, top, total, pairs, queries, head_grad, near, scale)
+    near, returns = after(near, returns)
+    returned = lax.all_to_all(returns, "seq", split_axis=0, concat_axis=0, tiled=True)
+    parts = [sends[0]] + [swap(sends[mask], "seq", mask) for mask in range(1, members)]
+
+    own, send = weight_parts(near, half_grads, rep_count)
+    bit = 1
+    while 2 * bit < rep_count:
+        own, send = weight_fold(own, swap(send, "rep", bit))
+        bit *= 2
+    own, send = weight_split(own, swap(send, "rep", bit))
+    other = swap(send, "seq", members)
+    mixed_out, token = project(parts, out_weight)
+    weight_quarter = weight_sum(token, own, other, 1.0 / math.sqrt(rep_count * tokens))
+    query_grad, key_grad, value_grad, token = unpack(
+        returned, parts, tokens_here, query_in.shape[2]
+    )
+    weight_grad = weight_join(gather_rep(weight_quarter))
+    return (mixed_out[None], query_grad[None], key_grad[None], value_grad[None], weight_grad)
 
 
 def local(query_in, key_in, value_in, out_weight, grad_out, pattern):
+    seq_count, rep_count = lax.axis_size("seq"), lax.axis_size("rep")
+    one_head_each = seq_count * HD == query_in.shape[2] and query_in.shape[0] == 1
+    paired = seq_count & (seq_count - 1) == 0 and rep_count == 4
+    if one_head_each and paired and seq_count > 2:
+        return dense_local(query_in, key_in, value_in, out_weight, grad_out, pattern)
+    return general_local(query_in, key_in, value_in, out_weight, grad_out, pattern)
+
+
+def general_local(query_in, key_in, value_in, out_weight, grad_out, pattern):
     seq_count = lax.axis_size("seq")
     rep_count = lax.axis_size("rep")
     tokens_here = query_in.shape[1]

time: 239 us -> 95.1 us (0.40)
  waiting for transfers between devices: 85.8 us -> 37.3 us
  blocking collectives: 31.5 us -> 0 us
  other arithmetic: 31.1 us -> 0.1 us
  matrix products: 26.4 us -> 0 us
  Pallas kernels: 0 us -> 18.6 us
  between operations: 14.3 us -> 0.8 us
  local copies, waits for them, and re-layouts: 18.1 us -> 10.3 us
    reduce_scatter x1 -> x0, waiting for transfers between devices: 59.2 us -> none  [local(): lax.psum_scatter(lax.dot_general(attended, grad_local, (((0,), (0,)), (()...]
    ppermute x0 -> x15, waiting for transfers between devices: none -> 37.3 us  [swap(): lax.ppermute(array, axis, [(i, i ^ mask) for i in range(lax.axis_size(axi...]
    scatter-add x2 -> x0, other arithmetic: 27.1 us -> none  [the longest x1 13.6 us: attend_step(): value_acc.at[pattern_run]]
    all_to_all x6 -> x2, waiting for transfers between devices: 26.6 us -> 0.01 us  [the longest x1 0.01 us: dense_local(): lax.all_to_all(pack(key_in[0], value_in[0], seq_count), 'seq', split_axis...]
    all_to_all x2 -> x0, blocking collectives: 25 us -> none  [the longest x1 13.2 us: local(): lax.all_to_all(to_heads(attended_grad), 'seq', split_axis=0, concat_axis=...]
    dot_general x8 -> x0, matrix products: 24.1 us -> none  [the longest x1 4.51 us: local(): lax.dot_general(attended, grad_local, (((0,), (0,)), ((), ())), preferred...]
    pallas_call x0 -> x12, Pallas kernels: none -> 18.6 us  [the longest x1 4.56 us: backward(): pl.pallas_call(functools.partial(backward_kernel, 2 * here, scale), out_s...]
    all_to_all x6 -> x2, starting transfers between devices: 29.7 us -> 11.5 us  [the longest x1 7.26 us: dense_local(): lax.all_to_all(pack(key_in[0], value_in[0], seq_count), 'seq', split_axis...]
  transfers between devices with their start and end apart: 7 -> 17, of which waited for: 5 -> 11; matrix products, arithmetic and copies ran while one was open for 26% -> 0% of each run, Pallas kernels for 0% -> 16%
where the time goes in v2:
time: 95.1 us; the launch traced here: 94.7 us
  waiting for transfers between devices  37.3 us (39%)
  starting transfers between devices  27.5 us (29%)
  Pallas kernels  18.6 us (20%)
  local copies, waits for them, and re-layouts  10.3 us (11%)
    ppermute x15, waiting for transfers between devices, swap(): lax.ppermute(array, axis, [(i, i ^ mask) for i in range(lax.axis_size(axi...  37.3 us
    ppermute x15, starting transfers between devices, swap(): lax.ppermute(array, axis, [(i, i ^ mask) for i in range(lax.axis_size(axi...  16.1 us
    unnamed x37, local copies, waits for them, and re-layouts  10 us
    all_to_all x1, starting transfers between devices, dense_local(): lax.all_to_all(pack(key_in[0], value_in[0], seq_count), 'seq', split_axis...  7.26 us
    pallas_call x1, Pallas kernels, backward(): pl.pallas_call(functools.partial(backward_kernel, 2 * here, scale), out_s...  4.56 us
    all_to_all x1, starting transfers between devices, dense_local(): lax.all_to_all(returns, 'seq', split_axis=0, concat_axis=0, tiled=True)  4.2 us
    pallas_call x1, Pallas kernels, forward(): pl.pallas_call(functools.partial(forward_kernel, chunk, scale), out_shape...  3.49 us
    pallas_call x1, Pallas kernels, project(): pl.pallas_call(project_kernel, out_shape=[struct(rows, width), struct(16,...  2.61 us
  transfers between devices with their start and end apart: 17, of which 11 were waited for; matrix products, arithmetic and copies ran while one was open for 0% of the time, Pallas kernels for 16%

profile of v2, /device:TPU:0, one launch (start us, length us, event | category | flops | bytes accessed | tf_op | source)
XLA Modules:
  0.0 94.7 jit_solution(6754355480684238738)
XLA Ops:
  0.7 2.1 %pack_keys.1 = bf16[8,512,128]{2,1,0:T(8,128)(2,1)} custom-call(bf16[128,1024]{1,0:T(8,128)(2,1)} %bitcast.16, bf16[128,1024]{1,0:T(8,128)(2,1)} %bitcast.17), custom_call_target="tpu_custom_call" | custom-call | flops 1 | bytes 1 | tf_op jit(solution)/shard_map/pack_keys/pallas_call | solution.py:98
  2.8 7.3 %all-to-all-start = ((bf16[8,512,128]{2,1,0:T(8,128)(2,1)}), bf16[8,512,128]{2,1,0:T(8,128)(2,1)S(1)}, u32[]{:S(2)}, u32[]{:S(2)}) async-start(bf16[8,512,128]{2,1,0:T(8,128)(2,1)} %pack_keys.1), calls=%async_computation | async-start | bytes 2097152 | tf_op jit(solution)/shard_map/all_to_all | solution.py:480
  10.1 2.2 %copy-done = bf16[1024,2048]{1,0:T(8,128)(2,1)S(1)} copy-done((bf16[1024,2048]{1,0:T(8,128)(2,1)S(1)}, bf16[1024,2048]{1,0:T(8,128)(2,1)}, u32[]{:S(2)}) %copy-start) | copy-done | bytes 4194328
  14.2 1.7 %head_grads.1 = (bf16[512,128]{1,0:T(8,128)(2,1)S(1)}, bf16[512,128]{1,0:T(8,128)(2,1)S(1)}, bf16[512,128]{1,0:T(8,128)(2,1)S(1)}, bf16[512,128]{1,0:T(8,128)(2,1)S(1)}) custom-call(bf16[128,1024]{1,0:T(8,128)(2,1)S(1)} %bitcast.15, bf16[128,2048]{1,0:T(8,128)(2,1)S(1)} %bitcast.10, bf16[1024,2048]{1,0:T(8,128)(2,1)S(1)} %copy-done), custom_call_target="tpu_custom_call" | custom-call | flops 1 | bytes 1 | tf_op jit(solution)/shard_map/head_grads/pallas_call | solution.py:137
  16.0 2.1 %collective-permute-start = (bf16[512,128]{1,0:T(8,128)(2,1)S(1)}, bf16[512,128]{1,0:T(8,128)(2,1)S(1)}, u32[]{:S(2)}, u32[]{:S(2)}) collective-permute-start(bf16[512,128]{1,0:T(8,128)(2,1)S(1)} %get-tuple-element.35), channel_id=1, source_target_pairs={{0,4},{4,0},{8,12},{12,8},{16,20},{20,16},{24,28},{28,24},{1,5},{5... | collective-permute-start | bytes 393224 | tf_op jit(solution)/shard_map/ppermute | solution.py:46
  20.1 3.4 %collective-permute-done.refs_1_ = bf16[512,128]{1,0:T(8,128)(2,1)S(1)} collective-permute-done((bf16[512,128]{1,0:T(8,128)(2,1)S(1)}, bf16[512,128]{1,0:T(8,128)(2,1)S(1)}, u32[]{:S(2)}, u32[]{:S(2)}) %collective-permute-start) | collective-permute-done | bytes 131104 | tf_op jit(solution)/shard_map/ppermute | solution.py:46
  23.5 1.7 %collective-permute-start.6 = (bf16[128,2048]{1,0:T(8,128)(2,1)S(1)}, bf16[128,2048]{1,0:T(8,128)(2,1)S(1)}, u32[]{:S(2)}, u32[]{:S(2)}) collective-permute-start(bf16[128,2048]{1,0:T(8,128)(2,1)S(1)} %bitcast.11), channel_id=1, source_target_pairs={{0,4},{4,0},{8,12},{12,8},{16,20},{20,16},{24,28},{28,24},{1,5},{5... | collective-permute-start | bytes 1572872 | tf_op jit(solution)/shard_map/ppermute | solution.py:46
  27.0 4.1 %collective-permute-done.1.refs_2_ = bf16[512,128]{1,0:T(8,128)(2,1)S(1)} collective-permute-done((bf16[512,128]{1,0:T(8,128)(2,1)S(1)}, bf16[512,128]{1,0:T(8,128)(2,1)S(1)}, u32[]{:S(2)}, u32[]{:S(2)}) %collective-permute-start.1) | collective-permute-done | bytes 131104 | tf_op jit(solution)/shard_map/ppermute | solution.py:46
  31.8 5.1 %collective-permute-done.2.refs_3_ = bf16[512,128]{1,0:T(8,128)(2,1)S(1)} collective-permute-done((bf16[512,128]{1,0:T(8,128)(2,1)S(1)}, bf16[512,128]{1,0:T(8,128)(2,1)S(1)}, u32[]{:S(2)}, u32[]{:S(2)}) %collective-permute-start.2) | collective-permute-done | bytes 131104 | tf_op jit(solution)/shard_map/ppermute | solution.py:46
  39.4 3.5 %attend.1 = (bf16[1024,128]{1,0:T(8,128)(2,1)S(1)}, f32[2,512]{1,0:T(2,128)S(1)}, f32[2,512]{1,0:T(2,128)S(1)}) custom-call(f32[16,1024]{1,0:T(8,128)S(1)} %reshape.14.bias_ref, bf16[8,512,128]{2,1,0:T(8,128)(2,1)S(1)} %all-to-all-done.pairs, bf16[2,512,128]{2,1,0:T(8,128)(2,1)S(1)} %get-tuple-element.39.queries), custom_call_target="tpu_custom_call" | custom-call | flops 1 | bytes 1 | tf_op jit(solution)/shard_map/attend/pallas_call | solution.py:217
  42.9 4.6 %attend_back.1 = (bf16[8,512,128]{2,1,0:T(8,128)(2,1)}, bf16[512,128]{1,0:T(8,128)(2,1)S(1)}, bf16[512,128]{1,0:T(8,128)(2,1)S(1)}, bf16[512,128]{1,0:T(8,128)(2,1)S(1)}, bf16[512,128]{1,0:T(8,128)(2,1)S(1)}) custom-call(f32[16,1024]{1,0:T(8,128)S(1)} %reshape.14.bias_ref, f32[2,512]{1,0:T(2,128)S(1)} %get-tuple-element.40.top_ref, ...), custom_call_target="tpu_custom_call" | custom-call | flops 1 | bytes 1 | tf_op jit(solution)/shard_map/attend_back/pallas_call | solution.py:272
  50.1 4.2 %all-to-all-start.1 = ((bf16[8,512,128]{2,1,0:T(8,128)(2,1)}), bf16[8,512,128]{2,1,0:T(8,128)(2,1)S(1)}, u32[]{:S(2)}, u32[]{:S(2)}) async-start(bf16[8,512,128]{2,1,0:T(8,128)(2,1)} %get-tuple-element.50), calls=%async_computation.1 | async-start | bytes 2097152 | tf_op jit(solution)/shard_map/all_to_all | solution.py:492
  54.3 6.6 %collective-permute-done.8.refs_3_ = bf16[128,2048]{1,0:T(8,128)(2,1)} collective-permute-done((bf16[128,2048]{1,0:T(8,128)(2,1)S(1)}, bf16[128,2048]{1,0:T(8,128)(2,1)}, u32[]{:S(2)}, u32[]{:S(2)}) %collective-permute-start.8) | collective-permute-done | bytes 524320 | tf_op jit(solution)/shard_map/ppermute | solution.py:46
  60.9 1.8 %weight_part.1 = (f32[512,512]{1,0:T(8,128)S(1)}, bf16[512,512]{1,0:T(8,128)(2,1)S(1)}) custom-call(bf16[1024,128]{1,0:T(8,128)(2,1)S(1)} %get-tuple-element.55.near, bf16[128,2048]{1,0:T(8,128)(2,1)S(1)} %bitcast.14, bf16[128,2048]{1,0:T(8,128)(2,1)S(1)} %collective-permute-done.6.refs_1_, bf16[128,2048]{1,0:T(8,128)(2,1)S(1)} %collective-permute-done.7.refs_2_, ...), custom_call_target="tpu_custom_call" | custom-call | flops 1 | bytes 1 | tf_op jit(solution)/shard_map/weight_part/pallas_call | solution.py:374
  62.8 1.9 %collective-permute-done.9.other = bf16[512,512]{1,0:T(8,128)(2,1)S(1)} collective-permute-done((bf16[512,512]{1,0:T(8,128)(2,1)S(1)}, bf16[512,512]{1,0:T(8,128)(2,1)S(1)}, u32[]{:S(2)}, u32[]{:S(2)}) %collective-permute-start.9) | collective-permute-done | bytes 524320 | tf_op jit(solution)/shard_map/ppermute | solution.py:46
  64.8 1.6 %collective-permute-start.10 = (bf16[256,512]{1,0:T(8,128)(2,1)S(1)}, bf16[256,512]{1,0:T(8,128)(2,1)S(1)}, u32[]{:S(2)}, u32[]{:S(2)}) collective-permute-start(bf16[256,512]{1,0:T(8,128)(2,1)S(1)} %get-tuple-element.60), channel_id=1, source_target_pairs={{0,2},{1,3},{2,0},{3,1},{4,6},{5,7},{6,4},{7,5},{8,10},{9,11},{10,... | collective-permute-start | bytes 786440 | tf_op jit(solution)/shard_map/ppermute | solution.py:46
  66.6 3.2 %collective-permute-start.5 = (bf16[512,128]{1,0:T(8,128)(2,1)S(1)}, bf16[512,128]{1,0:T(8,128)(2,1)S(1)}, u32[]{:S(2)}, u32[]{:S(2)}) collective-permute-start(bf16[512,128]{1,0:T(8,128)(2,1)S(1)} %copy-done.8), channel_id=1, source_target_pairs={{0,12},{4,8},{8,4},{12,0},{16,28},{20,24},{24,20},{28,16},{1,13},{... | collective-permute-start | bytes 393224 | tf_op jit(solution)/shard_map/ppermute | solution.py:46
  69.9 3.3 %collective-permute-done.10.other = bf16[256,512]{1,0:T(8,128)(2,1)S(1)} collective-permute-done((bf16[256,512]{1,0:T(8,128)(2,1)S(1)}, bf16[256,512]{1,0:T(8,128)(2,1)S(1)}, u32[]{:S(2)}, u32[]{:S(2)}) %collective-permute-start.10) | collective-permute-done | bytes 262176 | tf_op jit(solution)/shard_map/ppermute | solution.py:46
  73.3 2.2 %collective-permute-start.11 = (bf16[128,512]{1,0:T(8,128)(2,1)S(1)}, bf16[128,512]{1,0:T(8,128)(2,1)S(1)}, u32[]{:S(2)}, u32[]{:S(2)}) collective-permute-start(bf16[128,512]{1,0:T(8,128)(2,1)S(1)} %get-tuple-element.62), channel_id=1, source_target_pairs={{0,16},{4,20},{8,24},{12,28},{16,0},{20,4},{24,8},{28,12},{1,17},{... | collective-permute-start | bytes 393224 | tf_op jit(solution)/shard_map/ppermute | solution.py:46
  76.2 2.8 %collective-permute-done.4.refs_2_ = bf16[512,128]{1,0:T(8,128)(2,1)S(1)} collective-permute-done((bf16[512,128]{1,0:T(8,128)(2,1)S(1)}, bf16[512,128]{1,0:T(8,128)(2,1)S(1)}, u32[]{:S(2)}, u32[]{:S(2)}) %collective-permute-start.4) | collective-permute-done | bytes 131104 | tf_op jit(solution)/shard_map/ppermute | solution.py:46
  79.0 4.6 %collective-permute-done.5.refs_3_ = bf16[512,128]{1,0:T(8,128)(2,1)S(1)} collective-permute-done((bf16[512,128]{1,0:T(8,128)(2,1)S(1)}, bf16[512,128]{1,0:T(8,128)(2,1)S(1)}, u32[]{:S(2)}, u32[]{:S(2)}) %collective-permute-start.5) | collective-permute-done | bytes 131104 | tf_op jit(solution)/shard_map/ppermute | solution.py:46
  83.6 2.6 %project.1 = (bf16[128,2048]{1,0:T(8,128)(2,1)}, bf16[16,128]{1,0:T(8,128)(2,1)S(1)}) custom-call(bf16[512,128]{1,0:T(8,128)(2,1)S(1)} %copy-done.6, bf16[512,128]{1,0:T(8,128)(2,1)S(1)} %collective-permute-done.3.refs_1_, bf16[512,128]{1,0:T(8,128)(2,1)S(1)} %collective-permute-done.4.refs_2_, bf16[512,128]{1,0:T(8,128)(2,1)S(1)} %collective-permute-done.5.refs_3_, ...), custom_call_target="tpu_custom_call" | custom-call | flops 4294967296 | bytes 1 | tf_op jit(solution)/shard_map/project/pallas_call | solution.py:335
  86.2 1.6 %collective-permute-start.13 = (bf16[128,512]{1,0:T(8,128)(2,1)S(1)}, bf16[128,512]{1,0:T(8,128)(2,1)S(1)}, u32[]{:S(2)}, u32[]{:S(2)}) collective-permute-start(bf16[128,512]{1,0:T(8,128)(2,1)S(1)} %weight_sum.1.refs_0_), channel_id=1, source_target_pairs={{0,2},{1,3},{2,0},{3,1},{4,6},{5,7},{6,4},{7,5},{8,10},{9,11},{10,... | collective-permute-start | bytes 393224 | tf_op jit(solution)/shard_map/ppermute | solution.py:46
  87.8 3.4 %collective-permute-done.13.refs_2_ = bf16[128,512]{1,0:T(8,128)(2,1)S(1)} collective-permute-done((bf16[128,512]{1,0:T(8,128)(2,1)S(1)}, bf16[128,512]{1,0:T(8,128)(2,1)S(1)}, u32[]{:S(2)}, u32[]{:S(2)}) %collective-permute-start.13) | collective-permute-done | bytes 131104 | tf_op jit(solution)/shard_map/ppermute | solution.py:46
  (64 shorter events, 16.2 us)
Async XLA Ops:
  0.6 19.0 %copy-start.17 = (s32[16,8]{0,1:T(8,128)S(1)}, s32[16,8]{0,1:T(8,128)}, u32[]{:S(2)}) copy-start(s32[16,8]{0,1:T(8,128)} %param.11) | copy-start | bytes 1540
  0.6 22.9 %copy-start.3 = (bf16[1,128,2048]{2,1,0:T(8,128)(2,1)S(1)}, bf16[1,128,2048]{2,1,0:T(8,128)(2,1)}, u32[]{:S(2)}) copy-start(bf16[1,128,2048]{2,1,0:T(8,128)(2,1)} %param.10) | copy-start | bytes 1572868
  2.8 36.6 %all-to-all-start = ((bf16[8,512,128]{2,1,0:T(8,128)(2,1)}), bf16[8,512,128]{2,1,0:T(8,128)(2,1)S(1)}, u32[]{:S(2)}, u32[]{:S(2)}) async-start(bf16[8,512,128]{2,1,0:T(8,128)(2,1)} %pack_keys.1), calls=%async_computation | async-start | bytes 2097152 | tf_op jit(solution)/shard_map/all_to_all | solution.py:480
  16.0 7.5 %collective-permute-start = (bf16[512,128]{1,0:T(8,128)(2,1)S(1)}, bf16[512,128]{1,0:T(8,128)(2,1)S(1)}, u32[]{:S(2)}, u32[]{:S(2)}) collective-permute-start(bf16[512,128]{1,0:T(8,128)(2,1)S(1)} %get-tuple-element.35), channel_id=1, source_target_pairs={{0,4},{4,0},{8,12},{12,8},{16,20},{20,16},{24,28},{28,24},{1,5},{5... | collective-permute-start | bytes 393224 | tf_op jit(solution)/shard_map/ppermute | solution.py:46
  18.1 13.0 %collective-permute-start.1 = (bf16[512,128]{1,0:T(8,128)(2,1)S(1)}, bf16[512,128]{1,0:T(8,128)(2,1)S(1)}, u32[]{:S(2)}, u32[]{:S(2)}) collective-permute-start(bf16[512,128]{1,0:T(8,128)(2,1)S(1)} %get-tuple-element.37), channel_id=1, source_target_pairs={{0,8},{4,12},{8,0},{12,4},{16,24},{20,28},{24,16},{28,20},{1,9},{5... | collective-permute-start | bytes 393224 | tf_op jit(solution)/shard_map/ppermute | solution.py:46
  19.5 17.3 %collective-permute-start.2 = (bf16[512,128]{1,0:T(8,128)(2,1)S(1)}, bf16[512,128]{1,0:T(8,128)(2,1)S(1)}, u32[]{:S(2)}, u32[]{:S(2)}) collective-permute-start(bf16[512,128]{1,0:T(8,128)(2,1)S(1)} %get-tuple-element.38), channel_id=1, source_target_pairs={{0,12},{4,8},{8,4},{12,0},{16,28},{20,24},{24,20},{28,16},{1,13},{... | collective-permute-start | bytes 393224 | tf_op jit(solution)/shard_map/ppermute | solution.py:46
  23.5 30.8 %collective-permute-start.6 = (bf16[128,2048]{1,0:T(8,128)(2,1)S(1)}, bf16[128,2048]{1,0:T(8,128)(2,1)S(1)}, u32[]{:S(2)}, u32[]{:S(2)}) collective-permute-start(bf16[128,2048]{1,0:T(8,128)(2,1)S(1)} %bitcast.11), channel_id=1, source_target_pairs={{0,4},{4,0},{8,12},{12,8},{16,20},{20,16},{24,28},{28,24},{1,5},{5... | collective-permute-start | bytes 1572872 | tf_op jit(solution)/shard_map/ppermute | solution.py:46
  25.2 29.1 %collective-permute-start.7 = (bf16[128,2048]{1,0:T(8,128)(2,1)S(1)}, bf16[128,2048]{1,0:T(8,128)(2,1)S(1)}, u32[]{:S(2)}, u32[]{:S(2)}) collective-permute-start(bf16[128,2048]{1,0:T(8,128)(2,1)S(1)} %bitcast.12), channel_id=1, source_target_pairs={{0,8},{4,12},{8,0},{12,4},{16,24},{20,28},{24,16},{28,20},{1,9},{5... | collective-permute-start | bytes 1572872 | tf_op jit(solution)/shard_map/ppermute | solution.py:46
  25.7 35.2 %collective-permute-start.8 = (bf16[128,2048]{1,0:T(8,128)(2,1)S(1)}, bf16[128,2048]{1,0:T(8,128)(2,1)}, u32[]{:S(2)}, u32[]{:S(2)}) collective-permute-start(bf16[128,2048]{1,0:T(8,128)(2,1)S(1)} %bitcast.13), channel_id=1, source_target_pairs={{0,12},{4,8},{8,4},{12,0},{16,28},{20,24},{24,20},{28,16},{1,13},{... | collective-permute-start | bytes 1572872 | tf_op jit(solution)/shard_map/ppermute | solution.py:46
  50.1 16.3 %copy-start.12 = (bf16[512,128]{1,0:T(8,128)(2,1)S(1)}, bf16[512,128]{1,0:T(8,128)(2,1)}, u32[]{:S(2)}) copy-start(bf16[512,128]{1,0:T(8,128)(2,1)} %copy-done.11) | copy-start | bytes 393220
  50.1 16.3 %copy-start.10 = (bf16[512,128]{1,0:T(8,128)(2,1)S(1)}, bf16[512,128]{1,0:T(8,128)(2,1)}, u32[]{:S(2)}) copy-start(bf16[512,128]{1,0:T(8,128)(2,1)} %copy-done.9) | copy-start | bytes 393220
  50.1 16.6 %copy-start.8 = (bf16[512,128]{1,0:T(8,128)(2,1)S(1)}, bf16[512,128]{1,0:T(8,128)(2,1)}, u32[]{:S(2)}) copy-start(bf16[512,128]{1,0:T(8,128)(2,1)} %copy-done.7) | copy-start | bytes 393220
  50.1 33.5 %copy-start.6 = (bf16[512,128]{1,0:T(8,128)(2,1)S(1)}, bf16[512,128]{1,0:T(8,128)(2,1)}, u32[]{:S(2)}) copy-start(bf16[512,128]{1,0:T(8,128)(2,1)} %copy-done.5) | copy-start | bytes 393220
  50.1 43.6 %all-to-all-start.1 = ((bf16[8,512,128]{2,1,0:T(8,128)(2,1)}), bf16[8,512,128]{2,1,0:T(8,128)(2,1)S(1)}, u32[]{:S(2)}, u32[]{:S(2)}) async-start(bf16[8,512,128]{2,1,0:T(8,128)(2,1)} %get-tuple-element.50), calls=%async_computation.1 | async-start | bytes 2097152 | tf_op jit(solution)/shard_map/all_to_all | solution.py:492
  54.3 29.3 %copy-start.1 = (bf16[1024,2048]{1,0:T(8,128)(2,1)S(1)}, bf16[1024,2048]{1,0:T(8,128)(2,1)}, u32[]{:S(2)}) copy-start(bf16[1024,2048]{1,0:T(8,128)(2,1)} %refs_4_.1) | copy-start | bytes 12582916
  62.7 2.0 %collective-permute-start.9 = (bf16[512,512]{1,0:T(8,128)(2,1)S(1)}, bf16[512,512]{1,0:T(8,128)(2,1)S(1)}, u32[]{:S(2)}, u32[]{:S(2)}) collective-permute-start(bf16[512,512]{1,0:T(8,128)(2,1)S(1)} %get-tuple-element.58), channel_id=1, source_target_pairs={{0,1},{1,0},{2,3},{3,2},{4,5},{5,4},{6,7},{7,6},{8,9},{9,8},{10,11... | collective-permute-start | bytes 1572872 | tf_op jit(solution)/shard_map/ppermute | solution.py:46
  64.8 8.4 %collective-permute-start.10 = (bf16[256,512]{1,0:T(8,128)(2,1)S(1)}, bf16[256,512]{1,0:T(8,128)(2,1)S(1)}, u32[]{:S(2)}, u32[]{:S(2)}) collective-permute-start(bf16[256,512]{1,0:T(8,128)(2,1)S(1)} %get-tuple-element.60), channel_id=1, source_target_pairs={{0,2},{1,3},{2,0},{3,1},{4,6},{5,7},{6,4},{7,5},{8,10},{9,11},{10,... | collective-permute-start | bytes 786440 | tf_op jit(solution)/shard_map/ppermute | solution.py:46
  66.4 9.8 %collective-permute-start.3 = (bf16[512,128]{1,0:T(8,128)(2,1)S(1)}, bf16[512,128]{1,0:T(8,128)(2,1)S(1)}, u32[]{:S(2)}, u32[]{:S(2)}) collective-permute-start(bf16[512,128]{1,0:T(8,128)(2,1)S(1)} %copy-done.12), channel_id=1, source_target_pairs={{0,4},{4,0},{8,12},{12,8},{16,20},{20,16},{24,28},{28,24},{1,5},{5... | collective-permute-start | bytes 393224 | tf_op jit(solution)/shard_map/ppermute | solution.py:46
  66.4 12.6 %collective-permute-start.4 = (bf16[512,128]{1,0:T(8,128)(2,1)S(1)}, bf16[512,128]{1,0:T(8,128)(2,1)S(1)}, u32[]{:S(2)}, u32[]{:S(2)}) collective-permute-start(bf16[512,128]{1,0:T(8,128)(2,1)S(1)} %copy-done.10), channel_id=1, source_target_pairs={{0,8},{4,12},{8,0},{12,4},{16,24},{20,28},{24,16},{28,20},{1,9},{5... | collective-permute-start | bytes 393224 | tf_op jit(solution)/shard_map/ppermute | solution.py:46
  66.6 17.0 %collective-permute-start.5 = (bf16[512,128]{1,0:T(8,128)(2,1)S(1)}, bf16[512,128]{1,0:T(8,128)(2,1)S(1)}, u32[]{:S(2)}, u32[]{:S(2)}) collective-permute-start(bf16[512,128]{1,0:T(8,128)(2,1)S(1)} %copy-done.8), channel_id=1, source_target_pairs={{0,12},{4,8},{8,4},{12,0},{16,28},{20,24},{24,20},{28,16},{1,13},{... | collective-permute-start | bytes 393224 | tf_op jit(solution)/shard_map/ppermute | solution.py:46
  73.3 12.9 %collective-permute-start.11 = (bf16[128,512]{1,0:T(8,128)(2,1)S(1)}, bf16[128,512]{1,0:T(8,128)(2,1)S(1)}, u32[]{:S(2)}, u32[]{:S(2)}) collective-permute-start(bf16[128,512]{1,0:T(8,128)(2,1)S(1)} %get-tuple-element.62), channel_id=1, source_target_pairs={{0,16},{4,20},{8,24},{12,28},{16,0},{20,4},{24,8},{28,12},{1,17},{... | collective-permute-start | bytes 393224 | tf_op jit(solution)/shard_map/ppermute | solution.py:46
  86.2 5.0 %collective-permute-start.13 = (bf16[128,512]{1,0:T(8,128)(2,1)S(1)}, bf16[128,512]{1,0:T(8,128)(2,1)S(1)}, u32[]{:S(2)}, u32[]{:S(2)}) collective-permute-start(bf16[128,512]{1,0:T(8,128)(2,1)S(1)} %weight_sum.1.refs_0_), channel_id=1, source_target_pairs={{0,2},{1,3},{2,0},{3,1},{4,6},{5,7},{6,4},{7,5},{8,10},{9,11},{10,... | collective-permute-start | bytes 393224 | tf_op jit(solution)/shard_map/ppermute | solution.py:46
  87.8 3.5 %collective-permute-start.12 = (bf16[128,512]{1,0:T(8,128)(2,1)S(1)}, bf16[128,512]{1,0:T(8,128)(2,1)S(1)}, u32[]{:S(2)}, u32[]{:S(2)}) collective-permute-start(bf16[128,512]{1,0:T(8,128)(2,1)S(1)} %weight_sum.1.refs_0_), channel_id=1, source_target_pairs={{0,1},{1,0},{2,3},{3,2},{4,5},{5,4},{6,7},{7,6},{8,9},{9,8},{10,11... | collective-permute-start | bytes 393224 | tf_op jit(solution)/shard_map/ppermute | solution.py:46
  91.3 1.3 %collective-permute-start.14 = (bf16[128,512]{1,0:T(8,128)(2,1)S(1)}, bf16[128,512]{1,0:T(8,128)(2,1)S(1)}, u32[]{:S(2)}, u32[]{:S(2)}) collective-permute-start(bf16[128,512]{1,0:T(8,128)(2,1)S(1)} %collective-permute-done.13.refs_2_), channel_id=1, source_target_pairs={{0,1},{1,0},{2,3},{3,2},{4,5},{5,4},{6,7},{7,6},{8,9},{9,8},{10,11... | collective-permute-start | bytes 393224 | tf_op jit(solution)/shard_map/ppermute | solution.py:46
  (11 other events, 9.9 us)

commit v3 on v2

--- a/solution.py
+++ b/solution.py
@@ -18,8 +18,11 @@
 NN = (((1,), (0,)), ((), ()))
 TN = (((0,), (0,)), ((), ()))
 WIDE = 58
-PROJECT_FLOPS = 4 << 30
+HEAD_MIB = 58
+PROJECT_FLOPS = 1
 JOIN_FLOPS = 2 << 30
+SCALE_FLOPS = 8 << 30
+HEADS_FLOPS = 1
 
 
 def dot(left, right, dims):
@@ -38,20 +41,16 @@
     return jax.ShapeDtypeStruct(shape, dtype)
 
 
+def in_hbm(array):
+    return pltpu.with_memory_space_constraint(array, pltpu.HBM)
+
+
 def span(index, size):
     return pl.ds(pl.multiple_of(index * size, size), size)
 
 
 def swap(array, axis, mask):
     return lax.ppermute(array, axis, [(i, i ^ mask) for i in range(lax.axis_size(axis))])
-
-
-def gather_rep(block):
-    blocks, bit = {0: block}, lax.axis_size("rep") // 2
-    while bit:
-        blocks |= {mask | bit: swap(item, "rep", bit) for mask, item in blocks.items()}
-        bit //= 2
-    return [blocks[mask] for mask in sorted(blocks)]
 
 
 def after(*arrays):
@@ -108,7 +107,8 @@
 
 
 def head_grad_kernel(query_ref, grad_ref, weight_ref, *refs):
-    sends, (query, grad, weight, head_grad, sem) = refs[:-5], refs[-5:]
+    sends, (mine, theirs), refs = refs[:-7], refs[-7:-5], refs[-5:]
+    query, grad, weight, head_grad, sem = refs
     rows = query_ref.shape[0]
     members = len(sends)
     loads = [
@@ -124,6 +124,9 @@
         for slot in range(2):
             send[slot * rows : (slot + 1) * rows] = query[:, span(member(mask) + slot * members, HD)]
     loads[1].wait()
+    side = lax.axis_index("seq") & 1
+    mine[...] = grad[:, span(side, mine.shape[1])]
+    theirs[...] = grad[:, span(1 - side, theirs.shape[1])]
     loads[2].wait()
     head_grad[...] = dot(weight[...], grad[...], NT).astype(jnp.bfloat16)
     for mask, send in enumerate(sends):
@@ -136,9 +139,10 @@
     rows, width = queries.shape
     return pl.pallas_call(
         head_grad_kernel,
-        out_shape=[struct(2 * rows + 2 * HD, HD)] * members,
+        out_shape=[pltpu.HBM((2 * rows + 2 * HD, HD), jnp.bfloat16)] * members
+        + [pltpu.HBM((rows, grads.shape[1] // 2), jnp.bfloat16)] * 2,
         in_specs=[ANY_SPEC] * 3,
-        out_specs=[VMEM_SPEC] * members,
+        out_specs=[VMEM_SPEC] * (members + 2),
         scratch_shapes=[
             VMEM(queries.shape, jnp.bfloat16),
             VMEM(grads.shape, jnp.bfloat16),
@@ -146,7 +150,7 @@
             VMEM((width, rows), jnp.bfloat16),
             pltpu.SemaphoreType.DMA((3,)),
         ],
-        compiler_params=params(24),
+        compiler_params=params(HEAD_MIB),
         cost_estimate=cost(),
         name="head_grads",
     )(queries, grads, out_weight)
@@ -172,7 +176,7 @@
         compiler_params=params(8),
         cost_estimate=cost(JOIN_FLOPS),
         name="join_queries",
-    )(*parts)
+    )(*map(in_hbm, parts))
 
 
 def load_heads(pairs, keys, values):
@@ -271,7 +275,7 @@
     here = tokens // peers
     return pl.pallas_call(
         functools.partial(backward_kernel, 2 * here, scale),
-        out_shape=[struct(peers, 4 * here, HD)] + [struct(4 * here, HD)] * members,
+        out_shape=[struct(peers, 4 * here, HD)] + [pltpu.HBM((4 * here, HD), jnp.bfloat16)] * members,
         in_specs=[VMEM_SPEC] * 7,
         out_specs=[VMEM_SPEC] * (1 + members),
         scratch_shapes=[VMEM((2, tokens, HD), jnp.bfloat16)] * 2
@@ -310,79 +314,91 @@
         compiler_params=params(16),
         cost_estimate=cost(1, 24 * rows * width),
         name="unpack_grads",
-    )(returned, *queries)
-
-
-def project_kernel(*refs):
-    parts, (weight_ref, out_ref, token, attended) = refs[:-4], refs[-4:]
+    )(returned, *map(in_hbm, queries))
+
+
+def join_heads_kernel(*refs):
+    parts, attended = refs[:-1], refs[-1]
+    rows = attended.shape[0]
+    for mask, part in enumerate(parts):
+        for slot in range(2):
+            columns = span(member(mask) + slot * len(parts), HD)
+            attended[:, columns] = part[(2 + slot) * rows : (3 + slot) * rows]
+
+
+def join_heads(parts):
+    rows = parts[0].shape[0] // 4
+    return pl.pallas_call(
+        join_heads_kernel,
+        out_shape=struct(rows, 2 * HD * len(parts)),
+        in_specs=[VMEM_SPEC] * len(parts),
+        out_specs=VMEM_SPEC,
+        compiler_params=params(8),
+        cost_estimate=cost(HEADS_FLOPS),
+        name="join_heads",
+    )(*map(in_hbm, parts))
+
+
+def project_kernel(attended, weight_ref, out_ref, token):
     token[...] = jnp.zeros_like(token)
-    rows = out_ref.shape[0]
-
-    @pl.when(pl.program_id(0) == 0)
-    def _():
-        for mask, part in enumerate(parts):
-            for slot in range(2):
-                columns = span(member(mask) + slot * len(parts), HD)
-                attended[:, columns] = part[(2 + slot) * rows : (3 + slot) * rows]
-
     out_ref[...] = dot(attended[...], weight_ref[...], NN).astype(jnp.bfloat16)
 
 
-def project(parts, out_weight):
-    rows = parts[0].shape[0] // 4
+def project(attended, out_weight):
+    rows = attended.shape[0]
     depth, width = out_weight.shape
     tile = width // 4
     return pl.pallas_call(
         project_kernel,
         out_shape=[struct(rows, width), struct(16, HD)],
         grid=(width // tile,),
-        in_specs=[pl.BlockSpec(part.shape, lambda i: (0, 0)) for part in parts]
-        + [pl.BlockSpec((depth, tile), lambda i: (0, i))],
+        in_specs=[
+            pl.BlockSpec((rows, depth), lambda i: (0, 0)),
+            pl.BlockSpec((depth, tile), lambda i: (0, i)),
+        ],
         out_specs=[
             pl.BlockSpec((rows, tile), lambda i: (0, i)),
             pl.BlockSpec((16, HD), lambda i: (0, 0)),
         ],
-        scratch_shapes=[VMEM((rows, depth), jnp.bfloat16)],
         compiler_params=params(24),
         cost_estimate=cost(PROJECT_FLOPS, 1),
         name="project",
-    )(*parts, out_weight)
-
-
-def weight_part_kernel(docs, near, *refs):
+    )(attended, out_weight)
+
+
+def weight_part_kernel(docs, near, near_pair, *refs):
     grads, (own, send) = refs[:-2], refs[-2:]
     members = len(grads)
     rows = grads[0].shape[0]
     width = grads[0].shape[1] // docs
     lefts = []
-    for slot in range(2):
-        places = [span(slot * members + member(mask), rows) for mask in range(members)]
-        lefts.append(jnp.concatenate([near[place] for place in places], axis=0).T)
+    for source in (near, near_pair):
+        for slot in range(2):
+            places = [span(slot * members + member(mask), rows) for mask in range(members)]
+            lefts.append(jnp.concatenate([source[place] for place in places], axis=0))
+    left = jnp.concatenate(lefts, axis=1).T
     for mask in range(docs):
         columns = span(lax.axis_index("rep") ^ mask, width)
         right = jnp.concatenate([grad[:, columns] for grad in grads], axis=0)
-        for slot, left in enumerate(lefts):
-            place = pl.ds((mask // 2 * 2 + slot) * HD, HD)
-            if mask % 2:
-                send[place] = dot(left, right, NN).astype(jnp.bfloat16)
-            else:
-                own[place] = dot(left, right, NN)
-
-
-def weight_parts(near, grads, docs):
+        place = pl.ds(mask // 2 * left.shape[0], left.shape[0])
+        if mask % 2:
+            send[place] = dot(left, right, NN).astype(jnp.bfloat16)
+        else:
+            own[place] = dot(left, right, NN)
+
+
+def weight_parts(near, near_pair, grads, docs):
     width = grads[0].shape[1] // docs
+    rows = docs // 2 * 4 * HD
     return pl.pallas_call(
         functools.partial(weight_part_kernel, docs),
-        out_shape=[
-            struct(docs * HD, width, dtype=jnp.float32),
-            struct(docs * HD, width),
-        ],
-        in_specs=[VMEM_SPEC] * (1 + len(grads)),
+        out_shape=[struct(rows, width, dtype=jnp.float32), struct(rows, width)],
+        in_specs=[VMEM_SPEC] * (2 + len(grads)),
         out_specs=[VMEM_SPEC] * 2,
         compiler_params=params(24),
         cost_estimate=cost(),
         name="weight_part",
-    )(near, *grads)
+    )(near, near_pair, *map(in_hbm, grads))
 
 
 def weight_fold_kernel(own, other, keep, send):
@@ -404,61 +420,69 @@
     )(own, other)
 
 
-def weight_split_kernel(own, other, keep, send):
-    lower = half_of() == 0
-    rows = keep.shape[0]
-    first = own[:rows] + other[:rows].astype(jnp.float32)
-    second = own[rows:] + other[rows:].astype(jnp.float32)
-    keep[...] = jnp.where(lower, first, second)
-    send[...] = jnp.where(lower, second, first).astype(jnp.bfloat16)
-
-
-def weight_split(own, other):
+def weight_spread_kernel(own, other, *targets):
+    rows = targets[0].shape[0]
+    half = half_of()
+    for index, target in enumerate(targets):
+        block = span(index // 2 * 2 + (1 - half if index % 2 else half), rows)
+        target[...] = (own[block] + other[block].astype(jnp.float32)).astype(target.dtype)
+
+
+def weight_spread(own, other):
     rows, width = own.shape
     return pl.pallas_call(
-        weight_split_kernel,
-        out_shape=[struct(rows // 2, width, dtype=jnp.float32), struct(rows // 2, width)],
+        weight_spread_kernel,
+        out_shape=[struct(rows // 4, width, dtype=jnp.float32)] + [struct(rows // 4, width)] * 3,
         in_specs=[VMEM_SPEC] * 2,
-        out_specs=[VMEM_SPEC] * 2,
+        out_specs=[VMEM_SPEC] * 4,
         compiler_params=params(8),
         cost_estimate=cost(),
-        name="weight_split",
+        name="weight_spread",
     )(own, other)
 
 
-def weight_sum_kernel(factor, own, other, total):
-    total[...] = ((own[...] + other[...].astype(jnp.float32)) * factor).astype(jnp.bfloat16)
-
-
-def weight_sum(anchor, own, other, factor):
-    return pl.pallas_call(
-        anchored(functools.partial(weight_sum_kernel, factor)),
-        out_shape=struct(*own.shape),
-        in_specs=[ANY_SPEC] + [VMEM_SPEC] * 2,
+def weight_scale_kernel(factor, own, across, pair, diagonal, total):
+    rows = own.shape[0]
+    total[:rows] = ((own[...] + across[...].astype(jnp.float32)) * factor).astype(jnp.bfloat16)
+    other = pair[...].astype(jnp.float32) + diagonal[...].astype(jnp.float32)
+    total[rows:] = (other * factor).astype(jnp.bfloat16)
+
+
+def weight_scale(anchor, own, across, pair, diagonal, factor):
+    rows, width = own.shape
+    return pl.pallas_call(
+        anchored(functools.partial(weight_scale_kernel, factor)),
+        out_shape=struct(2 * rows, width),
+        in_specs=[ANY_SPEC] + [VMEM_SPEC] * 4,
         out_specs=VMEM_SPEC,
         compiler_params=params(8),
-        cost_estimate=cost(),
-        name="weight_sum",
-    )(anchor, own, other)
+        cost_estimate=cost(SCALE_FLOPS),
+        name="weight_scale",
+    )(anchor, own, across, pair, diagonal)
 
 
 def weight_join_kernel(*refs):
-    width = refs[0].shape[1]
-    for mask, part in enumerate(refs[:-1]):
-        refs[-1][:, span(lax.axis_index("rep") ^ mask, width)] = part[...].astype(jnp.float32)
-
-
-def weight_join(parts):
-    rows, width = parts[0].shape
-    return pl.pallas_call(
-        weight_join_kernel,
-        out_shape=struct(rows, width * len(parts), dtype=jnp.float32),
-        in_specs=[VMEM_SPEC] * len(parts),
+    parts, total = refs[:-1], refs[-1]
+    rows, width = total.shape[0], parts[0].shape[1]
+    side = lax.axis_index("seq") & 1
+    for mask, part in enumerate(parts):
+        share = lax.axis_index("rep") ^ mask
+        for index, place in ((0, side), (1, 1 - side)):
+            block = part[index * rows : (index + 1) * rows]
+            total[:, span(place * len(parts) + share, width)] = block.astype(jnp.float32)
+
+
+def weight_join(anchor, pairs):
+    rows, width = HD, pairs[0].shape[1]
+    return pl.pallas_call(
+        anchored(weight_join_kernel),
+        out_shape=struct(rows, 2 * width * len(pairs), dtype=jnp.float32),
+        in_specs=[ANY_SPEC] + [VMEM_SPEC] * len(pairs),
         out_specs=VMEM_SPEC,
         compiler_params=params(8),
         cost_estimate=cost(),
         name="weight_join",
-    )(*parts)
+    )(anchor, *pairs)
 
 
 def dense_bias(pattern, tokens):
@@ -480,31 +504,43 @@
     pairs = lax.all_to_all(
         pack(key_in[0], value_in[0], seq_count), "seq", split_axis=0, concat_axis=0, tiled=True
     )
-    sends = head_grads(query_in[0], grad_out[0], out_weight, members)
+    *sends, grad_mine, grad_theirs = head_grads(query_in[0], grad_out[0], out_weight, members)
     parts = [sends[0]] + [swap(sends[mask], "seq", mask) for mask in range(1, members)]
-    grads, near_part = after(grad_out[0], parts[1])
-    queries, head_grad = join_queries(parts[:1] + [near_part] + parts[2:])
-    half_grads = [grads] + [swap(grads, "seq", mask) for mask in range(1, members)]
+    grad_mine, grad_theirs, *parts[1:3] = after(grad_mine, grad_theirs, *parts[1:3])
+    queries, head_grad = join_queries(parts)
+    half_grads = [grad_mine] + [
+        swap(grad_theirs if mask & 1 else grad_mine, "seq", mask) for mask in range(1, members)
+    ]
 
     near, top, total = forward(bias, pairs, queries, scale)
+    near_pair = swap(near, "seq", 1)
     returns, *sends = backward(bias, top, total, pairs, queries, head_grad, near, scale)
     near, returns = after(near, returns)
     returned = lax.all_to_all(returns, "seq", split_axis=0, concat_axis=0, tiled=True)
     parts = [sends[0]] + [swap(sends[mask], "seq", mask) for mask in range(1, members)]
 
-    own, send = weight_parts(near, half_grads, rep_count)
+    own, send = weight_parts(near, near_pair, half_grads, rep_count)
     bit = 1
     while 2 * bit < rep_count:
         own, send = weight_fold(own, swap(send, "rep", bit))
         bit *= 2
-    own, send = weight_split(own, swap(send, "rep", bit))
-    other = swap(send, "seq", members)
-    mixed_out, token = project(parts, out_weight)
-    weight_quarter = weight_sum(token, own, other, 1.0 / math.sqrt(rep_count * tokens))
+    own, *sends = weight_spread(own, swap(send, "rep", bit))
+    arrived = [swap(block, "seq", mask) for block, mask in zip(sends, (members, 1, members + 1))]
+    mixed_out, token = project(join_heads(parts), out_weight)
+    factor = 1.0 / math.sqrt(rep_count * tokens)
+    pair = weight_scale(token, own, *arrived, factor)
     query_grad, key_grad, value_grad, token = unpack(
         returned, parts, tokens_here, query_in.shape[2]
     )
-    weight_grad = weight_join(gather_rep(weight_quarter))
+    across, token = after(swap(pair, "rep", 2), token)
+    quarters = [pair, swap(pair, "rep", 1), across, swap(across, "rep", 1)]
+    weight_grad = weight_join(token, quarters)
+    return (mixed_out[None], query_grad[None], key_grad[None], value_grad[None], weight_grad)
+
+
+    return (mixed_out[None], query_grad[None], key_grad[None], value_grad[None], weight_grad)
+
+
     return (mixed_out[None], query_grad[None], key_grad[None], value_grad[None], weight_grad)
 
 

time: 95.1 us -> 89.4 us (0.940)
  waiting for transfers between devices: 37.3 us -> 26.5 us
  local copies, waits for them, and re-layouts: 10.3 us -> 2.46 us
  Pallas kernels: 18.6 us -> 25.6 us
  starting transfers between devices: 27.5 us -> 33.5 us
    ppermute x15 -> x18, waiting for transfers between devices: 37.3 us -> 26.5 us  [swap(): lax.ppermute(array, axis, [(i, i ^ mask) for i in range(lax.axis_size(axi...]
    unnamed x37 -> x29, local copies, waits for them, and re-layouts: 10 us -> 2.2 us
    ppermute x15 -> x18, starting transfers between devices: 16.1 us -> 20.9 us  [swap(): lax.ppermute(array, axis, [(i, i ^ mask) for i in range(lax.axis_size(axi...]
    pallas_call x4 -> x5, Pallas kernels: 2.88 us -> 6.91 us  [the longest x1 4.63 us: head_grads(): pl.pallas_call(head_grad_kernel, out_shape=[pltpu.HBM((2 * rows + 2 * HD,...]
    all_to_all x1, starting transfers between devices: 4.2 us -> 5.38 us  [dense_local(): lax.all_to_all(returns, 'seq', split_axis=0, concat_axis=0, tiled=True)]
    pallas_call x1, Pallas kernels: 0.07 us -> 1.16 us  [join_queries(): pl.pallas_call(join_queries_kernel, out_shape=[struct(2, tokens, HD), str...]
    pallas_call x1, Pallas kernels: 1.01 us -> 2.09 us  [unpack(): pl.pallas_call(unpack_kernel, out_shape=[struct(rows, width)] * 3 + [stru...]
  transfers between devices with their start and end apart: 17 -> 20, of which waited for: 11 -> 10; matrix products, arithmetic and copies ran while one was open for 0% -> 0% of each run, Pallas kernels for 16% -> 25%
where the time goes in v3:
time: 89.4 us; the launch traced here: 89.1 us
  starting transfers between devices  33.5 us (37%)
  waiting for transfers between devices  26.5 us (30%)
  Pallas kernels  25.6 us (29%)
  local copies, waits for them, and re-layouts  2.46 us (3%)
    ppermute x18, waiting for transfers between devices, swap(): lax.ppermute(array, axis, [(i, i ^ mask) for i in range(lax.axis_size(axi...  26.5 us
    ppermute x18, starting transfers between devices, swap(): lax.ppermute(array, axis, [(i, i ^ mask) for i in range(lax.axis_size(axi...  20.9 us
    all_to_all x1, starting transfers between devices, dense_local(): lax.all_to_all(pack(key_in[0], value_in[0], seq_count), 'seq', split_axis...  7.26 us
    all_to_all x1, starting transfers between devices, dense_local(): lax.all_to_all(returns, 'seq', split_axis=0, concat_axis=0, tiled=True)  5.38 us
    pallas_call x1, Pallas kernels, backward(): pl.pallas_call(functools.partial(backward_kernel, 2 * here, scale), out_s...  4.68 us
    pallas_call x1, Pallas kernels, head_grads(): pl.pallas_call(head_grad_kernel, out_shape=[pltpu.HBM((2 * rows + 2 * HD,...  4.63 us
    pallas_call x1, Pallas kernels, forward(): pl.pallas_call(functools.partial(forward_kernel, chunk, scale), out_shape...  3.5 us
    pallas_call x1, Pallas kernels, weight_parts(): pl.pallas_call(functools.partial(weight_part_kernel, docs), out_shape=[st...  2.57 us
  transfers between devices with their start and end apart: 20, of which 10 were waited for; matrix products, arithmetic and copies ran while one was open for 0% of the time, Pallas kernels for 25%

profile of v3, /device:TPU:0, one launch (start us, length us, event | category | flops | bytes accessed | tf_op | source)
XLA Modules:
  0.0 89.1 jit_solution(11265625626824882142)
XLA Ops:
  0.6 2.1 %pack_keys.1 = bf16[8,512,128]{2,1,0:T(8,128)(2,1)} custom-call(bf16[128,1024]{1,0:T(8,128)(2,1)} %bitcast.12, bf16[128,1024]{1,0:T(8,128)(2,1)} %bitcast.13), custom_call_target="tpu_custom_call" | custom-call | flops 1 | bytes 1 | tf_op jit(solution)/shard_map/pack_keys/pallas_call | solution.py:97
  2.7 7.3 %all-to-all-start = ((bf16[8,512,128]{2,1,0:T(8,128)(2,1)}), bf16[8,512,128]{2,1,0:T(8,128)(2,1)S(1)}, u32[]{:S(2)}, u32[]{:S(2)}) async-start(bf16[8,512,128]{2,1,0:T(8,128)(2,1)} %pack_keys.1), calls=%async_computation | async-start | bytes 2097152 | tf_op jit(solution)/shard_map/all_to_all | solution.py:504
  10.0 4.6 %head_grads.1 = (bf16[512,128]{1,0:T(8,128)(2,1)}, bf16[512,128]{1,0:T(8,128)(2,1)}, bf16[512,128]{1,0:T(8,128)(2,1)}, bf16[512,128]{1,0:T(8,128)(2,1)}, bf16[12...) custom-call(bf16[128,1024]{1,0:T(8,128)(2,1)} %bitcast.11, bf16[128,2048]{1,0:T(8,128)(2,1)} %bitcast.10, ...), custom_call_target="tpu_custom_call" | custom-call | flops 1 | bytes 1 | tf_op jit(solution)/shard_map/head_grads/pallas_call | solution.py:140
  14.6 2.1 %collective-permute-start = (bf16[512,128]{1,0:T(8,128)(2,1)}, bf16[512,128]{1,0:T(8,128)(2,1)S(1)}, u32[]{:S(2)}, u32[]{:S(2)}) collective-permute-start(bf16[512,128]{1,0:T(8,128)(2,1)} %get-tuple-element.46), channel_id=1, source_target_pairs={{0,4},{4,0},{8,12},{12,8},{16,20},{20,16},{24,28},{28,24},{1,5},{5... | collective-permute-start | bytes 393224 | tf_op jit(solution)/shard_map/ppermute | solution.py:53
  18.7 4.4 %collective-permute-done.refs_1_ = bf16[512,128]{1,0:T(8,128)(2,1)S(1)} collective-permute-done((bf16[512,128]{1,0:T(8,128)(2,1)}, bf16[512,128]{1,0:T(8,128)(2,1)S(1)}, u32[]{:S(2)}, u32[]{:S(2)}) %collective-permute-start) | collective-permute-done | bytes 131104 | tf_op jit(solution)/shard_map/ppermute | solution.py:53
  23.1 8.1 %collective-permute-done.1.refs_2_ = bf16[512,128]{1,0:T(8,128)(2,1)S(1)} collective-permute-done((bf16[512,128]{1,0:T(8,128)(2,1)}, bf16[512,128]{1,0:T(8,128)(2,1)S(1)}, u32[]{:S(2)}, u32[]{:S(2)}) %collective-permute-start.1) | collective-permute-done | bytes 131104 | tf_op jit(solution)/shard_map/ppermute | solution.py:53
  31.1 3.8 %collective-permute-start.9 = (bf16[128,1024]{1,0:T(8,128)(2,1)}, bf16[128,1024]{1,0:T(8,128)(2,1)S(1)}, u32[]{:S(2)}, u32[]{:S(2)}) collective-permute-start(bf16[128,1024]{1,0:T(8,128)(2,1)} %get-tuple-element.69), channel_id=1, source_target_pairs={{0,12},{4,8},{8,4},{12,0},{16,28},{20,24},{24,20},{28,16},{1,13},{... | collective-permute-start | bytes 786440 | tf_op jit(solution)/shard_map/ppermute | solution.py:53
  37.3 3.5 %attend.1 = (bf16[1024,128]{1,0:T(8,128)(2,1)S(1)}, f32[2,512]{1,0:T(2,128)S(1)}, f32[2,512]{1,0:T(2,128)S(1)}) custom-call(f32[16,1024]{1,0:T(8,128)S(1)} %reshape.14.bias_ref, bf16[8,512,128]{2,1,0:T(8,128)(2,1)S(1)} %all-to-all-done.pairs, bf16[2,512,128]{2,1,0:T(8,128)(2,1)S(1)} %get-tuple-element.51.queries), custom_call_target="tpu_custom_call" | custom-call | flops 1 | bytes 1 | tf_op jit(solution)/shard_map/attend/pallas_call | solution.py:221
  40.8 1.5 %collective-permute-start.6 = (bf16[1024,128]{1,0:T(8,128)(2,1)S(1)}, bf16[1024,128]{1,0:T(8,128)(2,1)S(1)}, u32[]{:S(2)}, u32[]{:S(2)}) collective-permute-start(bf16[1024,128]{1,0:T(8,128)(2,1)S(1)} %get-tuple-element.67.near), channel_id=1, source_target_pairs={{0,4},{4,0},{8,12},{12,8},{16,20},{20,16},{24,28},{28,24},{1,5},{5... | collective-permute-start | bytes 786440 | tf_op jit(solution)/shard_map/ppermute | solution.py:53
  42.3 4.7 %attend_back.1 = (bf16[8,512,128]{2,1,0:T(8,128)(2,1)}, bf16[512,128]{1,0:T(8,128)(2,1)}, bf16[512,128]{1,0:T(8,128)(2,1)}, bf16[512,128]{1,0:T(8,128)(2,1)}, bf16[512,128]{1,0:T(8,128)(2,1)}) custom-call(f32[16,1024]{1,0:T(8,128)S(1)} %reshape.14.bias_ref, f32[2,512]{1,0:T(2,128)S(1)} %get-tuple-element.52.top_ref, f32[2,512]{1,0:T(2,128)S(1)} %get-tuple-element.53.sum_ref, ...), custom_call_target="tpu_custom_call" | custom-call | flops 1 | bytes 1 | tf_op jit(solution)/shard_map/attend_back/pallas_call | solution.py:276
  47.0 5.4 %all-to-all-start.1 = ((bf16[8,512,128]{2,1,0:T(8,128)(2,1)}), bf16[8,512,128]{2,1,0:T(8,128)(2,1)S(1)}, u32[]{:S(2)}, u32[]{:S(2)}) async-start(bf16[8,512,128]{2,1,0:T(8,128)(2,1)} %get-tuple-element.62), calls=%async_computation.1 | async-start | bytes 2097152 | tf_op jit(solution)/shard_map/all_to_all | solution.py:519
  53.3 2.6 %weight_part.1 = (f32[1024,256]{1,0:T(8,128)S(1)}, bf16[1024,256]{1,0:T(8,128)(2,1)S(1)}) custom-call(bf16[1024,128]{1,0:T(8,128)(2,1)S(1)} %get-tuple-element.67.near, bf16[1024,128]{1,0:T(8,128)(2,1)S(1)} %collective-permute-done.6.near_pair, bf16[128,1024]{1,0:T(8,128)(2,1)} %get-tuple-element.68.refs_0_, bf16[128,1024]{1,0:T(8,128)(2,1)} %copy-done.5, ...), custom_call_target="tpu_custom_call" | custom-call | flops 1 | bytes 1 | tf_op jit(solution)/shard_map/weight_part/pallas_call | solution.py:393
  56.0 1.9 %collective-permute-done.10.other = bf16[1024,256]{1,0:T(8,128)(2,1)S(1)} collective-permute-done((bf16[1024,256]{1,0:T(8,128)(2,1)S(1)}, bf16[1024,256]{1,0:T(8,128)(2,1)S(1)}, u32[]{:S(2)}, u32[]{:S(2)}) %collective-permute-start.10) | collective-permute-done | bytes 524320 | tf_op jit(solution)/shard_map/ppermute | solution.py:53
  57.9 1.6 %collective-permute-start.11 = (bf16[512,256]{1,0:T(8,128)(2,1)S(1)}, bf16[512,256]{1,0:T(8,128)(2,1)S(1)}, u32[]{:S(2)}, u32[]{:S(2)}) collective-permute-start(bf16[512,256]{1,0:T(8,128)(2,1)S(1)} %get-tuple-element.73), channel_id=1, source_target_pairs={{0,2},{1,3},{2,0},{3,1},{4,6},{5,7},{6,4},{7,5},{8,10},{9,11},{10,... | collective-permute-start | bytes 786440 | tf_op jit(solution)/shard_map/ppermute | solution.py:53
  59.5 2.0 %collective-permute-start.3 = (bf16[512,128]{1,0:T(8,128)(2,1)S(1)}, bf16[512,128]{1,0:T(8,128)(2,1)S(1)}, u32[]{:S(2)}, u32[]{:S(2)}) collective-permute-start(bf16[512,128]{1,0:T(8,128)(2,1)S(1)} %copy-done.10), channel_id=1, source_target_pairs={{0,4},{4,0},{8,12},{12,8},{16,20},{20,16},{24,28},{28,24},{1,5},{5... | collective-permute-start | bytes 393224 | tf_op jit(solution)/shard_map/ppermute | solution.py:53
  63.1 3.3 %collective-permute-done.11.other = bf16[512,256]{1,0:T(8,128)(2,1)S(1)} collective-permute-done((bf16[512,256]{1,0:T(8,128)(2,1)S(1)}, bf16[512,256]{1,0:T(8,128)(2,1)S(1)}, u32[]{:S(2)}, u32[]{:S(2)}) %collective-permute-start.11) | collective-permute-done | bytes 262176 | tf_op jit(solution)/shard_map/ppermute | solution.py:53
  66.4 3.0 %collective-permute-start.12 = (bf16[128,256]{1,0:T(8,128)(2,1)S(1)}, bf16[128,256]{1,0:T(8,128)(2,1)S(1)}, u32[]{:S(2)}, u32[]{:S(2)}) collective-permute-start(bf16[128,256]{1,0:T(8,128)(2,1)S(1)} %get-tuple-element.75), channel_id=1, source_target_pairs={{0,16},{4,20},{8,24},{12,28},{16,0},{20,4},{24,8},{28,12},{1,17},{... | collective-permute-start | bytes 196616 | tf_op jit(solution)/shard_map/ppermute | solution.py:53
  69.4 1.6 %collective-permute-start.13 = (bf16[128,256]{1,0:T(8,128)(2,1)S(1)}, bf16[128,256]{1,0:T(8,128)(2,1)S(1)}, u32[]{:S(2)}, u32[]{:S(2)}) collective-permute-start(bf16[128,256]{1,0:T(8,128)(2,1)S(1)} %get-tuple-element.76), channel_id=1, source_target_pairs={{0,4},{4,0},{8,12},{12,8},{16,20},{20,16},{24,28},{28,24},{1,5},{5... | collective-permute-start | bytes 196616 | tf_op jit(solution)/shard_map/ppermute | solution.py:53
  71.0 1.6 %collective-permute-done.4.refs_2_ = bf16[512,128]{1,0:T(8,128)(2,1)S(1)} collective-permute-done((bf16[512,128]{1,0:T(8,128)(2,1)S(1)}, bf16[512,128]{1,0:T(8,128)(2,1)S(1)}, u32[]{:S(2)}, u32[]{:S(2)}) %collective-permute-start.4) | collective-permute-done | bytes 131104 | tf_op jit(solution)/shard_map/ppermute | solution.py:53
  72.6 1.8 %collective-permute-done.5.refs_3_ = bf16[512,128]{1,0:T(8,128)(2,1)S(1)} collective-permute-done((bf16[512,128]{1,0:T(8,128)(2,1)S(1)}, bf16[512,128]{1,0:T(8,128)(2,1)S(1)}, u32[]{:S(2)}, u32[]{:S(2)}) %collective-permute-start.5) | collective-permute-done | bytes 131104 | tf_op jit(solution)/shard_map/ppermute | solution.py:53
  76.2 2.5 %project.1 = (bf16[128,2048]{1,0:T(8,128)(2,1)}, bf16[16,128]{1,0:T(8,128)(2,1)S(1)}) custom-call(bf16[128,1024]{1,0:T(8,128)(2,1)S(1)} %join_heads.1.attended, bf16[1024,2048]{1,0:T(8,128)(2,1)S(1)} %copy-done), custom_call_target="tpu_custom_call" | custom-call | flops 1 | bytes 1 | tf_op jit(solution)/shard_map/project/pallas_call | solution.py:351
  78.8 1.5 %collective-permute-done.12.refs_1_ = bf16[128,256]{1,0:T(8,128)(2,1)S(1)} collective-permute-done((bf16[128,256]{1,0:T(8,128)(2,1)S(1)}, bf16[128,256]{1,0:T(8,128)(2,1)S(1)}, u32[]{:S(2)}, u32[]{:S(2)}) %collective-permute-start.12) | collective-permute-done | bytes 65568 | tf_op jit(solution)/shard_map/ppermute | solution.py:53
  81.6 1.6 %collective-permute-start.15 = (bf16[256,256]{1,0:T(8,128)(2,1)S(1)}, bf16[256,256]{1,0:T(8,128)(2,1)S(1)}, u32[]{:S(2)}, u32[]{:S(2)}) collective-permute-start(bf16[256,256]{1,0:T(8,128)(2,1)S(1)} %weight_scale.1.refs_0_), channel_id=1, source_target_pairs={{0,2},{1,3},{2,0},{3,1},{4,6},{5,7},{6,4},{7,5},{8,10},{9,11},{10,... | collective-permute-start | bytes 393224 | tf_op jit(solution)/shard_map/ppermute | solution.py:53
  83.2 2.1 %unpack_grads.1 = (bf16[128,1024]{1,0:T(8,128)(2,1)}, bf16[128,1024]{1,0:T(8,128)(2,1)}, bf16[128,1024]{1,0:T(8,128)(2,1)}, bf16[16,128]{1,0:T(8,128)(2,1)S(1)}) custom-call(bf16[8,512,128]{2,1,0:T(8,128)(2,1)S(1)} %all-to-all-done.1.returned, bf16[512,128]{1,0:T(8,128)(2,1)} %get-tuple-element.56.refs_0_, bf16[512,128]{1,0:T(8,128)(2,1)} %copy-done.1, ...), custom_call_target="tpu_custom_call" | custom-call | flops 1 | bytes 3145728 | tf_op jit(solution)/shard_map/unpack_grads/pallas_call | solution.py:309
  (63 shorter events, 13.9 us)
Async XLA Ops:
  0.6 17.6 %copy-start.7 = (s32[16,8]{0,1:T(8,128)S(1)}, s32[16,8]{0,1:T(8,128)}, u32[]{:S(2)}) copy-start(s32[16,8]{0,1:T(8,128)} %param.11) | copy-start | bytes 1540
  2.7 34.6 %all-to-all-start = ((bf16[8,512,128]{2,1,0:T(8,128)(2,1)}), bf16[8,512,128]{2,1,0:T(8,128)(2,1)S(1)}, u32[]{:S(2)}, u32[]{:S(2)}) async-start(bf16[8,512,128]{2,1,0:T(8,128)(2,1)} %pack_keys.1), calls=%async_computation | async-start | bytes 2097152 | tf_op jit(solution)/shard_map/all_to_all | solution.py:504
  14.6 8.4 %collective-permute-start = (bf16[512,128]{1,0:T(8,128)(2,1)}, bf16[512,128]{1,0:T(8,128)(2,1)S(1)}, u32[]{:S(2)}, u32[]{:S(2)}) collective-permute-start(bf16[512,128]{1,0:T(8,128)(2,1)} %get-tuple-element.46), channel_id=1, source_target_pairs={{0,4},{4,0},{8,12},{12,8},{16,20},{20,16},{24,28},{28,24},{1,5},{5... | collective-permute-start | bytes 393224 | tf_op jit(solution)/shard_map/ppermute | solution.py:53
  16.7 14.4 %collective-permute-start.1 = (bf16[512,128]{1,0:T(8,128)(2,1)}, bf16[512,128]{1,0:T(8,128)(2,1)S(1)}, u32[]{:S(2)}, u32[]{:S(2)}) collective-permute-start(bf16[512,128]{1,0:T(8,128)(2,1)} %get-tuple-element.47), channel_id=1, source_target_pairs={{0,8},{4,12},{8,0},{12,4},{16,24},{20,28},{24,16},{28,20},{1,9},{5... | collective-permute-start | bytes 393224 | tf_op jit(solution)/shard_map/ppermute | solution.py:53
  18.2 17.3 %collective-permute-start.2 = (bf16[512,128]{1,0:T(8,128)(2,1)}, bf16[512,128]{1,0:T(8,128)(2,1)S(1)}, u32[]{:S(2)}, u32[]{:S(2)}) collective-permute-start(bf16[512,128]{1,0:T(8,128)(2,1)} %get-tuple-element.50), channel_id=1, source_target_pairs={{0,12},{4,8},{8,4},{12,0},{16,28},{20,24},{24,20},{28,16},{1,13},{... | collective-permute-start | bytes 393224 | tf_op jit(solution)/shard_map/ppermute | solution.py:53
  31.1 21.3 %collective-permute-start.9 = (bf16[128,1024]{1,0:T(8,128)(2,1)}, bf16[128,1024]{1,0:T(8,128)(2,1)S(1)}, u32[]{:S(2)}, u32[]{:S(2)}) collective-permute-start(bf16[128,1024]{1,0:T(8,128)(2,1)} %get-tuple-element.69), channel_id=1, source_target_pairs={{0,12},{4,8},{8,4},{12,0},{16,28},{20,24},{24,20},{28,16},{1,13},{... | collective-permute-start | bytes 786440 | tf_op jit(solution)/shard_map/ppermute | solution.py:53
  34.9 17.5 %collective-permute-start.7 = (bf16[128,1024]{1,0:T(8,128)(2,1)}, bf16[128,1024]{1,0:T(8,128)(2,1)S(1)}, u32[]{:S(2)}, u32[]{:S(2)}) collective-permute-start(bf16[128,1024]{1,0:T(8,128)(2,1)} %get-tuple-element.69), channel_id=1, source_target_pairs={{0,4},{4,0},{8,12},{12,8},{16,20},{20,16},{24,28},{28,24},{1,5},{5... | collective-permute-start | bytes 786440 | tf_op jit(solution)/shard_map/ppermute | solution.py:53
  35.0 17.4 %collective-permute-start.8 = (bf16[128,1024]{1,0:T(8,128)(2,1)}, bf16[128,1024]{1,0:T(8,128)(2,1)S(1)}, u32[]{:S(2)}, u32[]{:S(2)}) collective-permute-start(bf16[128,1024]{1,0:T(8,128)(2,1)} %get-tuple-element.68.refs_0_), channel_id=1, source_target_pairs={{0,8},{4,12},{8,0},{12,4},{16,24},{20,28},{24,16},{28,20},{1,9},{5... | collective-permute-start | bytes 786440 | tf_op jit(solution)/shard_map/ppermute | solution.py:53
  40.8 11.7 %collective-permute-start.6 = (bf16[1024,128]{1,0:T(8,128)(2,1)S(1)}, bf16[1024,128]{1,0:T(8,128)(2,1)S(1)}, u32[]{:S(2)}, u32[]{:S(2)}) collective-permute-start(bf16[1024,128]{1,0:T(8,128)(2,1)S(1)} %get-tuple-element.67.near), channel_id=1, source_target_pairs={{0,4},{4,0},{8,12},{12,8},{16,20},{20,16},{24,28},{28,24},{1,5},{5... | collective-permute-start | bytes 786440 | tf_op jit(solution)/shard_map/ppermute | solution.py:53
  47.0 14.5 %copy-start.9 = (bf16[512,128]{1,0:T(8,128)(2,1)S(1)}, bf16[512,128]{1,0:T(8,128)(2,1)}, u32[]{:S(2)}) copy-start(bf16[512,128]{1,0:T(8,128)(2,1)} %get-tuple-element.58) | copy-start | bytes 393220
  47.0 16.0 %copy-start.8 = (bf16[512,128]{1,0:T(8,128)(2,1)S(1)}, bf16[512,128]{1,0:T(8,128)(2,1)}, u32[]{:S(2)}) copy-start(bf16[512,128]{1,0:T(8,128)(2,1)} %get-tuple-element.59) | copy-start | bytes 393220
  47.0 36.2 %all-to-all-start.1 = ((bf16[8,512,128]{2,1,0:T(8,128)(2,1)}), bf16[8,512,128]{2,1,0:T(8,128)(2,1)S(1)}, u32[]{:S(2)}, u32[]{:S(2)}) async-start(bf16[8,512,128]{2,1,0:T(8,128)(2,1)} %get-tuple-element.62), calls=%async_computation.1 | async-start | bytes 2097152 | tf_op jit(solution)/shard_map/all_to_all | solution.py:519
  52.4 23.8 %copy-start = (bf16[1024,2048]{1,0:T(8,128)(2,1)S(1)}, bf16[1024,2048]{1,0:T(8,128)(2,1)}, u32[]{:S(2)}) copy-start(bf16[1024,2048]{1,0:T(8,128)(2,1)} %weight_ref.3) | copy-start | bytes 12582916
  55.9 2.0 %collective-permute-start.10 = (bf16[1024,256]{1,0:T(8,128)(2,1)S(1)}, bf16[1024,256]{1,0:T(8,128)(2,1)S(1)}, u32[]{:S(2)}, u32[]{:S(2)}) collective-permute-start(bf16[1024,256]{1,0:T(8,128)(2,1)S(1)} %get-tuple-element.71), channel_id=1, source_target_pairs={{0,1},{1,0},{2,3},{3,2},{4,5},{5,4},{6,7},{7,6},{8,9},{9,8},{10,11... | collective-permute-start | bytes 1572872 | tf_op jit(solution)/shard_map/ppermute | solution.py:53
  57.9 8.4 %collective-permute-start.11 = (bf16[512,256]{1,0:T(8,128)(2,1)S(1)}, bf16[512,256]{1,0:T(8,128)(2,1)S(1)}, u32[]{:S(2)}, u32[]{:S(2)}) collective-permute-start(bf16[512,256]{1,0:T(8,128)(2,1)S(1)} %get-tuple-element.73), channel_id=1, source_target_pairs={{0,2},{1,3},{2,0},{3,1},{4,6},{5,7},{6,4},{7,5},{8,10},{9,11},{10,... | collective-permute-start | bytes 786440 | tf_op jit(solution)/shard_map/ppermute | solution.py:53
  59.5 11.5 %collective-permute-start.3 = (bf16[512,128]{1,0:T(8,128)(2,1)S(1)}, bf16[512,128]{1,0:T(8,128)(2,1)S(1)}, u32[]{:S(2)}, u32[]{:S(2)}) collective-permute-start(bf16[512,128]{1,0:T(8,128)(2,1)S(1)} %copy-done.10), channel_id=1, source_target_pairs={{0,4},{4,0},{8,12},{12,8},{16,20},{20,16},{24,28},{28,24},{1,5},{5... | collective-permute-start | bytes 393224 | tf_op jit(solution)/shard_map/ppermute | solution.py:53
  61.6 11.1 %collective-permute-start.4 = (bf16[512,128]{1,0:T(8,128)(2,1)S(1)}, bf16[512,128]{1,0:T(8,128)(2,1)S(1)}, u32[]{:S(2)}, u32[]{:S(2)}) collective-permute-start(bf16[512,128]{1,0:T(8,128)(2,1)S(1)} %copy-done.9), channel_id=1, source_target_pairs={{0,8},{4,12},{8,0},{12,4},{16,24},{20,28},{24,16},{28,20},{1,9},{5... | collective-permute-start | bytes 393224 | tf_op jit(solution)/shard_map/ppermute | solution.py:53
  63.0 11.4 %collective-permute-start.5 = (bf16[512,128]{1,0:T(8,128)(2,1)S(1)}, bf16[512,128]{1,0:T(8,128)(2,1)S(1)}, u32[]{:S(2)}, u32[]{:S(2)}) collective-permute-start(bf16[512,128]{1,0:T(8,128)(2,1)S(1)} %copy-done.8), channel_id=1, source_target_pairs={{0,12},{4,8},{8,4},{12,0},{16,28},{20,24},{24,20},{28,16},{1,13},{... | collective-permute-start | bytes 393224 | tf_op jit(solution)/shard_map/ppermute | solution.py:53
  66.4 13.9 %collective-permute-start.12 = (bf16[128,256]{1,0:T(8,128)(2,1)S(1)}, bf16[128,256]{1,0:T(8,128)(2,1)S(1)}, u32[]{:S(2)}, u32[]{:S(2)}) collective-permute-start(bf16[128,256]{1,0:T(8,128)(2,1)S(1)} %get-tuple-element.75), channel_id=1, source_target_pairs={{0,16},{4,20},{8,24},{12,28},{16,0},{20,4},{24,8},{28,12},{1,17},{... | collective-permute-start | bytes 196616 | tf_op jit(solution)/shard_map/ppermute | solution.py:53
  69.4 10.9 %collective-permute-start.13 = (bf16[128,256]{1,0:T(8,128)(2,1)S(1)}, bf16[128,256]{1,0:T(8,128)(2,1)S(1)}, u32[]{:S(2)}, u32[]{:S(2)}) collective-permute-start(bf16[128,256]{1,0:T(8,128)(2,1)S(1)} %get-tuple-element.76), channel_id=1, source_target_pairs={{0,4},{4,0},{8,12},{12,8},{16,20},{20,16},{24,28},{28,24},{1,5},{5... | collective-permute-start | bytes 196616 | tf_op jit(solution)/shard_map/ppermute | solution.py:53
  71.0 10.6 %collective-permute-start.14 = (bf16[128,256]{1,0:T(8,128)(2,1)S(1)}, bf16[128,256]{1,0:T(8,128)(2,1)S(1)}, u32[]{:S(2)}, u32[]{:S(2)}) collective-permute-start(bf16[128,256]{1,0:T(8,128)(2,1)S(1)} %get-tuple-element.77), channel_id=1, source_target_pairs={{0,20},{4,16},{8,28},{12,24},{16,4},{20,0},{24,12},{28,8},{1,21},{... | collective-permute-start | bytes 196616 | tf_op jit(solution)/shard_map/ppermute | solution.py:53
  81.6 5.0 %collective-permute-start.15 = (bf16[256,256]{1,0:T(8,128)(2,1)S(1)}, bf16[256,256]{1,0:T(8,128)(2,1)S(1)}, u32[]{:S(2)}, u32[]{:S(2)}) collective-permute-start(bf16[256,256]{1,0:T(8,128)(2,1)S(1)} %weight_scale.1.refs_0_), channel_id=1, source_target_pairs={{0,2},{1,3},{2,0},{3,1},{4,6},{5,7},{6,4},{7,5},{8,10},{9,11},{10,... | collective-permute-start | bytes 393224 | tf_op jit(solution)/shard_map/ppermute | solution.py:53
  83.2 3.5 %collective-permute-start.16 = (bf16[256,256]{1,0:T(8,128)(2,1)S(1)}, bf16[256,256]{1,0:T(8,128)(2,1)S(1)}, u32[]{:S(2)}, u32[]{:S(2)}) collective-permute-start(bf16[256,256]{1,0:T(8,128)(2,1)S(1)} %weight_scale.1.refs_0_), channel_id=1, source_target_pairs={{0,1},{1,0},{2,3},{3,2},{4,5},{5,4},{6,7},{7,6},{8,9},{9,8},{10,11... | collective-permute-start | bytes 393224 | tf_op jit(solution)/shard_map/ppermute | solution.py:53
  86.7 1.3 %collective-permute-start.17 = (bf16[256,256]{1,0:T(8,128)(2,1)S(1)}, bf16[256,256]{1,0:T(8,128)(2,1)S(1)}, u32[]{:S(2)}, u32[]{:S(2)}) collective-permute-start(bf16[256,256]{1,0:T(8,128)(2,1)S(1)} %collective-permute-done.15.refs_2_), channel_id=1, source_target_pairs={{0,1},{1,0},{2,3},{3,2},{4,5},{5,4},{6,7},{7,6},{8,9},{9,8},{10,11... | collective-permute-start | bytes 393224 | tf_op jit(solution)/shard_map/ppermute | solution.py:53
  (10 other events, 38.1 us)

commit v4 on v3

--- a/solution.py
+++ b/solution.py
@@ -11,6 +11,7 @@
 HD = 128
 BLK = 64
 MASKED = -1e30
+LOG2E = math.log2(math.e)
 VMEM = pltpu.VMEM
 ANY_SPEC = pl.BlockSpec(memory_space=pl.ANY)
 VMEM_SPEC = pl.BlockSpec()
@@ -156,27 +157,14 @@
     )(queries, grads, out_weight)
 
 
-def join_queries_kernel(*refs):
-    parts, (queries, grads) = refs[:-2], refs[-2:]
+def load_queries(parts, queries, grads=None):
     rows = parts[0].shape[0] // 4
     for mask, part in enumerate(parts):
         for slot in range(2):
             queries[slot, span(member(mask), rows)] = part[slot * rows : (slot + 1) * rows]
-            grad = part[2 * rows + slot * HD : 2 * rows + (slot + 1) * HD]
-            grads[slot, :, span(member(mask), rows)] = grad
-
-
-def join_queries(parts):
-    tokens = len(parts) * parts[0].shape[0] // 4
-    return pl.pallas_call(
-        join_queries_kernel,
-        out_shape=[struct(2, tokens, HD), struct(2, HD, tokens)],
-        in_specs=[VMEM_SPEC] * len(parts),
-        out_specs=[VMEM_SPEC] * 2,
-        compiler_params=params(8),
-        cost_estimate=cost(JOIN_FLOPS),
-        name="join_queries",
-    )(*map(in_hbm, parts))
+            if grads is not None:
+                grad = part[2 * rows + slot * HD : 2 * rows + (slot + 1) * HD]
+                grads[slot, :, span(member(mask), rows)] = grad
 
 
 def load_heads(pairs, keys, values):
@@ -190,13 +178,15 @@
 
 def scores_of(keys, queries, bias, scale):
     blocks = bias.shape[0]
-    scores = dot(keys, queries, NT) * scale
+    scores = dot(keys, queries, NT) * (scale * LOG2E)
     shaped = scores.reshape(blocks, BLK, queries.shape[0]) + bias[:, None, :]
     return shaped.reshape(scores.shape)
 
 
-def forward_kernel(chunk, scale, bias_ref, pairs, queries, near, top_ref, sum_ref, keys, values):
+def forward_kernel(members, chunk, scale, bias_ref, pairs, *refs):
+    parts, (near, norm_ref, keys, values, queries) = refs[:members], refs[members:]
     load_heads(pairs, keys, values)
+    load_queries(parts, queries)
     tokens = queries.shape[1]
     for slot in range(2):
         value_cols = values[slot].T
@@ -205,34 +195,36 @@
             bias = bias_ref[:, span(half_of() * (tokens // chunk) + step, chunk)]
             scores = scores_of(keys[slot], queries[slot, rows], bias, scale)
             top = jnp.max(scores, axis=0, keepdims=True)
-            weights = jnp.exp(scores - top)
-            total = 1.0 / jnp.sum(weights, axis=0, keepdims=True)
-            probs_low = (weights * total).astype(jnp.bfloat16)
+            weights = jnp.exp2(scores - top)
+            total = jnp.sum(weights, axis=0, keepdims=True)
+            probs_low = (weights * (1.0 / total)).astype(jnp.bfloat16)
             place = pl.ds(slot * tokens + step * chunk, chunk)
             near[place] = dot(value_cols, probs_low, NN).T.astype(jnp.bfloat16)
-            top_ref[slot : slot + 1, rows] = top
-            sum_ref[slot : slot + 1, rows] = total
-
-
-def forward(bias, pairs, queries, scale):
+            norm_ref[slot : slot + 1, rows] = top + jnp.log2(total)
+
+
+def forward(bias, pairs, parts, scale):
     tokens = bias.shape[1]
-    chunk = 2 * tokens // pairs.shape[0]
+    chunk = 4 * tokens // pairs.shape[0]
     stats = struct(2, tokens // 2, dtype=jnp.float32)
     return pl.pallas_call(
-        functools.partial(forward_kernel, chunk, scale),
-        out_shape=[struct(tokens, HD), stats, stats],
-        in_specs=[VMEM_SPEC] * 3,
-        out_specs=[VMEM_SPEC] * 3,
-        scratch_shapes=[VMEM((2, tokens, HD), jnp.bfloat16)] * 2,
-        compiler_params=params(24),
+        functools.partial(forward_kernel, len(parts), chunk, scale),
+        out_shape=[struct(tokens, HD), stats],
+        in_specs=[VMEM_SPEC] * (2 + len(parts)),
+        out_specs=[VMEM_SPEC] * 2,
+        scratch_shapes=[VMEM((2, tokens, HD), jnp.bfloat16)] * 2
+        + [VMEM((2, tokens // 2, HD), jnp.bfloat16)],
+        compiler_params=params(30),
         cost_estimate=cost(),
         name="attend",
-    )(bias, pairs, queries)
-
-
-def backward_kernel(chunk, scale, bias_ref, top_ref, sum_ref, pairs, queries, grads, near, *refs):
-    returns, outs, (keys, values, query_grad, key_sum, value_sum) = refs[0], refs[1:-5], refs[-5:]
+    )(bias, pairs, *parts)
+
+
+def backward_kernel(members, chunk, scale, bias_ref, norm_ref, pairs, near, *refs):
+    parts, returns, outs, refs = refs[:members], refs[members], refs[members + 1 : -5], refs[-5:]
+    keys, values, queries, grads, query_grad = refs
     load_heads(pairs, keys, values)
+    load_queries(parts, queries, grads)
     tokens = queries.shape[1]
     peers = returns.shape[0]
     here = returns.shape[1] // 4
@@ -241,27 +233,20 @@
         for step in range(tokens // chunk):
             rows = slice(step * chunk, (step + 1) * chunk)
             bias = bias_ref[:, span(half_of() * (tokens // chunk) + step, chunk)]
-            scores = scores_of(keys[slot], queries[slot, rows], bias, scale)
-            probs = jnp.exp(scores - top_ref[slot : slot + 1, rows]) * sum_ref[slot : slot + 1, rows]
+            bias = bias - norm_ref[slot : slot + 1, rows]
+            probs = jnp.exp2(scores_of(keys[slot], queries[slot, rows], bias, scale))
             prob_grad = dot(values[slot], grads[slot, :, rows], NN)
             delta = jnp.sum(probs * prob_grad, axis=0, keepdims=True)
             score_grad = (probs * (prob_grad - delta)).astype(jnp.bfloat16)
             value_part = dot(probs.astype(jnp.bfloat16), grads[slot, :, rows], NT)
             key_part = dot(score_grad, queries[slot, rows], NN)
-            if step == 0:
-                value_sum[...] = value_part
-                key_sum[...] = key_part
-            else:
-                value_sum[...] += value_part
-                key_sum[...] += key_part
+            key_total = key_part if step == 0 else key_total + key_part
+            value_total = value_part if step == 0 else value_total + value_part
             query_part = dot(key_cols, score_grad, NN) * scale
             query_grad[slot, rows] = query_part.T.astype(jnp.bfloat16)
-        for peer in range(peers):
-            place = slice(peer * here, (peer + 1) * here)
-            key_low = (key_sum[place] * scale).astype(jnp.bfloat16)
-            returns[peer, slot * here : (slot + 1) * here] = key_low
-            value_low = value_sum[place].astype(jnp.bfloat16)
-            returns[peer, (2 + slot) * here : (3 + slot) * here] = value_low
+        for first, total in ((slot, key_total * scale), (2 + slot, value_total)):
+            low = total.astype(jnp.bfloat16).reshape(peers, here, HD)
+            returns[:, first * here : (first + 1) * here] = low
         for mask, out in enumerate(outs):
             theirs = span(member(mask), here)
             out[slot * here : (slot + 1) * here] = query_grad[slot, theirs]
@@ -269,22 +254,22 @@
             out[(2 + slot) * here : (3 + slot) * here] = near[theirs]
 
 
-def backward(bias, top, total, pairs, queries, grads, near, scale):
+def backward(bias, norm, pairs, parts, near, scale):
     peers, tokens = pairs.shape[0], bias.shape[1]
     members = members_of(peers)
     here = tokens // peers
     return pl.pallas_call(
-        functools.partial(backward_kernel, 2 * here, scale),
+        functools.partial(backward_kernel, members, 4 * here, scale),
         out_shape=[struct(peers, 4 * here, HD)] + [pltpu.HBM((4 * here, HD), jnp.bfloat16)] * members,
-        in_specs=[VMEM_SPEC] * 7,
+        in_specs=[VMEM_SPEC] * (4 + members),
         out_specs=[VMEM_SPEC] * (1 + members),
         scratch_shapes=[VMEM((2, tokens, HD), jnp.bfloat16)] * 2
-        + [VMEM((2, tokens // 2, HD), jnp.bfloat16)]
-        + [VMEM((tokens, HD), jnp.float32)] * 2,
-        compiler_params=params(24),
+        + [VMEM((2, tokens // 2, HD), jnp.bfloat16), VMEM((2, HD, tokens // 2), jnp.bfloat16)]
+        + [VMEM((2, tokens // 2, HD), jnp.bfloat16)],
+        compiler_params=params(30),
         cost_estimate=cost(),
         name="attend_back",
-    )(bias, top, total, pairs, queries, grads, near)
+    )(bias, norm, pairs, near, *parts)
 
 
 def unpack_kernel(returned, *refs):
@@ -360,7 +345,7 @@
             pl.BlockSpec((rows, tile), lambda i: (0, i)),
             pl.BlockSpec((16, HD), lambda i: (0, 0)),
         ],
-        compiler_params=params(24),
+        compiler_params=params(30),
         cost_estimate=cost(PROJECT_FLOPS, 1),
         name="project",
     )(attended, out_weight)
@@ -395,7 +380,7 @@
         out_shape=[struct(rows, width, dtype=jnp.float32), struct(rows, width)],
         in_specs=[VMEM_SPEC] * (2 + len(grads)),
         out_specs=[VMEM_SPEC] * 2,
-        compiler_params=params(24),
+        compiler_params=params(30),
         cost_estimate=cost(),
         name="weight_part",
     )(near, near_pair, *map(in_hbm, grads))
@@ -489,7 +474,7 @@
     blocks = pattern.shape[0]
     named = pattern[:, :, None] == jnp.arange(blocks, dtype=pattern.dtype)
     counts = jnp.sum(named.astype(jnp.float32), axis=1).T
-    bias = jnp.where(counts > 0, jnp.log(jnp.maximum(counts, 1.0)), MASKED)
+    bias = jnp.where(counts > 0, jnp.log2(jnp.maximum(counts, 1.0)), MASKED)
     return jnp.repeat(bias, tokens // blocks, axis=1)
 
 
@@ -506,15 +491,14 @@
     )
     *sends, grad_mine, grad_theirs = head_grads(query_in[0], grad_out[0], out_weight, members)
     parts = [sends[0]] + [swap(sends[mask], "seq", mask) for mask in range(1, members)]
-    grad_mine, grad_theirs, *parts[1:3] = after(grad_mine, grad_theirs, *parts[1:3])
-    queries, head_grad = join_queries(parts)
+    grad_mine, grad_theirs, *parts[1:2] = after(grad_mine, grad_theirs, *parts[1:2])
     half_grads = [grad_mine] + [
         swap(grad_theirs if mask & 1 else grad_mine, "seq", mask) for mask in range(1, members)
     ]
 
-    near, top, total = forward(bias, pairs, queries, scale)
+    near, norm = forward(bias, pairs, parts, scale)
     near_pair = swap(near, "seq", 1)
-    returns, *sends = backward(bias, top, total, pairs, queries, head_grad, near, scale)
+    returns, *sends = backward(bias, norm, pairs, parts, near, scale)
     near, returns = after(near, returns)
     returned = lax.all_to_all(returns, "seq", split_axis=0, concat_axis=0, tiled=True)
     parts = [sends[0]] + [swap(sends[mask], "seq", mask) for mask in range(1, members)]

time: 89.4 us -> 87.5 us (0.979)
  Pallas kernels: 25.6 us -> 22.7 us
  waiting for transfers between devices: 26.5 us -> 27.5 us
    pallas_call x3 -> x2, Pallas kernels: 9.33 us -> 6.38 us  [the longest x1 4.26 us: backward(): pl.pallas_call(functools.partial(backward_kernel, members, 4 * here, scal...]
    ppermute x18, waiting for transfers between devices: 26.5 us -> 27.5 us  [swap(): lax.ppermute(array, axis, [(i, i ^ mask) for i in range(lax.axis_size(axi...]
    unnamed x29 -> x25, local copies, waits for them, and re-layouts: 2.2 us -> 2.46 us
  transfers between devices with their start and end apart: 20 -> 20, of which waited for: 10 -> 11; matrix products, arithmetic and copies ran while one was open for 0% -> 0% of each run, Pallas kernels for 25% -> 22%
where the time goes in v4:
time: 87.5 us; the launch traced here: 87.1 us
  starting transfers between devices  33.3 us (38%)
  waiting for transfers between devices  27.5 us (31%)
  Pallas kernels  22.7 us (26%)
  local copies, waits for them, and re-layouts  2.72 us (3%)
    ppermute x18, waiting for transfers between devices, swap(): lax.ppermute(array, axis, [(i, i ^ mask) for i in range(lax.axis_size(axi...  27.5 us
    ppermute x18, starting transfers between devices, swap(): lax.ppermute(array, axis, [(i, i ^ mask) for i in range(lax.axis_size(axi...  20.8 us
    all_to_all x1, starting transfers between devices, dense_local(): lax.all_to_all(pack(key_in[0], value_in[0], seq_count), 'seq', split_axis...  7.26 us
    all_to_all x1, starting transfers between devices, dense_local(): lax.all_to_all(returns, 'seq', split_axis=0, concat_axis=0, tiled=True)  5.19 us
    pallas_call x1, Pallas kernels, head_grads(): pl.pallas_call(head_grad_kernel, out_shape=[pltpu.HBM((2 * rows + 2 * HD,...  4.63 us
    pallas_call x1, Pallas kernels, backward(): pl.pallas_call(functools.partial(backward_kernel, members, 4 * here, scal...  4.26 us
    pallas_call x1, Pallas kernels, weight_parts(): pl.pallas_call(functools.partial(weight_part_kernel, docs), out_shape=[st...  2.57 us
    pallas_call x1, Pallas kernels, project(): pl.pallas_call(project_kernel, out_shape=[struct(rows, width), struct(16,...  2.55 us
  transfers between devices with their start and end apart: 20, of which 11 were waited for; matrix products, arithmetic and copies ran while one was open for 0% of the time, Pallas kernels for 22%

profile of v4, /device:TPU:0, one launch (start us, length us, event | category | flops | bytes accessed | tf_op | source)
XLA Modules:
  0.0 87.1 jit_solution(5681641697422329940)
XLA Ops:
  0.6 2.1 %pack_keys.1 = bf16[8,512,128]{2,1,0:T(8,128)(2,1)} custom-call(bf16[128,1024]{1,0:T(8,128)(2,1)} %bitcast.12, bf16[128,1024]{1,0:T(8,128)(2,1)} %bitcast.13), custom_call_target="tpu_custom_call" | custom-call | flops 1 | bytes 1 | tf_op jit(solution)/shard_map/pack_keys/pallas_call | solution.py:98
  2.7 7.3 %all-to-all-start = ((bf16[8,512,128]{2,1,0:T(8,128)(2,1)}), bf16[8,512,128]{2,1,0:T(8,128)(2,1)S(1)}, u32[]{:S(2)}, u32[]{:S(2)}) async-start(bf16[8,512,128]{2,1,0:T(8,128)(2,1)} %pack_keys.1), calls=%async_computation | async-start | bytes 2097152 | tf_op jit(solution)/shard_map/all_to_all | solution.py:489
  10.0 4.6 %head_grads.1 = (bf16[512,128]{1,0:T(8,128)(2,1)}, bf16[512,128]{1,0:T(8,128)(2,1)}, bf16[512,128]{1,0:T(8,128)(2,1)}, bf16[512,128]{1,0:T(8,128)(2,1)}, bf16[12...) custom-call(bf16[128,1024]{1,0:T(8,128)(2,1)} %bitcast.11, bf16[128,2048]{1,0:T(8,128)(2,1)} %bitcast.10, ...), custom_call_target="tpu_custom_call" | custom-call | flops 1 | bytes 1 | tf_op jit(solution)/shard_map/head_grads/pallas_call | solution.py:141
  14.6 2.1 %collective-permute-start = (bf16[512,128]{1,0:T(8,128)(2,1)}, bf16[512,128]{1,0:T(8,128)(2,1)S(1)}, u32[]{:S(2)}, u32[]{:S(2)}) collective-permute-start(bf16[512,128]{1,0:T(8,128)(2,1)} %get-tuple-element.42), channel_id=1, source_target_pairs={{0,4},{4,0},{8,12},{12,8},{16,20},{20,16},{24,28},{28,24},{1,5},{5... | collective-permute-start | bytes 393224 | tf_op jit(solution)/shard_map/ppermute | solution.py:54
  18.7 4.4 %collective-permute-done.refs_1_ = bf16[512,128]{1,0:T(8,128)(2,1)S(1)} collective-permute-done((bf16[512,128]{1,0:T(8,128)(2,1)}, bf16[512,128]{1,0:T(8,128)(2,1)S(1)}, u32[]{:S(2)}, u32[]{:S(2)}) %collective-permute-start) | collective-permute-done | bytes 131104 | tf_op jit(solution)/shard_map/ppermute | solution.py:54
  23.1 2.0 %collective-permute-start.9 = (bf16[128,1024]{1,0:T(8,128)(2,1)}, bf16[128,1024]{1,0:T(8,128)(2,1)S(1)}, u32[]{:S(2)}, u32[]{:S(2)}) collective-permute-start(bf16[128,1024]{1,0:T(8,128)(2,1)} %get-tuple-element.61), channel_id=1, source_target_pairs={{0,12},{4,8},{8,4},{12,0},{16,28},{20,24},{24,20},{28,16},{1,13},{... | collective-permute-start | bytes 786440 | tf_op jit(solution)/shard_map/ppermute | solution.py:54
  25.1 1.5 %collective-permute-start.8 = (bf16[128,1024]{1,0:T(8,128)(2,1)}, bf16[128,1024]{1,0:T(8,128)(2,1)S(1)}, u32[]{:S(2)}, u32[]{:S(2)}) collective-permute-start(bf16[128,1024]{1,0:T(8,128)(2,1)} %get-tuple-element.60.refs_0_), channel_id=1, source_target_pairs={{0,8},{4,12},{8,0},{12,4},{16,24},{20,28},{24,16},{28,20},{1,9},{5... | collective-permute-start | bytes 786440 | tf_op jit(solution)/shard_map/ppermute | solution.py:54
  26.6 4.6 %collective-permute-done.1.refs_2_ = bf16[512,128]{1,0:T(8,128)(2,1)S(1)} collective-permute-done((bf16[512,128]{1,0:T(8,128)(2,1)}, bf16[512,128]{1,0:T(8,128)(2,1)S(1)}, u32[]{:S(2)}, u32[]{:S(2)}) %collective-permute-start.1) | collective-permute-done | bytes 131104 | tf_op jit(solution)/shard_map/ppermute | solution.py:54
  31.1 5.7 %collective-permute-done.2.refs_3_ = bf16[512,128]{1,0:T(8,128)(2,1)S(1)} collective-permute-done((bf16[512,128]{1,0:T(8,128)(2,1)}, bf16[512,128]{1,0:T(8,128)(2,1)S(1)}, u32[]{:S(2)}, u32[]{:S(2)}) %collective-permute-start.2) | collective-permute-done | bytes 131104 | tf_op jit(solution)/shard_map/ppermute | solution.py:54
  37.8 2.1 %attend.1 = (bf16[1024,128]{1,0:T(8,128)(2,1)S(1)}, f32[2,512]{1,0:T(2,128)S(1)}) custom-call(f32[16,1024]{1,0:T(8,128)S(1)} %reshape.14.bias_ref, bf16[8,512,128]{2,1,0:T(8,128)(2,1)S(1)} %all-to-all-done.pairs, bf16[512,128]{1,0:T(8,128)(2,1)S(1)} %copy-done.1, bf16[512,128]{1,0:T(8,128)(2,1)S(1)} %collective-permute-done.refs_1_, ...), custom_call_target="tpu_custom_call" | custom-call | flops 1 | bytes 1 | tf_op jit(solution)/shard_map/attend/pallas_call | solution.py:210
  40.4 4.3 %attend_back.1 = (bf16[8,512,128]{2,1,0:T(8,128)(2,1)}, bf16[512,128]{1,0:T(8,128)(2,1)}, bf16[512,128]{1,0:T(8,128)(2,1)}, bf16[512,128]{1,0:T(8,128)(2,1)}, bf16[512,128]{1,0:T(8,128)(2,1)}) custom-call(f32[16,1024]{1,0:T(8,128)S(1)} %reshape.14.bias_ref, f32[2,512]{1,0:T(2,128)S(1)} %get-tuple-element.46.norm_ref, ...), custom_call_target="tpu_custom_call" | custom-call | flops 1 | bytes 1 | tf_op jit(solution)/shard_map/attend_back/pallas_call | solution.py:261
  44.7 5.2 %all-to-all-start.1 = ((bf16[8,512,128]{2,1,0:T(8,128)(2,1)}), bf16[8,512,128]{2,1,0:T(8,128)(2,1)S(1)}, u32[]{:S(2)}, u32[]{:S(2)}) async-start(bf16[8,512,128]{2,1,0:T(8,128)(2,1)} %get-tuple-element.54), calls=%async_computation.1 | async-start | bytes 2097152 | tf_op jit(solution)/shard_map/all_to_all | solution.py:503
  50.7 2.6 %weight_part.1 = (f32[1024,256]{1,0:T(8,128)S(1)}, bf16[1024,256]{1,0:T(8,128)(2,1)S(1)}) custom-call(bf16[1024,128]{1,0:T(8,128)(2,1)S(1)} %get-tuple-element.59.near, bf16[1024,128]{1,0:T(8,128)(2,1)S(1)} %collective-permute-done.6.near_pair, bf16[128,1024]{1,0:T(8,128)(2,1)} %get-tuple-element.60.refs_0_, bf16[128,1024]{1,0:T(8,128)(2,1)} %copy-done.6, ...), custom_call_target="tpu_custom_call" | custom-call | flops 1 | bytes 1 | tf_op jit(solution)/shard_map/weight_part/pallas_call | solution.py:378
  53.4 1.9 %collective-permute-done.10.other = bf16[1024,256]{1,0:T(8,128)(2,1)S(1)} collective-permute-done((bf16[1024,256]{1,0:T(8,128)(2,1)S(1)}, bf16[1024,256]{1,0:T(8,128)(2,1)S(1)}, u32[]{:S(2)}, u32[]{:S(2)}) %collective-permute-start.10) | collective-permute-done | bytes 524320 | tf_op jit(solution)/shard_map/ppermute | solution.py:54
  55.4 1.6 %collective-permute-start.11 = (bf16[512,256]{1,0:T(8,128)(2,1)S(1)}, bf16[512,256]{1,0:T(8,128)(2,1)S(1)}, u32[]{:S(2)}, u32[]{:S(2)}) collective-permute-start(bf16[512,256]{1,0:T(8,128)(2,1)S(1)} %get-tuple-element.65), channel_id=1, source_target_pairs={{0,2},{1,3},{2,0},{3,1},{4,6},{5,7},{6,4},{7,5},{8,10},{9,11},{10,... | collective-permute-start | bytes 786440 | tf_op jit(solution)/shard_map/ppermute | solution.py:54
  57.0 2.0 %collective-permute-start.3 = (bf16[512,128]{1,0:T(8,128)(2,1)S(1)}, bf16[512,128]{1,0:T(8,128)(2,1)S(1)}, u32[]{:S(2)}, u32[]{:S(2)}) collective-permute-start(bf16[512,128]{1,0:T(8,128)(2,1)S(1)} %copy-done.11), channel_id=1, source_target_pairs={{0,4},{4,0},{8,12},{12,8},{16,20},{20,16},{24,28},{28,24},{1,5},{5... | collective-permute-start | bytes 393224 | tf_op jit(solution)/shard_map/ppermute | solution.py:54
  60.5 3.3 %collective-permute-done.11.other = bf16[512,256]{1,0:T(8,128)(2,1)S(1)} collective-permute-done((bf16[512,256]{1,0:T(8,128)(2,1)S(1)}, bf16[512,256]{1,0:T(8,128)(2,1)S(1)}, u32[]{:S(2)}, u32[]{:S(2)}) %collective-permute-start.11) | collective-permute-done | bytes 262176 | tf_op jit(solution)/shard_map/ppermute | solution.py:54
  63.8 4.3 %collective-permute-start.12 = (bf16[128,256]{1,0:T(8,128)(2,1)S(1)}, bf16[128,256]{1,0:T(8,128)(2,1)S(1)}, u32[]{:S(2)}, u32[]{:S(2)}) collective-permute-start(bf16[128,256]{1,0:T(8,128)(2,1)S(1)} %get-tuple-element.67), channel_id=1, source_target_pairs={{0,16},{4,20},{8,24},{12,28},{16,0},{20,4},{24,8},{28,12},{1,17},{... | collective-permute-start | bytes 196616 | tf_op jit(solution)/shard_map/ppermute | solution.py:54
  68.3 2.0 %collective-permute-start.14 = (bf16[128,256]{1,0:T(8,128)(2,1)S(1)}, bf16[128,256]{1,0:T(8,128)(2,1)S(1)}, u32[]{:S(2)}, u32[]{:S(2)}) collective-permute-start(bf16[128,256]{1,0:T(8,128)(2,1)S(1)} %get-tuple-element.69), channel_id=1, source_target_pairs={{0,20},{4,16},{8,28},{12,24},{16,4},{20,0},{24,12},{28,8},{1,21},{... | collective-permute-start | bytes 196616 | tf_op jit(solution)/shard_map/ppermute | solution.py:54
  70.6 1.8 %collective-permute-done.5.refs_3_ = bf16[512,128]{1,0:T(8,128)(2,1)S(1)} collective-permute-done((bf16[512,128]{1,0:T(8,128)(2,1)S(1)}, bf16[512,128]{1,0:T(8,128)(2,1)S(1)}, u32[]{:S(2)}, u32[]{:S(2)}) %collective-permute-start.5) | collective-permute-done | bytes 131104 | tf_op jit(solution)/shard_map/ppermute | solution.py:54
  74.3 2.5 %project.1 = (bf16[128,2048]{1,0:T(8,128)(2,1)}, bf16[16,128]{1,0:T(8,128)(2,1)S(1)}) custom-call(bf16[128,1024]{1,0:T(8,128)(2,1)S(1)} %join_heads.1.attended, bf16[1024,2048]{1,0:T(8,128)(2,1)S(1)} %copy-done), custom_call_target="tpu_custom_call" | custom-call | flops 1 | bytes 1 | tf_op jit(solution)/shard_map/project/pallas_call | solution.py:336
  76.8 1.5 %collective-permute-done.12.refs_1_ = bf16[128,256]{1,0:T(8,128)(2,1)S(1)} collective-permute-done((bf16[128,256]{1,0:T(8,128)(2,1)S(1)}, bf16[128,256]{1,0:T(8,128)(2,1)S(1)}, u32[]{:S(2)}, u32[]{:S(2)}) %collective-permute-start.12) | collective-permute-done | bytes 65568 | tf_op jit(solution)/shard_map/ppermute | solution.py:54
  79.7 1.6 %collective-permute-start.15 = (bf16[256,256]{1,0:T(8,128)(2,1)S(1)}, bf16[256,256]{1,0:T(8,128)(2,1)S(1)}, u32[]{:S(2)}, u32[]{:S(2)}) collective-permute-start(bf16[256,256]{1,0:T(8,128)(2,1)S(1)} %weight_scale.1.refs_0_), channel_id=1, source_target_pairs={{0,2},{1,3},{2,0},{3,1},{4,6},{5,7},{6,4},{7,5},{8,10},{9,11},{10,... | collective-permute-start | bytes 393224 | tf_op jit(solution)/shard_map/ppermute | solution.py:54
  81.3 2.1 %unpack_grads.1 = (bf16[128,1024]{1,0:T(8,128)(2,1)}, bf16[128,1024]{1,0:T(8,128)(2,1)}, bf16[128,1024]{1,0:T(8,128)(2,1)}, bf16[16,128]{1,0:T(8,128)(2,1)S(1)}) custom-call(bf16[8,512,128]{2,1,0:T(8,128)(2,1)S(1)} %all-to-all-done.1.returned, bf16[512,128]{1,0:T(8,128)(2,1)} %get-tuple-element.48.refs_0_, bf16[512,128]{1,0:T(8,128)(2,1)} %copy-done.2, ...), custom_call_target="tpu_custom_call" | custom-call | flops 1 | bytes 3145728 | tf_op jit(solution)/shard_map/unpack_grads/pallas_call | solution.py:294
  (58 shorter events, 13.4 us)
Async XLA Ops:
  0.6 17.6 %copy-start.8 = (s32[16,8]{0,1:T(8,128)S(1)}, s32[16,8]{0,1:T(8,128)}, u32[]{:S(2)}) copy-start(s32[16,8]{0,1:T(8,128)} %param.11) | copy-start | bytes 1540
  2.7 34.1 %all-to-all-start = ((bf16[8,512,128]{2,1,0:T(8,128)(2,1)}), bf16[8,512,128]{2,1,0:T(8,128)(2,1)S(1)}, u32[]{:S(2)}, u32[]{:S(2)}) async-start(bf16[8,512,128]{2,1,0:T(8,128)(2,1)} %pack_keys.1), calls=%async_computation | async-start | bytes 2097152 | tf_op jit(solution)/shard_map/all_to_all | solution.py:489
  14.6 8.4 %collective-permute-start = (bf16[512,128]{1,0:T(8,128)(2,1)}, bf16[512,128]{1,0:T(8,128)(2,1)S(1)}, u32[]{:S(2)}, u32[]{:S(2)}) collective-permute-start(bf16[512,128]{1,0:T(8,128)(2,1)} %get-tuple-element.42), channel_id=1, source_target_pairs={{0,4},{4,0},{8,12},{12,8},{16,20},{20,16},{24,28},{28,24},{1,5},{5... | collective-permute-start | bytes 393224 | tf_op jit(solution)/shard_map/ppermute | solution.py:54
  16.7 14.4 %collective-permute-start.1 = (bf16[512,128]{1,0:T(8,128)(2,1)}, bf16[512,128]{1,0:T(8,128)(2,1)S(1)}, u32[]{:S(2)}, u32[]{:S(2)}) collective-permute-start(bf16[512,128]{1,0:T(8,128)(2,1)} %get-tuple-element.44), channel_id=1, source_target_pairs={{0,8},{4,12},{8,0},{12,4},{16,24},{20,28},{24,16},{28,20},{1,9},{5... | collective-permute-start | bytes 393224 | tf_op jit(solution)/shard_map/ppermute | solution.py:54
  18.2 18.7 %collective-permute-start.2 = (bf16[512,128]{1,0:T(8,128)(2,1)}, bf16[512,128]{1,0:T(8,128)(2,1)S(1)}, u32[]{:S(2)}, u32[]{:S(2)}) collective-permute-start(bf16[512,128]{1,0:T(8,128)(2,1)} %get-tuple-element.45), channel_id=1, source_target_pairs={{0,12},{4,8},{8,4},{12,0},{16,28},{20,24},{24,20},{28,16},{1,13},{... | collective-permute-start | bytes 393224 | tf_op jit(solution)/shard_map/ppermute | solution.py:54
  23.1 26.8 %collective-permute-start.9 = (bf16[128,1024]{1,0:T(8,128)(2,1)}, bf16[128,1024]{1,0:T(8,128)(2,1)S(1)}, u32[]{:S(2)}, u32[]{:S(2)}) collective-permute-start(bf16[128,1024]{1,0:T(8,128)(2,1)} %get-tuple-element.61), channel_id=1, source_target_pairs={{0,12},{4,8},{8,4},{12,0},{16,28},{20,24},{24,20},{28,16},{1,13},{... | collective-permute-start | bytes 786440 | tf_op jit(solution)/shard_map/ppermute | solution.py:54
  25.1 24.8 %collective-permute-start.7 = (bf16[128,1024]{1,0:T(8,128)(2,1)}, bf16[128,1024]{1,0:T(8,128)(2,1)S(1)}, u32[]{:S(2)}, u32[]{:S(2)}) collective-permute-start(bf16[128,1024]{1,0:T(8,128)(2,1)} %get-tuple-element.61), channel_id=1, source_target_pairs={{0,4},{4,0},{8,12},{12,8},{16,20},{20,16},{24,28},{28,24},{1,5},{5... | collective-permute-start | bytes 786440 | tf_op jit(solution)/shard_map/ppermute | solution.py:54
  25.1 24.8 %collective-permute-start.8 = (bf16[128,1024]{1,0:T(8,128)(2,1)}, bf16[128,1024]{1,0:T(8,128)(2,1)S(1)}, u32[]{:S(2)}, u32[]{:S(2)}) collective-permute-start(bf16[128,1024]{1,0:T(8,128)(2,1)} %get-tuple-element.60.refs_0_), channel_id=1, source_target_pairs={{0,8},{4,12},{8,0},{12,4},{16,24},{20,28},{24,16},{28,20},{1,9},{5... | collective-permute-start | bytes 786440 | tf_op jit(solution)/shard_map/ppermute | solution.py:54
  39.9 10.0 %collective-permute-start.6 = (bf16[1024,128]{1,0:T(8,128)(2,1)S(1)}, bf16[1024,128]{1,0:T(8,128)(2,1)S(1)}, u32[]{:S(2)}, u32[]{:S(2)}) collective-permute-start(bf16[1024,128]{1,0:T(8,128)(2,1)S(1)} %get-tuple-element.59.near), channel_id=1, source_target_pairs={{0,4},{4,0},{8,12},{12,8},{16,20},{20,16},{24,28},{28,24},{1,5},{5... | collective-permute-start | bytes 786440 | tf_op jit(solution)/shard_map/ppermute | solution.py:54
  44.6 14.3 %copy-start.10 = (bf16[512,128]{1,0:T(8,128)(2,1)S(1)}, bf16[512,128]{1,0:T(8,128)(2,1)}, u32[]{:S(2)}) copy-start(bf16[512,128]{1,0:T(8,128)(2,1)} %get-tuple-element.50) | copy-start | bytes 393220
  44.6 15.8 %copy-start.9 = (bf16[512,128]{1,0:T(8,128)(2,1)S(1)}, bf16[512,128]{1,0:T(8,128)(2,1)}, u32[]{:S(2)}) copy-start(bf16[512,128]{1,0:T(8,128)(2,1)} %get-tuple-element.51) | copy-start | bytes 393220
  44.7 36.6 %all-to-all-start.1 = ((bf16[8,512,128]{2,1,0:T(8,128)(2,1)}), bf16[8,512,128]{2,1,0:T(8,128)(2,1)S(1)}, u32[]{:S(2)}, u32[]{:S(2)}) async-start(bf16[8,512,128]{2,1,0:T(8,128)(2,1)} %get-tuple-element.54), calls=%async_computation.1 | async-start | bytes 2097152 | tf_op jit(solution)/shard_map/all_to_all | solution.py:503
  49.8 24.4 %copy-start = (bf16[1024,2048]{1,0:T(8,128)(2,1)S(1)}, bf16[1024,2048]{1,0:T(8,128)(2,1)}, u32[]{:S(2)}) copy-start(bf16[1024,2048]{1,0:T(8,128)(2,1)} %weight_ref.3) | copy-start | bytes 12582916
  53.3 2.0 %collective-permute-start.10 = (bf16[1024,256]{1,0:T(8,128)(2,1)S(1)}, bf16[1024,256]{1,0:T(8,128)(2,1)S(1)}, u32[]{:S(2)}, u32[]{:S(2)}) collective-permute-start(bf16[1024,256]{1,0:T(8,128)(2,1)S(1)} %get-tuple-element.63), channel_id=1, source_target_pairs={{0,1},{1,0},{2,3},{3,2},{4,5},{5,4},{6,7},{7,6},{8,9},{9,8},{10,11... | collective-permute-start | bytes 1572872 | tf_op jit(solution)/shard_map/ppermute | solution.py:54
  55.4 8.4 %collective-permute-start.11 = (bf16[512,256]{1,0:T(8,128)(2,1)S(1)}, bf16[512,256]{1,0:T(8,128)(2,1)S(1)}, u32[]{:S(2)}, u32[]{:S(2)}) collective-permute-start(bf16[512,256]{1,0:T(8,128)(2,1)S(1)} %get-tuple-element.65), channel_id=1, source_target_pairs={{0,2},{1,3},{2,0},{3,1},{4,6},{5,7},{6,4},{7,5},{8,10},{9,11},{10,... | collective-permute-start | bytes 786440 | tf_op jit(solution)/shard_map/ppermute | solution.py:54
  57.0 11.3 %collective-permute-start.3 = (bf16[512,128]{1,0:T(8,128)(2,1)S(1)}, bf16[512,128]{1,0:T(8,128)(2,1)S(1)}, u32[]{:S(2)}, u32[]{:S(2)}) collective-permute-start(bf16[512,128]{1,0:T(8,128)(2,1)S(1)} %copy-done.11), channel_id=1, source_target_pairs={{0,4},{4,0},{8,12},{12,8},{16,20},{20,16},{24,28},{28,24},{1,5},{5... | collective-permute-start | bytes 393224 | tf_op jit(solution)/shard_map/ppermute | solution.py:54
  59.0 11.6 %collective-permute-start.4 = (bf16[512,128]{1,0:T(8,128)(2,1)S(1)}, bf16[512,128]{1,0:T(8,128)(2,1)S(1)}, u32[]{:S(2)}, u32[]{:S(2)}) collective-permute-start(bf16[512,128]{1,0:T(8,128)(2,1)S(1)} %copy-done.10), channel_id=1, source_target_pairs={{0,8},{4,12},{8,0},{12,4},{16,24},{20,28},{24,16},{28,20},{1,9},{5... | collective-permute-start | bytes 393224 | tf_op jit(solution)/shard_map/ppermute | solution.py:54
  60.5 12.0 %collective-permute-start.5 = (bf16[512,128]{1,0:T(8,128)(2,1)S(1)}, bf16[512,128]{1,0:T(8,128)(2,1)S(1)}, u32[]{:S(2)}, u32[]{:S(2)}) collective-permute-start(bf16[512,128]{1,0:T(8,128)(2,1)S(1)} %copy-done.9), channel_id=1, source_target_pairs={{0,12},{4,8},{8,4},{12,0},{16,28},{20,24},{24,20},{28,16},{1,13},{... | collective-permute-start | bytes 393224 | tf_op jit(solution)/shard_map/ppermute | solution.py:54
  63.8 14.5 %collective-permute-start.12 = (bf16[128,256]{1,0:T(8,128)(2,1)S(1)}, bf16[128,256]{1,0:T(8,128)(2,1)S(1)}, u32[]{:S(2)}, u32[]{:S(2)}) collective-permute-start(bf16[128,256]{1,0:T(8,128)(2,1)S(1)} %get-tuple-element.67), channel_id=1, source_target_pairs={{0,16},{4,20},{8,24},{12,28},{16,0},{20,4},{24,8},{28,12},{1,17},{... | collective-permute-start | bytes 196616 | tf_op jit(solution)/shard_map/ppermute | solution.py:54
  68.1 10.2 %collective-permute-start.13 = (bf16[128,256]{1,0:T(8,128)(2,1)S(1)}, bf16[128,256]{1,0:T(8,128)(2,1)S(1)}, u32[]{:S(2)}, u32[]{:S(2)}) collective-permute-start(bf16[128,256]{1,0:T(8,128)(2,1)S(1)} %get-tuple-element.68), channel_id=1, source_target_pairs={{0,4},{4,0},{8,12},{12,8},{16,20},{20,16},{24,28},{28,24},{1,5},{5... | collective-permute-start | bytes 196616 | tf_op jit(solution)/shard_map/ppermute | solution.py:54
  68.3 11.4 %collective-permute-start.14 = (bf16[128,256]{1,0:T(8,128)(2,1)S(1)}, bf16[128,256]{1,0:T(8,128)(2,1)S(1)}, u32[]{:S(2)}, u32[]{:S(2)}) collective-permute-start(bf16[128,256]{1,0:T(8,128)(2,1)S(1)} %get-tuple-element.69), channel_id=1, source_target_pairs={{0,20},{4,16},{8,28},{12,24},{16,4},{20,0},{24,12},{28,8},{1,21},{... | collective-permute-start | bytes 196616 | tf_op jit(solution)/shard_map/ppermute | solution.py:54
  79.7 5.0 %collective-permute-start.15 = (bf16[256,256]{1,0:T(8,128)(2,1)S(1)}, bf16[256,256]{1,0:T(8,128)(2,1)S(1)}, u32[]{:S(2)}, u32[]{:S(2)}) collective-permute-start(bf16[256,256]{1,0:T(8,128)(2,1)S(1)} %weight_scale.1.refs_0_), channel_id=1, source_target_pairs={{0,2},{1,3},{2,0},{3,1},{4,6},{5,7},{6,4},{7,5},{8,10},{9,11},{10,... | collective-permute-start | bytes 393224 | tf_op jit(solution)/shard_map/ppermute | solution.py:54
  81.3 3.5 %collective-permute-start.16 = (bf16[256,256]{1,0:T(8,128)(2,1)S(1)}, bf16[256,256]{1,0:T(8,128)(2,1)S(1)}, u32[]{:S(2)}, u32[]{:S(2)}) collective-permute-start(bf16[256,256]{1,0:T(8,128)(2,1)S(1)} %weight_scale.1.refs_0_), channel_id=1, source_target_pairs={{0,1},{1,0},{2,3},{3,2},{4,5},{5,4},{6,7},{7,6},{8,9},{9,8},{10,11... | collective-permute-start | bytes 393224 | tf_op jit(solution)/shard_map/ppermute | solution.py:54
  84.7 1.3 %collective-permute-start.17 = (bf16[256,256]{1,0:T(8,128)(2,1)S(1)}, bf16[256,256]{1,0:T(8,128)(2,1)S(1)}, u32[]{:S(2)}, u32[]{:S(2)}) collective-permute-start(bf16[256,256]{1,0:T(8,128)(2,1)S(1)} %collective-permute-done.15.refs_2_), channel_id=1, source_target_pairs={{0,1},{1,0},{2,3},{3,2},{4,5},{5,4},{6,7},{7,6},{8,9},{9,8},{10,11... | collective-permute-start | bytes 393224 | tf_op jit(solution)/shard_map/ppermute | solution.py:54
  (8 other events, 22.2 us)

commit v5 on v4

--- a/solution.py
+++ b/solution.py
@@ -17,11 +17,9 @@
 VMEM_SPEC = pl.BlockSpec()
 NT = (((1,), (1,)), ((), ()))
 NN = (((1,), (0,)), ((), ()))
-TN = (((0,), (0,)), ((), ()))
 WIDE = 58
 HEAD_MIB = 58
 PROJECT_FLOPS = 1
-JOIN_FLOPS = 2 << 30
 SCALE_FLOPS = 8 << 30
 HEADS_FLOPS = 1
 
@@ -351,8 +349,8 @@
     )(attended, out_weight)
 
 
-def weight_part_kernel(docs, near, near_pair, *refs):
-    grads, (own, send) = refs[:-2], refs[-2:]
+def weight_part_kernel(masks, docs, near, near_pair, *refs):
+    grads, out = refs[:-1], refs[-1]
     members = len(grads)
     rows = grads[0].shape[0]
     width = grads[0].shape[1] // docs
@@ -362,25 +360,22 @@
             places = [span(slot * members + member(mask), rows) for mask in range(members)]
             lefts.append(jnp.concatenate([source[place] for place in places], axis=0))
     left = jnp.concatenate(lefts, axis=1).T
-    for mask in range(docs):
+    for index, mask in enumerate(masks):
         columns = span(lax.axis_index("rep") ^ mask, width)
         right = jnp.concatenate([grad[:, columns] for grad in grads], axis=0)
-        place = pl.ds(mask // 2 * left.shape[0], left.shape[0])
-        if mask % 2:
-            send[place] = dot(left, right, NN).astype(jnp.bfloat16)
-        else:
-            own[place] = dot(left, right, NN)
-
-
-def weight_parts(near, near_pair, grads, docs):
+        place = pl.ds(index * left.shape[0], left.shape[0])
+        out[place] = dot(left, right, NN).astype(out.dtype)
+
+
+def weight_part(near, near_pair, grads, docs, first, dtype):
+    masks = range(first, docs, 2)
     width = grads[0].shape[1] // docs
-    rows = docs // 2 * 4 * HD
-    return pl.pallas_call(
-        functools.partial(weight_part_kernel, docs),
-        out_shape=[struct(rows, width, dtype=jnp.float32), struct(rows, width)],
+    return pl.pallas_call(
+        functools.partial(weight_part_kernel, masks, docs),
+        out_shape=struct(len(masks) * 4 * HD, width, dtype=dtype),
         in_specs=[VMEM_SPEC] * (2 + len(grads)),
-        out_specs=[VMEM_SPEC] * 2,
-        compiler_params=params(30),
+        out_specs=VMEM_SPEC,
+        compiler_params=params(24),
         cost_estimate=cost(),
         name="weight_part",
     )(near, near_pair, *map(in_hbm, grads))
@@ -426,48 +421,45 @@
     )(own, other)
 
 
-def weight_scale_kernel(factor, own, across, pair, diagonal, total):
-    rows = own.shape[0]
-    total[:rows] = ((own[...] + across[...].astype(jnp.float32)) * factor).astype(jnp.bfloat16)
-    other = pair[...].astype(jnp.float32) + diagonal[...].astype(jnp.float32)
-    total[rows:] = (other * factor).astype(jnp.bfloat16)
-
-
-def weight_scale(anchor, own, across, pair, diagonal, factor):
-    rows, width = own.shape
+def weight_scale_kernel(factor, first, second, total):
+    wide = first[...].astype(jnp.float32) + second[...].astype(jnp.float32)
+    total[...] = (wide * factor).astype(jnp.bfloat16)
+
+
+def weight_scale(anchor, first, second, factor, flops):
     return pl.pallas_call(
         anchored(functools.partial(weight_scale_kernel, factor)),
-        out_shape=struct(2 * rows, width),
-        in_specs=[ANY_SPEC] + [VMEM_SPEC] * 4,
+        out_shape=struct(*first.shape),
+        in_specs=[ANY_SPEC] + [VMEM_SPEC] * 2,
         out_specs=VMEM_SPEC,
         compiler_params=params(8),
-        cost_estimate=cost(SCALE_FLOPS),
+        cost_estimate=cost(flops),
         name="weight_scale",
-    )(anchor, own, across, pair, diagonal)
+    )(anchor, first, second)
 
 
 def weight_join_kernel(*refs):
     parts, total = refs[:-1], refs[-1]
-    rows, width = total.shape[0], parts[0].shape[1]
+    width = parts[0].shape[1]
+    count = len(parts) // 2
     side = lax.axis_index("seq") & 1
-    for mask, part in enumerate(parts):
-        share = lax.axis_index("rep") ^ mask
-        for index, place in ((0, side), (1, 1 - side)):
-            block = part[index * rows : (index + 1) * rows]
-            total[:, span(place * len(parts) + share, width)] = block.astype(jnp.float32)
-
-
-def weight_join(anchor, pairs):
-    rows, width = HD, pairs[0].shape[1]
+    for index, part in enumerate(parts):
+        share = lax.axis_index("rep") ^ (index % count)
+        place = side if index < count else 1 - side
+        total[:, span(place * count + share, width)] = part[...].astype(jnp.float32)
+
+
+def weight_join(anchor, parts):
+    rows, width = parts[0].shape
     return pl.pallas_call(
         anchored(weight_join_kernel),
-        out_shape=struct(rows, 2 * width * len(pairs), dtype=jnp.float32),
-        in_specs=[ANY_SPEC] + [VMEM_SPEC] * len(pairs),
+        out_shape=struct(rows, width * len(parts), dtype=jnp.float32),
+        in_specs=[ANY_SPEC] + [VMEM_SPEC] * len(parts),
         out_specs=VMEM_SPEC,
         compiler_params=params(8),
         cost_estimate=cost(),
         name="weight_join",
-    )(anchor, *pairs)
+    )(anchor, *parts)
 
 
 def dense_bias(pattern, tokens):
@@ -492,9 +484,12 @@
     *sends, grad_mine, grad_theirs = head_grads(query_in[0], grad_out[0], out_weight, members)
     parts = [sends[0]] + [swap(sends[mask], "seq", mask) for mask in range(1, members)]
     grad_mine, grad_theirs, *parts[1:2] = after(grad_mine, grad_theirs, *parts[1:2])
-    half_grads = [grad_mine] + [
-        swap(grad_theirs if mask & 1 else grad_mine, "seq", mask) for mask in range(1, members)
-    ]
+    half_grads = {1: swap(grad_theirs, "seq", 1)}
+    grad_mine, grad_theirs, *parts[2:3] = after(grad_mine, grad_theirs, *parts[2:3])
+    half_grads |= {
+        mask: swap(grad_theirs if mask & 1 else grad_mine, "seq", mask) for mask in range(2, members)
+    }
+    half_grads = [grad_mine] + [half_grads[mask] for mask in range(1, members)]
 
     near, norm = forward(bias, pairs, parts, scale)
     near_pair = swap(near, "seq", 1)
@@ -503,7 +498,8 @@
     returned = lax.all_to_all(returns, "seq", split_axis=0, concat_axis=0, tiled=True)
     parts = [sends[0]] + [swap(sends[mask], "seq", mask) for mask in range(1, members)]
 
-    own, send = weight_parts(near, near_pair, half_grads, rep_count)
+    send = weight_part(near, near_pair, half_grads, rep_count, 1, jnp.bfloat16)
+    own = weight_part(near, near_pair, half_grads, rep_count, 0, jnp.float32)
     bit = 1
     while 2 * bit < rep_count:
         own, send = weight_fold(own, swap(send, "rep", bit))
@@ -512,13 +508,16 @@
     arrived = [swap(block, "seq", mask) for block, mask in zip(sends, (members, 1, members + 1))]
     mixed_out, token = project(join_heads(parts), out_weight)
     factor = 1.0 / math.sqrt(rep_count * tokens)
-    pair = weight_scale(token, own, *arrived, factor)
+    mine = weight_scale(token, own, arrived[0], factor, 1)
+    other = weight_scale(token, arrived[1], arrived[2], factor, SCALE_FLOPS)
     query_grad, key_grad, value_grad, token = unpack(
         returned, parts, tokens_here, query_in.shape[2]
     )
-    across, token = after(swap(pair, "rep", 2), token)
-    quarters = [pair, swap(pair, "rep", 1), across, swap(across, "rep", 1)]
-    weight_grad = weight_join(token, quarters)
+    shares = []
+    for share in (mine, other):
+        across, token = after(swap(share, "rep", 2), token)
+        shares += [share, swap(share, "rep", 1), across, swap(across, "rep", 1)]
+    weight_grad = weight_join(token, shares)
     return (mixed_out[None], query_grad[None], key_grad[None], value_grad[None], weight_grad)
 
 

time: 87.5 us -> 87 us (level)
  waiting for transfers between devices: 27.5 us -> 22.3 us
  starting transfers between devices: 33.3 us -> 36.7 us
  Pallas kernels: 22.7 us -> 24.1 us
    ppermute x18 -> x21, waiting for transfers between devices: 27.5 us -> 21.4 us  [swap(): lax.ppermute(array, axis, [(i, i ^ mask) for i in range(lax.axis_size(axi...]
    ppermute x18 -> x21, starting transfers between devices: 20.8 us -> 24.4 us  [swap(): lax.ppermute(array, axis, [(i, i ^ mask) for i in range(lax.axis_size(axi...]
    pallas_call x2 -> x3, Pallas kernels: 3.62 us -> 5.02 us  [the longest x2 3.98 us: weight_part(): pl.pallas_call(functools.partial(weight_part_kernel, masks, docs), out_sh...]
    all_to_all x1, waiting for transfers between devices: 0.01 us -> 0.94 us  [dense_local(): lax.all_to_all(pack(key_in[0], value_in[0], seq_count), 'seq', split_axis...]
  transfers between devices with their start and end apart: 20 -> 23, of which waited for: 11 -> 11; matrix products, arithmetic and copies ran while one was open for 0% -> 1% of each run, Pallas kernels for 22% -> 24%
where the time goes in v5:
time: 87 us; the launch traced here: 86.7 us
  starting transfers between devices  36.7 us (42%)
  Pallas kernels  24.1 us (28%)
  waiting for transfers between devices  22.3 us (26%)
  local copies, waits for them, and re-layouts  2.72 us (3%)
    ppermute x21, starting transfers between devices, swap(): lax.ppermute(array, axis, [(i, i ^ mask) for i in range(lax.axis_size(axi...  24.4 us
    ppermute x21, waiting for transfers between devices, swap(): lax.ppermute(array, axis, [(i, i ^ mask) for i in range(lax.axis_size(axi...  21.4 us
    all_to_all x1, starting transfers between devices, dense_local(): lax.all_to_all(pack(key_in[0], value_in[0], seq_count), 'seq', split_axis...  7.26 us
    all_to_all x1, starting transfers between devices, dense_local(): lax.all_to_all(returns, 'seq', split_axis=0, concat_axis=0, tiled=True)  5.01 us
    pallas_call x1, Pallas kernels, head_grads(): pl.pallas_call(head_grad_kernel, out_shape=[pltpu.HBM((2 * rows + 2 * HD,...  4.63 us
    pallas_call x1, Pallas kernels, backward(): pl.pallas_call(functools.partial(backward_kernel, members, 4 * here, scal...  4.26 us
    pallas_call x2, Pallas kernels, weight_part(): pl.pallas_call(functools.partial(weight_part_kernel, masks, docs), out_sh...  3.98 us
    pallas_call x1, Pallas kernels, project(): pl.pallas_call(project_kernel, out_shape=[struct(rows, width), struct(16,...  2.54 us
  transfers between devices with their start and end apart: 23, of which 11 were waited for; matrix products, arithmetic and copies ran while one was open for 1% of the time, Pallas kernels for 24%

profile of v5, /device:TPU:0, one launch (start us, length us, event | category | flops | bytes accessed | tf_op | source)
XLA Modules:
  0.0 86.7 jit_solution(3250177934490773869)
XLA Ops:
  0.6 2.1 %pack_keys.1 = bf16[8,512,128]{2,1,0:T(8,128)(2,1)} custom-call(bf16[128,1024]{1,0:T(8,128)(2,1)} %bitcast.12, bf16[128,1024]{1,0:T(8,128)(2,1)} %bitcast.13), custom_call_target="tpu_custom_call" | custom-call | flops 1 | bytes 1 | tf_op jit(solution)/shard_map/pack_keys/pallas_call | solution.py:96
  2.7 7.3 %all-to-all-start = ((bf16[8,512,128]{2,1,0:T(8,128)(2,1)}), bf16[8,512,128]{2,1,0:T(8,128)(2,1)S(1)}, u32[]{:S(2)}, u32[]{:S(2)}) async-start(bf16[8,512,128]{2,1,0:T(8,128)(2,1)} %pack_keys.1), calls=%async_computation | async-start | bytes 2097152 | tf_op jit(solution)/shard_map/all_to_all | solution.py:481
  10.0 4.6 %head_grads.1 = (bf16[512,128]{1,0:T(8,128)(2,1)}, bf16[512,128]{1,0:T(8,128)(2,1)}, bf16[512,128]{1,0:T(8,128)(2,1)}, bf16[512,128]{1,0:T(8,128)(2,1)}, bf16[12...) custom-call(bf16[128,1024]{1,0:T(8,128)(2,1)} %bitcast.11, bf16[128,2048]{1,0:T(8,128)(2,1)} %bitcast.10, ...), custom_call_target="tpu_custom_call" | custom-call | flops 1 | bytes 1 | tf_op jit(solution)/shard_map/head_grads/pallas_call | solution.py:139
  14.6 2.1 %collective-permute-start = (bf16[512,128]{1,0:T(8,128)(2,1)}, bf16[512,128]{1,0:T(8,128)(2,1)S(1)}, u32[]{:S(2)}, u32[]{:S(2)}) collective-permute-start(bf16[512,128]{1,0:T(8,128)(2,1)} %get-tuple-element.45), channel_id=1, source_target_pairs={{0,4},{4,0},{8,12},{12,8},{16,20},{20,16},{24,28},{28,24},{1,5},{5... | collective-permute-start | bytes 393224 | tf_op jit(solution)/shard_map/ppermute | solution.py:52
  18.7 4.4 %collective-permute-done.refs_1_ = bf16[512,128]{1,0:T(8,128)(2,1)S(1)} collective-permute-done((bf16[512,128]{1,0:T(8,128)(2,1)}, bf16[512,128]{1,0:T(8,128)(2,1)S(1)}, u32[]{:S(2)}, u32[]{:S(2)}) %collective-permute-start) | collective-permute-done | bytes 131104 | tf_op jit(solution)/shard_map/ppermute | solution.py:52
  23.1 1.8 %collective-permute-start.7 = (bf16[128,1024]{1,0:T(8,128)(2,1)}, bf16[128,1024]{1,0:T(8,128)(2,1)S(1)}, u32[]{:S(2)}, u32[]{:S(2)}) collective-permute-start(bf16[128,1024]{1,0:T(8,128)(2,1)} %get-tuple-element.67), channel_id=1, source_target_pairs={{0,4},{4,0},{8,12},{12,8},{16,20},{20,16},{24,28},{28,24},{1,5},{5... | collective-permute-start | bytes 786440 | tf_op jit(solution)/shard_map/ppermute | solution.py:52
  24.9 6.3 %collective-permute-done.1.refs_2_ = bf16[512,128]{1,0:T(8,128)(2,1)S(1)} collective-permute-done((bf16[512,128]{1,0:T(8,128)(2,1)}, bf16[512,128]{1,0:T(8,128)(2,1)S(1)}, u32[]{:S(2)}, u32[]{:S(2)}) %collective-permute-start.1) | collective-permute-done | bytes 131104 | tf_op jit(solution)/shard_map/ppermute | solution.py:52
  31.1 3.8 %collective-permute-start.9 = (bf16[128,1024]{1,0:T(8,128)(2,1)}, bf16[128,1024]{1,0:T(8,128)(2,1)S(1)}, u32[]{:S(2)}, u32[]{:S(2)}) collective-permute-start(bf16[128,1024]{1,0:T(8,128)(2,1)} %get-tuple-element.67), channel_id=1, source_target_pairs={{0,12},{4,8},{8,4},{12,0},{16,28},{20,24},{24,20},{28,16},{1,13},{... | collective-permute-start | bytes 786440 | tf_op jit(solution)/shard_map/ppermute | solution.py:52
  36.8 2.1 %attend.1 = (bf16[1024,128]{1,0:T(8,128)(2,1)S(1)}, f32[2,512]{1,0:T(2,128)S(1)}) custom-call(f32[16,1024]{1,0:T(8,128)S(1)} %reshape.14.bias_ref, bf16[8,512,128]{2,1,0:T(8,128)(2,1)S(1)} %all-to-all-done.pairs, bf16[512,128]{1,0:T(8,128)(2,1)S(1)} %copy-done.1, bf16[512,128]{1,0:T(8,128)(2,1)S(1)} %collective-permute-done.refs_1_, ...), custom_call_target="tpu_custom_call" | custom-call | flops 1 | bytes 1 | tf_op jit(solution)/shard_map/attend/pallas_call | solution.py:208
  38.9 1.5 %collective-permute-start.6 = (bf16[1024,128]{1,0:T(8,128)(2,1)S(1)}, bf16[1024,128]{1,0:T(8,128)(2,1)S(1)}, u32[]{:S(2)}, u32[]{:S(2)}) collective-permute-start(bf16[1024,128]{1,0:T(8,128)(2,1)S(1)} %get-tuple-element.65.near), channel_id=1, source_target_pairs={{0,4},{4,0},{8,12},{12,8},{16,20},{20,16},{24,28},{28,24},{1,5},{5... | collective-permute-start | bytes 786440 | tf_op jit(solution)/shard_map/ppermute | solution.py:52
  40.4 4.3 %attend_back.1 = (bf16[8,512,128]{2,1,0:T(8,128)(2,1)}, bf16[512,128]{1,0:T(8,128)(2,1)}, bf16[512,128]{1,0:T(8,128)(2,1)}, bf16[512,128]{1,0:T(8,128)(2,1)}, bf16[512,128]{1,0:T(8,128)(2,1)}) custom-call(f32[16,1024]{1,0:T(8,128)S(1)} %reshape.14.bias_ref, f32[2,512]{1,0:T(2,128)S(1)} %get-tuple-element.52.norm_ref, ...), custom_call_target="tpu_custom_call" | custom-call | flops 1 | bytes 1 | tf_op jit(solution)/shard_map/attend_back/pallas_call | solution.py:259
  44.7 5.0 %all-to-all-start.1 = ((bf16[8,512,128]{2,1,0:T(8,128)(2,1)}), bf16[8,512,128]{2,1,0:T(8,128)(2,1)S(1)}, u32[]{:S(2)}, u32[]{:S(2)}) async-start(bf16[8,512,128]{2,1,0:T(8,128)(2,1)} %get-tuple-element.60), calls=%async_computation.1 | async-start | bytes 2097152 | tf_op jit(solution)/shard_map/all_to_all | solution.py:498
  50.6 2.3 %weight_part.3 = bf16[1024,256]{1,0:T(8,128)(2,1)S(1)} custom-call(bf16[1024,128]{1,0:T(8,128)(2,1)S(1)} %get-tuple-element.65.near, bf16[1024,128]{1,0:T(8,128)(2,1)S(1)} %collective-permute-done.6.near_pair, bf16[128,1024]{1,0:T(8,128)(2,1)} %get-tuple-element.66.refs_0_, bf16[128,1024]{1,0:T(8,128)(2,1)} %copy-done.2, bf16[128,1024]{1,0:T(8,128)(2,1)} %copy-done.4, ...), custom_call_target="tpu_custom_call" | custom-call | flops 1 | bytes 1 | tf_op jit(solution)/shard_map/weight_part/pallas_call | solution.py:373
  53.0 1.7 %weight_part.2.own = f32[1024,256]{1,0:T(8,128)S(1)} custom-call(bf16[1024,128]{1,0:T(8,128)(2,1)S(1)} %get-tuple-element.65.near, bf16[1024,128]{1,0:T(8,128)(2,1)S(1)} %collective-permute-done.6.near_pair, bf16[128,1024]{1,0:T(8,128)(2,1)} %get-tuple-element.66.refs_0_, bf16[128,1024]{1,0:T(8,128)(2,1)} %copy-done.2, bf16[128,1024]{1,0:T(8,128)(2,1)} %copy-done.4, ...), custom_call_target="tpu_custom_call" | custom-call | flops 1 | bytes 1 | tf_op jit(solution)/shard_map/weight_part/pallas_call | solution.py:373
  54.9 1.6 %collective-permute-start.11 = (bf16[512,256]{1,0:T(8,128)(2,1)S(1)}, bf16[512,256]{1,0:T(8,128)(2,1)S(1)}, u32[]{:S(2)}, u32[]{:S(2)}) collective-permute-start(bf16[512,256]{1,0:T(8,128)(2,1)S(1)} %get-tuple-element.69), channel_id=1, source_target_pairs={{0,2},{1,3},{2,0},{3,1},{4,6},{5,7},{6,4},{7,5},{8,10},{9,11},{10,... | collective-permute-start | bytes 786440 | tf_op jit(solution)/shard_map/ppermute | solution.py:52
  56.5 2.0 %collective-permute-start.3 = (bf16[512,128]{1,0:T(8,128)(2,1)S(1)}, bf16[512,128]{1,0:T(8,128)(2,1)S(1)}, u32[]{:S(2)}, u32[]{:S(2)}) collective-permute-start(bf16[512,128]{1,0:T(8,128)(2,1)S(1)} %copy-done.11), channel_id=1, source_target_pairs={{0,4},{4,0},{8,12},{12,8},{16,20},{20,16},{24,28},{28,24},{1,5},{5... | collective-permute-start | bytes 393224 | tf_op jit(solution)/shard_map/ppermute | solution.py:52
  60.1 3.4 %collective-permute-done.11.other = bf16[512,256]{1,0:T(8,128)(2,1)S(1)} collective-permute-done((bf16[512,256]{1,0:T(8,128)(2,1)S(1)}, bf16[512,256]{1,0:T(8,128)(2,1)S(1)}, u32[]{:S(2)}, u32[]{:S(2)}) %collective-permute-start.11) | collective-permute-done | bytes 262176 | tf_op jit(solution)/shard_map/ppermute | solution.py:52
  63.6 3.0 %collective-permute-start.15 = (bf16[128,256]{1,0:T(8,128)(2,1)S(1)}, bf16[128,256]{1,0:T(8,128)(2,1)S(1)}, u32[]{:S(2)}, u32[]{:S(2)}) collective-permute-start(bf16[128,256]{1,0:T(8,128)(2,1)S(1)} %get-tuple-element.73), channel_id=1, source_target_pairs={{0,16},{4,20},{8,24},{12,28},{16,0},{20,4},{24,8},{28,12},{1,17},{... | collective-permute-start | bytes 196616 | tf_op jit(solution)/shard_map/ppermute | solution.py:52
  68.1 2.5 %collective-permute-done.4.refs_2_ = bf16[512,128]{1,0:T(8,128)(2,1)S(1)} collective-permute-done((bf16[512,128]{1,0:T(8,128)(2,1)S(1)}, bf16[512,128]{1,0:T(8,128)(2,1)S(1)}, u32[]{:S(2)}, u32[]{:S(2)}) %collective-permute-start.4) | collective-permute-done | bytes 131104 | tf_op jit(solution)/shard_map/ppermute | solution.py:52
  70.6 1.7 %collective-permute-done.5.refs_3_ = bf16[512,128]{1,0:T(8,128)(2,1)S(1)} collective-permute-done((bf16[512,128]{1,0:T(8,128)(2,1)S(1)}, bf16[512,128]{1,0:T(8,128)(2,1)S(1)}, u32[]{:S(2)}, u32[]{:S(2)}) %collective-permute-start.5) | collective-permute-done | bytes 131104 | tf_op jit(solution)/shard_map/ppermute | solution.py:52
  74.1 2.5 %project.1 = (bf16[128,2048]{1,0:T(8,128)(2,1)}, bf16[16,128]{1,0:T(8,128)(2,1)S(1)}) custom-call(bf16[128,1024]{1,0:T(8,128)(2,1)S(1)} %join_heads.1.attended, bf16[1024,2048]{1,0:T(8,128)(2,1)S(1)} %copy-done), custom_call_target="tpu_custom_call" | custom-call | flops 1 | bytes 1 | tf_op jit(solution)/shard_map/project/pallas_call | solution.py:334
  76.6 1.6 %collective-permute-done.15.refs_1_ = bf16[128,256]{1,0:T(8,128)(2,1)S(1)} collective-permute-done((bf16[128,256]{1,0:T(8,128)(2,1)S(1)}, bf16[128,256]{1,0:T(8,128)(2,1)S(1)}, u32[]{:S(2)}, u32[]{:S(2)}) %collective-permute-start.15) | collective-permute-done | bytes 65568 | tf_op jit(solution)/shard_map/ppermute | solution.py:52
  78.3 1.6 %collective-permute-start.16 = (bf16[128,256]{1,0:T(8,128)(2,1)S(1)}, bf16[128,256]{1,0:T(8,128)(2,1)S(1)}, u32[]{:S(2)}, u32[]{:S(2)}) collective-permute-start(bf16[128,256]{1,0:T(8,128)(2,1)S(1)} %weight_scale.3.refs_0_), channel_id=1, source_target_pairs={{0,2},{1,3},{2,0},{3,1},{4,6},{5,7},{6,4},{7,5},{8,10},{9,11},{10,... | collective-permute-start | bytes 196616 | tf_op jit(solution)/shard_map/ppermute | solution.py:52
  81.8 2.1 %unpack_grads.1 = (bf16[128,1024]{1,0:T(8,128)(2,1)}, bf16[128,1024]{1,0:T(8,128)(2,1)}, bf16[128,1024]{1,0:T(8,128)(2,1)}, bf16[16,128]{1,0:T(8,128)(2,1)S(1)}) custom-call(bf16[8,512,128]{2,1,0:T(8,128)(2,1)S(1)} %all-to-all-done.1.returned, bf16[512,128]{1,0:T(8,128)(2,1)} %get-tuple-element.54.refs_0_, bf16[512,128]{1,0:T(8,128)(2,1)} %copy-done.5, ...), custom_call_target="tpu_custom_call" | custom-call | flops 1 | bytes 3145728 | tf_op jit(solution)/shard_map/unpack_grads/pallas_call | solution.py:292
  (66 shorter events, 14.7 us)
Async XLA Ops:
  2.7 33.1 %all-to-all-start = ((bf16[8,512,128]{2,1,0:T(8,128)(2,1)}), bf16[8,512,128]{2,1,0:T(8,128)(2,1)S(1)}, u32[]{:S(2)}, u32[]{:S(2)}) async-start(bf16[8,512,128]{2,1,0:T(8,128)(2,1)} %pack_keys.1), calls=%async_computation | async-start | bytes 2097152 | tf_op jit(solution)/shard_map/all_to_all | solution.py:481
  14.6 8.4 %collective-permute-start = (bf16[512,128]{1,0:T(8,128)(2,1)}, bf16[512,128]{1,0:T(8,128)(2,1)S(1)}, u32[]{:S(2)}, u32[]{:S(2)}) collective-permute-start(bf16[512,128]{1,0:T(8,128)(2,1)} %get-tuple-element.45), channel_id=1, source_target_pairs={{0,4},{4,0},{8,12},{12,8},{16,20},{20,16},{24,28},{28,24},{1,5},{5... | collective-permute-start | bytes 393224 | tf_op jit(solution)/shard_map/ppermute | solution.py:52
  16.7 14.4 %collective-permute-start.1 = (bf16[512,128]{1,0:T(8,128)(2,1)}, bf16[512,128]{1,0:T(8,128)(2,1)S(1)}, u32[]{:S(2)}, u32[]{:S(2)}) collective-permute-start(bf16[512,128]{1,0:T(8,128)(2,1)} %get-tuple-element.49), channel_id=1, source_target_pairs={{0,8},{4,12},{8,0},{12,4},{16,24},{20,28},{24,16},{28,20},{1,9},{5... | collective-permute-start | bytes 393224 | tf_op jit(solution)/shard_map/ppermute | solution.py:52
  18.2 16.7 %collective-permute-start.2 = (bf16[512,128]{1,0:T(8,128)(2,1)}, bf16[512,128]{1,0:T(8,128)(2,1)S(1)}, u32[]{:S(2)}, u32[]{:S(2)}) collective-permute-start(bf16[512,128]{1,0:T(8,128)(2,1)} %get-tuple-element.51), channel_id=1, source_target_pairs={{0,12},{4,8},{8,4},{12,0},{16,28},{20,24},{24,20},{28,16},{1,13},{... | collective-permute-start | bytes 393224 | tf_op jit(solution)/shard_map/ppermute | solution.py:52
  23.1 26.6 %collective-permute-start.7 = (bf16[128,1024]{1,0:T(8,128)(2,1)}, bf16[128,1024]{1,0:T(8,128)(2,1)S(1)}, u32[]{:S(2)}, u32[]{:S(2)}) collective-permute-start(bf16[128,1024]{1,0:T(8,128)(2,1)} %get-tuple-element.67), channel_id=1, source_target_pairs={{0,4},{4,0},{8,12},{12,8},{16,20},{20,16},{24,28},{28,24},{1,5},{5... | collective-permute-start | bytes 786440 | tf_op jit(solution)/shard_map/ppermute | solution.py:52
  31.1 18.5 %collective-permute-start.9 = (bf16[128,1024]{1,0:T(8,128)(2,1)}, bf16[128,1024]{1,0:T(8,128)(2,1)S(1)}, u32[]{:S(2)}, u32[]{:S(2)}) collective-permute-start(bf16[128,1024]{1,0:T(8,128)(2,1)} %get-tuple-element.67), channel_id=1, source_target_pairs={{0,12},{4,8},{8,4},{12,0},{16,28},{20,24},{24,20},{28,16},{1,13},{... | collective-permute-start | bytes 786440 | tf_op jit(solution)/shard_map/ppermute | solution.py:52
  34.9 14.8 %collective-permute-start.8 = (bf16[128,1024]{1,0:T(8,128)(2,1)}, bf16[128,1024]{1,0:T(8,128)(2,1)S(1)}, u32[]{:S(2)}, u32[]{:S(2)}) collective-permute-start(bf16[128,1024]{1,0:T(8,128)(2,1)} %get-tuple-element.66.refs_0_), channel_id=1, source_target_pairs={{0,8},{4,12},{8,0},{12,4},{16,24},{20,28},{24,16},{28,20},{1,9},{5... | collective-permute-start | bytes 786440 | tf_op jit(solution)/shard_map/ppermute | solution.py:52
  38.9 10.8 %collective-permute-start.6 = (bf16[1024,128]{1,0:T(8,128)(2,1)S(1)}, bf16[1024,128]{1,0:T(8,128)(2,1)S(1)}, u32[]{:S(2)}, u32[]{:S(2)}) collective-permute-start(bf16[1024,128]{1,0:T(8,128)(2,1)S(1)} %get-tuple-element.65.near), channel_id=1, source_target_pairs={{0,4},{4,0},{8,12},{12,8},{16,20},{20,16},{24,28},{28,24},{1,5},{5... | collective-permute-start | bytes 786440 | tf_op jit(solution)/shard_map/ppermute | solution.py:52
  44.7 37.1 %all-to-all-start.1 = ((bf16[8,512,128]{2,1,0:T(8,128)(2,1)}), bf16[8,512,128]{2,1,0:T(8,128)(2,1)S(1)}, u32[]{:S(2)}, u32[]{:S(2)}) async-start(bf16[8,512,128]{2,1,0:T(8,128)(2,1)} %get-tuple-element.60), calls=%async_computation.1 | async-start | bytes 2097152 | tf_op jit(solution)/shard_map/all_to_all | solution.py:498
  49.7 24.4 %copy-start = (bf16[1024,2048]{1,0:T(8,128)(2,1)S(1)}, bf16[1024,2048]{1,0:T(8,128)(2,1)}, u32[]{:S(2)}) copy-start(bf16[1024,2048]{1,0:T(8,128)(2,1)} %weight_ref.3) | copy-start | bytes 12582916
  52.9 2.0 %collective-permute-start.10 = (bf16[1024,256]{1,0:T(8,128)(2,1)S(1)}, bf16[1024,256]{1,0:T(8,128)(2,1)S(1)}, u32[]{:S(2)}, u32[]{:S(2)}) collective-permute-start(bf16[1024,256]{1,0:T(8,128)(2,1)S(1)} %weight_part.3), channel_id=1, source_target_pairs={{0,1},{1,0},{2,3},{3,2},{4,5},{5,4},{6,7},{7,6},{8,9},{9,8},{10,11... | collective-permute-start | bytes 1572872 | tf_op jit(solution)/shard_map/ppermute | solution.py:52
  54.9 8.6 %collective-permute-start.11 = (bf16[512,256]{1,0:T(8,128)(2,1)S(1)}, bf16[512,256]{1,0:T(8,128)(2,1)S(1)}, u32[]{:S(2)}, u32[]{:S(2)}) collective-permute-start(bf16[512,256]{1,0:T(8,128)(2,1)S(1)} %get-tuple-element.69), channel_id=1, source_target_pairs={{0,2},{1,3},{2,0},{3,1},{4,6},{5,7},{6,4},{7,5},{8,10},{9,11},{10,... | collective-permute-start | bytes 786440 | tf_op jit(solution)/shard_map/ppermute | solution.py:52
  56.5 11.5 %collective-permute-start.3 = (bf16[512,128]{1,0:T(8,128)(2,1)S(1)}, bf16[512,128]{1,0:T(8,128)(2,1)S(1)}, u32[]{:S(2)}, u32[]{:S(2)}) collective-permute-start(bf16[512,128]{1,0:T(8,128)(2,1)S(1)} %copy-done.11), channel_id=1, source_target_pairs={{0,4},{4,0},{8,12},{12,8},{16,20},{20,16},{24,28},{28,24},{1,5},{5... | collective-permute-start | bytes 393224 | tf_op jit(solution)/shard_map/ppermute | solution.py:52
  58.6 12.1 %collective-permute-start.4 = (bf16[512,128]{1,0:T(8,128)(2,1)S(1)}, bf16[512,128]{1,0:T(8,128)(2,1)S(1)}, u32[]{:S(2)}, u32[]{:S(2)}) collective-permute-start(bf16[512,128]{1,0:T(8,128)(2,1)S(1)} %copy-done.10), channel_id=1, source_target_pairs={{0,8},{4,12},{8,0},{12,4},{16,24},{20,28},{24,16},{28,20},{1,9},{5... | collective-permute-start | bytes 393224 | tf_op jit(solution)/shard_map/ppermute | solution.py:52
  60.0 12.3 %collective-permute-start.5 = (bf16[512,128]{1,0:T(8,128)(2,1)S(1)}, bf16[512,128]{1,0:T(8,128)(2,1)S(1)}, u32[]{:S(2)}, u32[]{:S(2)}) collective-permute-start(bf16[512,128]{1,0:T(8,128)(2,1)S(1)} %copy-done.9), channel_id=1, source_target_pairs={{0,12},{4,8},{8,4},{12,0},{16,28},{20,24},{24,20},{28,16},{1,13},{... | collective-permute-start | bytes 393224 | tf_op jit(solution)/shard_map/ppermute | solution.py:52
  63.6 14.7 %collective-permute-start.15 = (bf16[128,256]{1,0:T(8,128)(2,1)S(1)}, bf16[128,256]{1,0:T(8,128)(2,1)S(1)}, u32[]{:S(2)}, u32[]{:S(2)}) collective-permute-start(bf16[128,256]{1,0:T(8,128)(2,1)S(1)} %get-tuple-element.73), channel_id=1, source_target_pairs={{0,16},{4,20},{8,24},{12,28},{16,0},{20,4},{24,8},{28,12},{1,17},{... | collective-permute-start | bytes 196616 | tf_op jit(solution)/shard_map/ppermute | solution.py:52
  66.5 13.3 %collective-permute-start.12 = (bf16[128,256]{1,0:T(8,128)(2,1)S(1)}, bf16[128,256]{1,0:T(8,128)(2,1)S(1)}, u32[]{:S(2)}, u32[]{:S(2)}) collective-permute-start(bf16[128,256]{1,0:T(8,128)(2,1)S(1)} %get-tuple-element.70), channel_id=1, source_target_pairs={{0,4},{4,0},{8,12},{12,8},{16,20},{20,16},{24,28},{28,24},{1,5},{5... | collective-permute-start | bytes 196616 | tf_op jit(solution)/shard_map/ppermute | solution.py:52
  68.0 11.9 %collective-permute-start.13 = (bf16[128,256]{1,0:T(8,128)(2,1)S(1)}, bf16[128,256]{1,0:T(8,128)(2,1)S(1)}, u32[]{:S(2)}, u32[]{:S(2)}) collective-permute-start(bf16[128,256]{1,0:T(8,128)(2,1)S(1)} %get-tuple-element.71), channel_id=1, source_target_pairs={{0,20},{4,16},{8,28},{12,24},{16,4},{20,0},{24,12},{28,8},{1,21},{... | collective-permute-start | bytes 196616 | tf_op jit(solution)/shard_map/ppermute | solution.py:52
  78.3 5.6 %collective-permute-start.16 = (bf16[128,256]{1,0:T(8,128)(2,1)S(1)}, bf16[128,256]{1,0:T(8,128)(2,1)S(1)}, u32[]{:S(2)}, u32[]{:S(2)}) collective-permute-start(bf16[128,256]{1,0:T(8,128)(2,1)S(1)} %weight_scale.3.refs_0_), channel_id=1, source_target_pairs={{0,2},{1,3},{2,0},{3,1},{4,6},{5,7},{6,4},{7,5},{8,10},{9,11},{10,... | collective-permute-start | bytes 196616 | tf_op jit(solution)/shard_map/ppermute | solution.py:52
  79.9 4.3 %collective-permute-start.14 = (bf16[128,256]{1,0:T(8,128)(2,1)S(1)}, bf16[128,256]{1,0:T(8,128)(2,1)S(1)}, u32[]{:S(2)}, u32[]{:S(2)}) collective-permute-start(bf16[128,256]{1,0:T(8,128)(2,1)S(1)} %weight_scale.2.refs_4_), channel_id=1, source_target_pairs={{0,2},{1,3},{2,0},{3,1},{4,6},{5,7},{6,4},{7,5},{8,10},{9,11},{10,... | collective-permute-start | bytes 196616 | tf_op jit(solution)/shard_map/ppermute | solution.py:52
  81.2 3.5 %collective-permute-start.19 = (bf16[128,256]{1,0:T(8,128)(2,1)S(1)}, bf16[128,256]{1,0:T(8,128)(2,1)S(1)}, u32[]{:S(2)}, u32[]{:S(2)}) collective-permute-start(bf16[128,256]{1,0:T(8,128)(2,1)S(1)} %weight_scale.2.refs_4_), channel_id=1, source_target_pairs={{0,1},{1,0},{2,3},{3,2},{4,5},{5,4},{6,7},{7,6},{8,9},{9,8},{10,11... | collective-permute-start | bytes 196616 | tf_op jit(solution)/shard_map/ppermute | solution.py:52
  81.2 3.5 %collective-permute-start.17 = (bf16[128,256]{1,0:T(8,128)(2,1)S(1)}, bf16[128,256]{1,0:T(8,128)(2,1)S(1)}, u32[]{:S(2)}, u32[]{:S(2)}) collective-permute-start(bf16[128,256]{1,0:T(8,128)(2,1)S(1)} %weight_scale.3.refs_0_), channel_id=1, source_target_pairs={{0,1},{1,0},{2,3},{3,2},{4,5},{5,4},{6,7},{7,6},{8,9},{9,8},{10,11... | collective-permute-start | bytes 196616 | tf_op jit(solution)/shard_map/ppermute | solution.py:52
  84.2 1.3 %collective-permute-start.20 = (bf16[128,256]{1,0:T(8,128)(2,1)S(1)}, bf16[128,256]{1,0:T(8,128)(2,1)S(1)}, u32[]{:S(2)}, u32[]{:S(2)}) collective-permute-start(bf16[128,256]{1,0:T(8,128)(2,1)S(1)} %collective-permute-done.14.refs_6_), channel_id=1, source_target_pairs={{0,1},{1,0},{2,3},{3,2},{4,5},{5,4},{6,7},{7,6},{8,9},{9,8},{10,11... | collective-permute-start | bytes 196616 | tf_op jit(solution)/shard_map/ppermute | solution.py:52
  84.2 1.4 %collective-permute-start.18 = (bf16[128,256]{1,0:T(8,128)(2,1)S(1)}, bf16[128,256]{1,0:T(8,128)(2,1)S(1)}, u32[]{:S(2)}, u32[]{:S(2)}) collective-permute-start(bf16[128,256]{1,0:T(8,128)(2,1)S(1)} %collective-permute-done.16.refs_2_), channel_id=1, source_target_pairs={{0,1},{1,0},{2,3},{3,2},{4,5},{5,4},{6,7},{7,6},{8,9},{9,8},{10,11... | collective-permute-start | bytes 196616 | tf_op jit(solution)/shard_map/ppermute | solution.py:52
  (11 other events, 68.6 us)

commit v6 on v5

--- a/solution.py
+++ b/solution.py
@@ -297,7 +297,7 @@
         compiler_params=params(16),
         cost_estimate=cost(1, 24 * rows * width),
         name="unpack_grads",
-    )(returned, *map(in_hbm, queries))
+    )(returned, *queries)
 
 
 def join_heads_kernel(*refs):
@@ -319,7 +319,7 @@
         compiler_params=params(8),
         cost_estimate=cost(HEADS_FLOPS),
         name="join_heads",
-    )(*map(in_hbm, parts))
+    )(*parts)
 
 
 def project_kernel(attended, weight_ref, out_ref, token):

time: 87 us -> 87 us (level)
  waiting for transfers between devices: 22.3 us -> 25.2 us
  Pallas kernels: 24.1 us -> 21.9 us
    ppermute x21, waiting for transfers between devices: 21.4 us -> 24.2 us  [swap(): lax.ppermute(array, axis, [(i, i ^ mask) for i in range(lax.axis_size(axi...]
    pallas_call x1, Pallas kernels: 1.15 us -> 0.06 us  [join_heads(): pl.pallas_call(join_heads_kernel, out_shape=struct(rows, 2 * HD * len(par...]
    pallas_call x1, Pallas kernels: 2.09 us -> 1.01 us  [unpack(): pl.pallas_call(unpack_kernel, out_shape=[struct(rows, width)] * 3 + [stru...]
    unnamed x25 -> x21, local copies, waits for them, and re-layouts: 2.46 us -> 1.82 us
  transfers between devices with their start and end apart: 23 -> 23, of which waited for: 11 -> 11; matrix products, arithmetic and copies ran while one was open for 1% -> 1% of each run, Pallas kernels for 24% -> 22%
where the time goes in v6:
time: 87 us; the launch traced here: 86.7 us
  starting transfers between devices  36.7 us (42%)
  waiting for transfers between devices  25.2 us (29%)
  Pallas kernels  21.9 us (25%)
  local copies, waits for them, and re-layouts  2.08 us (2%)
    ppermute x21, starting transfers between devices, swap(): lax.ppermute(array, axis, [(i, i ^ mask) for i in range(lax.axis_size(axi...  24.4 us
    ppermute x21, waiting for transfers between devices, swap(): lax.ppermute(array, axis, [(i, i ^ mask) for i in range(lax.axis_size(axi...  24.2 us
    all_to_all x1, starting transfers between devices, dense_local(): lax.all_to_all(pack(key_in[0], value_in[0], seq_count), 'seq', split_axis...  7.26 us
    all_to_all x1, starting transfers between devices, dense_local(): lax.all_to_all(returns, 'seq', split_axis=0, concat_axis=0, tiled=True)  5.02 us
    pallas_call x1, Pallas kernels, head_grads(): pl.pallas_call(head_grad_kernel, out_shape=[pltpu.HBM((2 * rows + 2 * HD,...  4.63 us
    pallas_call x1, Pallas kernels, backward(): pl.pallas_call(functools.partial(backward_kernel, members, 4 * here, scal...  4.26 us
    pallas_call x2, Pallas kernels, weight_part(): pl.pallas_call(functools.partial(weight_part_kernel, masks, docs), out_sh...  3.97 us
    pallas_call x1, Pallas kernels, project(): pl.pallas_call(project_kernel, out_shape=[struct(rows, width), struct(16,...  2.54 us
  transfers between devices with their start and end apart: 23, of which 11 were waited for; matrix products, arithmetic and copies ran while one was open for 1% of the time, Pallas kernels for 22%

profile of v6, /device:TPU:0, one launch (start us, length us, event | category | flops | bytes accessed | tf_op | source)
XLA Modules:
  0.0 86.7 jit_solution(312721954350659063)
XLA Ops:
  0.6 2.1 %pack_keys.1 = bf16[8,512,128]{2,1,0:T(8,128)(2,1)} custom-call(bf16[128,1024]{1,0:T(8,128)(2,1)} %bitcast.12, bf16[128,1024]{1,0:T(8,128)(2,1)} %bitcast.13), custom_call_target="tpu_custom_call" | custom-call | flops 1 | bytes 1 | tf_op jit(solution)/shard_map/pack_keys/pallas_call | solution.py:96
  2.7 7.3 %all-to-all-start = ((bf16[8,512,128]{2,1,0:T(8,128)(2,1)}), bf16[8,512,128]{2,1,0:T(8,128)(2,1)S(1)}, u32[]{:S(2)}, u32[]{:S(2)}) async-start(bf16[8,512,128]{2,1,0:T(8,128)(2,1)} %pack_keys.1), calls=%async_computation | async-start | bytes 2097152 | tf_op jit(solution)/shard_map/all_to_all | solution.py:481
  10.0 4.6 %head_grads.1 = (bf16[512,128]{1,0:T(8,128)(2,1)}, bf16[512,128]{1,0:T(8,128)(2,1)}, bf16[512,128]{1,0:T(8,128)(2,1)}, bf16[512,128]{1,0:T(8,128)(2,1)}, bf16[12...) custom-call(bf16[128,1024]{1,0:T(8,128)(2,1)} %bitcast.11, bf16[128,2048]{1,0:T(8,128)(2,1)} %bitcast.10, ...), custom_call_target="tpu_custom_call" | custom-call | flops 1 | bytes 1 | tf_op jit(solution)/shard_map/head_grads/pallas_call | solution.py:139
  14.6 2.1 %collective-permute-start = (bf16[512,128]{1,0:T(8,128)(2,1)}, bf16[512,128]{1,0:T(8,128)(2,1)S(1)}, u32[]{:S(2)}, u32[]{:S(2)}) collective-permute-start(bf16[512,128]{1,0:T(8,128)(2,1)} %get-tuple-element.45), channel_id=1, source_target_pairs={{0,4},{4,0},{8,12},{12,8},{16,20},{20,16},{24,28},{28,24},{1,5},{5... | collective-permute-start | bytes 393224 | tf_op jit(solution)/shard_map/ppermute | solution.py:52
  18.7 4.4 %collective-permute-done.refs_1_ = bf16[512,128]{1,0:T(8,128)(2,1)S(1)} collective-permute-done((bf16[512,128]{1,0:T(8,128)(2,1)}, bf16[512,128]{1,0:T(8,128)(2,1)S(1)}, u32[]{:S(2)}, u32[]{:S(2)}) %collective-permute-start) | collective-permute-done | bytes 131104 | tf_op jit(solution)/shard_map/ppermute | solution.py:52
  23.1 1.8 %collective-permute-start.7 = (bf16[128,1024]{1,0:T(8,128)(2,1)}, bf16[128,1024]{1,0:T(8,128)(2,1)S(1)}, u32[]{:S(2)}, u32[]{:S(2)}) collective-permute-start(bf16[128,1024]{1,0:T(8,128)(2,1)} %get-tuple-element.67), channel_id=1, source_target_pairs={{0,4},{4,0},{8,12},{12,8},{16,20},{20,16},{24,28},{28,24},{1,5},{5... | collective-permute-start | bytes 786440 | tf_op jit(solution)/shard_map/ppermute | solution.py:52
  24.9 6.3 %collective-permute-done.1.refs_2_ = bf16[512,128]{1,0:T(8,128)(2,1)S(1)} collective-permute-done((bf16[512,128]{1,0:T(8,128)(2,1)}, bf16[512,128]{1,0:T(8,128)(2,1)S(1)}, u32[]{:S(2)}, u32[]{:S(2)}) %collective-permute-start.1) | collective-permute-done | bytes 131104 | tf_op jit(solution)/shard_map/ppermute | solution.py:52
  31.1 3.8 %collective-permute-start.9 = (bf16[128,1024]{1,0:T(8,128)(2,1)}, bf16[128,1024]{1,0:T(8,128)(2,1)S(1)}, u32[]{:S(2)}, u32[]{:S(2)}) collective-permute-start(bf16[128,1024]{1,0:T(8,128)(2,1)} %get-tuple-element.67), channel_id=1, source_target_pairs={{0,12},{4,8},{8,4},{12,0},{16,28},{20,24},{24,20},{28,16},{1,13},{... | collective-permute-start | bytes 786440 | tf_op jit(solution)/shard_map/ppermute | solution.py:52
  36.8 2.1 %attend.1 = (bf16[1024,128]{1,0:T(8,128)(2,1)S(1)}, f32[2,512]{1,0:T(2,128)S(1)}) custom-call(f32[16,1024]{1,0:T(8,128)S(1)} %reshape.14.bias_ref, bf16[8,512,128]{2,1,0:T(8,128)(2,1)S(1)} %all-to-all-done.pairs, bf16[512,128]{1,0:T(8,128)(2,1)S(1)} %copy-done.2, bf16[512,128]{1,0:T(8,128)(2,1)S(1)} %collective-permute-done.refs_1_, ...), custom_call_target="tpu_custom_call" | custom-call | flops 1 | bytes 1 | tf_op jit(solution)/shard_map/attend/pallas_call | solution.py:208
  38.9 1.5 %collective-permute-start.6 = (bf16[1024,128]{1,0:T(8,128)(2,1)S(1)}, bf16[1024,128]{1,0:T(8,128)(2,1)S(1)}, u32[]{:S(2)}, u32[]{:S(2)}) collective-permute-start(bf16[1024,128]{1,0:T(8,128)(2,1)S(1)} %get-tuple-element.65.near), channel_id=1, source_target_pairs={{0,4},{4,0},{8,12},{12,8},{16,20},{20,16},{24,28},{28,24},{1,5},{5... | collective-permute-start | bytes 786440 | tf_op jit(solution)/shard_map/ppermute | solution.py:52
  40.4 4.3 %attend_back.1 = (bf16[8,512,128]{2,1,0:T(8,128)(2,1)}, bf16[512,128]{1,0:T(8,128)(2,1)}, bf16[512,128]{1,0:T(8,128)(2,1)}, bf16[512,128]{1,0:T(8,128)(2,1)}, bf16[512,128]{1,0:T(8,128)(2,1)}) custom-call(f32[16,1024]{1,0:T(8,128)S(1)} %reshape.14.bias_ref, f32[2,512]{1,0:T(2,128)S(1)} %get-tuple-element.52.norm_ref, ...), custom_call_target="tpu_custom_call" | custom-call | flops 1 | bytes 1 | tf_op jit(solution)/shard_map/attend_back/pallas_call | solution.py:259
  44.7 5.0 %all-to-all-start.1 = ((bf16[8,512,128]{2,1,0:T(8,128)(2,1)}), bf16[8,512,128]{2,1,0:T(8,128)(2,1)S(1)}, u32[]{:S(2)}, u32[]{:S(2)}) async-start(bf16[8,512,128]{2,1,0:T(8,128)(2,1)} %get-tuple-element.60), calls=%async_computation.1 | async-start | bytes 2097152 | tf_op jit(solution)/shard_map/all_to_all | solution.py:498
  50.6 2.3 %weight_part.3 = bf16[1024,256]{1,0:T(8,128)(2,1)S(1)} custom-call(bf16[1024,128]{1,0:T(8,128)(2,1)S(1)} %get-tuple-element.65.near, bf16[1024,128]{1,0:T(8,128)(2,1)S(1)} %collective-permute-done.6.near_pair, bf16[128,1024]{1,0:T(8,128)(2,1)} %get-tuple-element.66.refs_0_, bf16[128,1024]{1,0:T(8,128)(2,1)} %copy-done.3, bf16[128,1024]{1,0:T(8,128)(2,1)} %copy-done.5, ...), custom_call_target="tpu_custom_call" | custom-call | flops 1 | bytes 1 | tf_op jit(solution)/shard_map/weight_part/pallas_call | solution.py:373
  53.0 1.7 %weight_part.2.own = f32[1024,256]{1,0:T(8,128)S(1)} custom-call(bf16[1024,128]{1,0:T(8,128)(2,1)S(1)} %get-tuple-element.65.near, bf16[1024,128]{1,0:T(8,128)(2,1)S(1)} %collective-permute-done.6.near_pair, bf16[128,1024]{1,0:T(8,128)(2,1)} %get-tuple-element.66.refs_0_, bf16[128,1024]{1,0:T(8,128)(2,1)} %copy-done.3, bf16[128,1024]{1,0:T(8,128)(2,1)} %copy-done.5, ...), custom_call_target="tpu_custom_call" | custom-call | flops 1 | bytes 1 | tf_op jit(solution)/shard_map/weight_part/pallas_call | solution.py:373
  55.0 1.6 %collective-permute-start.11 = (bf16[512,256]{1,0:T(8,128)(2,1)S(1)}, bf16[512,256]{1,0:T(8,128)(2,1)S(1)}, u32[]{:S(2)}, u32[]{:S(2)}) collective-permute-start(bf16[512,256]{1,0:T(8,128)(2,1)S(1)} %get-tuple-element.69), channel_id=1, source_target_pairs={{0,2},{1,3},{2,0},{3,1},{4,6},{5,7},{6,4},{7,5},{8,10},{9,11},{10,... | collective-permute-start | bytes 786440 | tf_op jit(solution)/shard_map/ppermute | solution.py:52
  56.5 2.0 %collective-permute-start.3 = (bf16[512,128]{1,0:T(8,128)(2,1)S(1)}, bf16[512,128]{1,0:T(8,128)(2,1)S(1)}, u32[]{:S(2)}, u32[]{:S(2)}) collective-permute-start(bf16[512,128]{1,0:T(8,128)(2,1)S(1)} %copy-done.9), channel_id=1, source_target_pairs={{0,4},{4,0},{8,12},{12,8},{16,20},{20,16},{24,28},{28,24},{1,5},{5... | collective-permute-start | bytes 393224 | tf_op jit(solution)/shard_map/ppermute | solution.py:52
  60.1 3.4 %collective-permute-done.11.other = bf16[512,256]{1,0:T(8,128)(2,1)S(1)} collective-permute-done((bf16[512,256]{1,0:T(8,128)(2,1)S(1)}, bf16[512,256]{1,0:T(8,128)(2,1)S(1)}, u32[]{:S(2)}, u32[]{:S(2)}) %collective-permute-start.11) | collective-permute-done | bytes 262176 | tf_op jit(solution)/shard_map/ppermute | solution.py:52
  63.6 3.0 %collective-permute-start.15 = (bf16[128,256]{1,0:T(8,128)(2,1)S(1)}, bf16[128,256]{1,0:T(8,128)(2,1)S(1)}, u32[]{:S(2)}, u32[]{:S(2)}) collective-permute-start(bf16[128,256]{1,0:T(8,128)(2,1)S(1)} %get-tuple-element.73), channel_id=1, source_target_pairs={{0,16},{4,20},{8,24},{12,28},{16,0},{20,4},{24,8},{28,12},{1,17},{... | collective-permute-start | bytes 196616 | tf_op jit(solution)/shard_map/ppermute | solution.py:52
  66.6 1.5 %collective-permute-start.12 = (bf16[128,256]{1,0:T(8,128)(2,1)S(1)}, bf16[128,256]{1,0:T(8,128)(2,1)S(1)}, u32[]{:S(2)}, u32[]{:S(2)}) collective-permute-start(bf16[128,256]{1,0:T(8,128)(2,1)S(1)} %get-tuple-element.70), channel_id=1, source_target_pairs={{0,4},{4,0},{8,12},{12,8},{16,20},{20,16},{24,28},{28,24},{1,5},{5... | collective-permute-start | bytes 196616 | tf_op jit(solution)/shard_map/ppermute | solution.py:52
  68.1 2.5 %collective-permute-done.4.refs_2_ = bf16[512,128]{1,0:T(8,128)(2,1)S(1)} collective-permute-done((bf16[512,128]{1,0:T(8,128)(2,1)S(1)}, bf16[512,128]{1,0:T(8,128)(2,1)S(1)}, u32[]{:S(2)}, u32[]{:S(2)}) %collective-permute-start.4) | collective-permute-done | bytes 131104 | tf_op jit(solution)/shard_map/ppermute | solution.py:52
  70.6 1.6 %collective-permute-done.5.refs_3_ = bf16[512,128]{1,0:T(8,128)(2,1)S(1)} collective-permute-done((bf16[512,128]{1,0:T(8,128)(2,1)S(1)}, bf16[512,128]{1,0:T(8,128)(2,1)S(1)}, u32[]{:S(2)}, u32[]{:S(2)}) %collective-permute-start.5) | collective-permute-done | bytes 131104 | tf_op jit(solution)/shard_map/ppermute | solution.py:52
  72.4 2.5 %project.1 = (bf16[128,2048]{1,0:T(8,128)(2,1)}, bf16[16,128]{1,0:T(8,128)(2,1)S(1)}) custom-call(bf16[128,1024]{1,0:T(8,128)(2,1)S(1)} %join_heads.1.attended, bf16[1024,2048]{1,0:T(8,128)(2,1)S(1)} %copy-done), custom_call_target="tpu_custom_call" | custom-call | flops 1 | bytes 1 | tf_op jit(solution)/shard_map/project/pallas_call | solution.py:334
  74.9 3.4 %collective-permute-done.15.refs_1_ = bf16[128,256]{1,0:T(8,128)(2,1)S(1)} collective-permute-done((bf16[128,256]{1,0:T(8,128)(2,1)S(1)}, bf16[128,256]{1,0:T(8,128)(2,1)S(1)}, u32[]{:S(2)}, u32[]{:S(2)}) %collective-permute-start.15) | collective-permute-done | bytes 65568 | tf_op jit(solution)/shard_map/ppermute | solution.py:52
  78.3 1.6 %collective-permute-start.16 = (bf16[128,256]{1,0:T(8,128)(2,1)S(1)}, bf16[128,256]{1,0:T(8,128)(2,1)S(1)}, u32[]{:S(2)}, u32[]{:S(2)}) collective-permute-start(bf16[128,256]{1,0:T(8,128)(2,1)S(1)} %weight_scale.3.refs_0_), channel_id=1, source_target_pairs={{0,2},{1,3},{2,0},{3,1},{4,6},{5,7},{6,4},{7,5},{8,10},{9,11},{10,... | collective-permute-start | bytes 196616 | tf_op jit(solution)/shard_map/ppermute | solution.py:52
  (62 shorter events, 13.6 us)
Async XLA Ops:
  2.7 33.1 %all-to-all-start = ((bf16[8,512,128]{2,1,0:T(8,128)(2,1)}), bf16[8,512,128]{2,1,0:T(8,128)(2,1)S(1)}, u32[]{:S(2)}, u32[]{:S(2)}) async-start(bf16[8,512,128]{2,1,0:T(8,128)(2,1)} %pack_keys.1), calls=%async_computation | async-start | bytes 2097152 | tf_op jit(solution)/shard_map/all_to_all | solution.py:481
  14.6 8.4 %collective-permute-start = (bf16[512,128]{1,0:T(8,128)(2,1)}, bf16[512,128]{1,0:T(8,128)(2,1)S(1)}, u32[]{:S(2)}, u32[]{:S(2)}) collective-permute-start(bf16[512,128]{1,0:T(8,128)(2,1)} %get-tuple-element.45), channel_id=1, source_target_pairs={{0,4},{4,0},{8,12},{12,8},{16,20},{20,16},{24,28},{28,24},{1,5},{5... | collective-permute-start | bytes 393224 | tf_op jit(solution)/shard_map/ppermute | solution.py:52
  16.7 14.4 %collective-permute-start.1 = (bf16[512,128]{1,0:T(8,128)(2,1)}, bf16[512,128]{1,0:T(8,128)(2,1)S(1)}, u32[]{:S(2)}, u32[]{:S(2)}) collective-permute-start(bf16[512,128]{1,0:T(8,128)(2,1)} %get-tuple-element.49), channel_id=1, source_target_pairs={{0,8},{4,12},{8,0},{12,4},{16,24},{20,28},{24,16},{28,20},{1,9},{5... | collective-permute-start | bytes 393224 | tf_op jit(solution)/shard_map/ppermute | solution.py:52
  18.2 16.7 %collective-permute-start.2 = (bf16[512,128]{1,0:T(8,128)(2,1)}, bf16[512,128]{1,0:T(8,128)(2,1)S(1)}, u32[]{:S(2)}, u32[]{:S(2)}) collective-permute-start(bf16[512,128]{1,0:T(8,128)(2,1)} %get-tuple-element.51), channel_id=1, source_target_pairs={{0,12},{4,8},{8,4},{12,0},{16,28},{20,24},{24,20},{28,16},{1,13},{... | collective-permute-start | bytes 393224 | tf_op jit(solution)/shard_map/ppermute | solution.py:52
  23.1 26.6 %collective-permute-start.7 = (bf16[128,1024]{1,0:T(8,128)(2,1)}, bf16[128,1024]{1,0:T(8,128)(2,1)S(1)}, u32[]{:S(2)}, u32[]{:S(2)}) collective-permute-start(bf16[128,1024]{1,0:T(8,128)(2,1)} %get-tuple-element.67), channel_id=1, source_target_pairs={{0,4},{4,0},{8,12},{12,8},{16,20},{20,16},{24,28},{28,24},{1,5},{5... | collective-permute-start | bytes 786440 | tf_op jit(solution)/shard_map/ppermute | solution.py:52
  31.1 18.5 %collective-permute-start.9 = (bf16[128,1024]{1,0:T(8,128)(2,1)}, bf16[128,1024]{1,0:T(8,128)(2,1)S(1)}, u32[]{:S(2)}, u32[]{:S(2)}) collective-permute-start(bf16[128,1024]{1,0:T(8,128)(2,1)} %get-tuple-element.67), channel_id=1, source_target_pairs={{0,12},{4,8},{8,4},{12,0},{16,28},{20,24},{24,20},{28,16},{1,13},{... | collective-permute-start | bytes 786440 | tf_op jit(solution)/shard_map/ppermute | solution.py:52
  34.9 14.8 %collective-permute-start.8 = (bf16[128,1024]{1,0:T(8,128)(2,1)}, bf16[128,1024]{1,0:T(8,128)(2,1)S(1)}, u32[]{:S(2)}, u32[]{:S(2)}) collective-permute-start(bf16[128,1024]{1,0:T(8,128)(2,1)} %get-tuple-element.66.refs_0_), channel_id=1, source_target_pairs={{0,8},{4,12},{8,0},{12,4},{16,24},{20,28},{24,16},{28,20},{1,9},{5... | collective-permute-start | bytes 786440 | tf_op jit(solution)/shard_map/ppermute | solution.py:52
  38.9 10.9 %collective-permute-start.6 = (bf16[1024,128]{1,0:T(8,128)(2,1)S(1)}, bf16[1024,128]{1,0:T(8,128)(2,1)S(1)}, u32[]{:S(2)}, u32[]{:S(2)}) collective-permute-start(bf16[1024,128]{1,0:T(8,128)(2,1)S(1)} %get-tuple-element.65.near), channel_id=1, source_target_pairs={{0,4},{4,0},{8,12},{12,8},{16,20},{20,16},{24,28},{28,24},{1,5},{5... | collective-permute-start | bytes 786440 | tf_op jit(solution)/shard_map/ppermute | solution.py:52
  44.7 27.6 %copy-start.1 = (bf16[512,128]{1,0:T(8,128)(2,1)S(1)}, bf16[512,128]{1,0:T(8,128)(2,1)}, u32[]{:S(2)}) copy-start(bf16[512,128]{1,0:T(8,128)(2,1)} %get-tuple-element.54.refs_0_) | copy-start | bytes 393220
  44.7 37.1 %all-to-all-start.1 = ((bf16[8,512,128]{2,1,0:T(8,128)(2,1)}), bf16[8,512,128]{2,1,0:T(8,128)(2,1)S(1)}, u32[]{:S(2)}, u32[]{:S(2)}) async-start(bf16[8,512,128]{2,1,0:T(8,128)(2,1)} %get-tuple-element.60), calls=%async_computation.1 | async-start | bytes 2097152 | tf_op jit(solution)/shard_map/all_to_all | solution.py:498
  52.9 2.0 %collective-permute-start.10 = (bf16[1024,256]{1,0:T(8,128)(2,1)S(1)}, bf16[1024,256]{1,0:T(8,128)(2,1)S(1)}, u32[]{:S(2)}, u32[]{:S(2)}) collective-permute-start(bf16[1024,256]{1,0:T(8,128)(2,1)S(1)} %weight_part.3), channel_id=1, source_target_pairs={{0,1},{1,0},{2,3},{3,2},{4,5},{5,4},{6,7},{7,6},{8,9},{9,8},{10,11... | collective-permute-start | bytes 1572872 | tf_op jit(solution)/shard_map/ppermute | solution.py:52
  55.0 8.6 %collective-permute-start.11 = (bf16[512,256]{1,0:T(8,128)(2,1)S(1)}, bf16[512,256]{1,0:T(8,128)(2,1)S(1)}, u32[]{:S(2)}, u32[]{:S(2)}) collective-permute-start(bf16[512,256]{1,0:T(8,128)(2,1)S(1)} %get-tuple-element.69), channel_id=1, source_target_pairs={{0,2},{1,3},{2,0},{3,1},{4,6},{5,7},{6,4},{7,5},{8,10},{9,11},{10,... | collective-permute-start | bytes 786440 | tf_op jit(solution)/shard_map/ppermute | solution.py:52
  56.5 11.5 %collective-permute-start.3 = (bf16[512,128]{1,0:T(8,128)(2,1)S(1)}, bf16[512,128]{1,0:T(8,128)(2,1)S(1)}, u32[]{:S(2)}, u32[]{:S(2)}) collective-permute-start(bf16[512,128]{1,0:T(8,128)(2,1)S(1)} %copy-done.9), channel_id=1, source_target_pairs={{0,4},{4,0},{8,12},{12,8},{16,20},{20,16},{24,28},{28,24},{1,5},{5... | collective-permute-start | bytes 393224 | tf_op jit(solution)/shard_map/ppermute | solution.py:52
  58.6 12.1 %collective-permute-start.4 = (bf16[512,128]{1,0:T(8,128)(2,1)S(1)}, bf16[512,128]{1,0:T(8,128)(2,1)S(1)}, u32[]{:S(2)}, u32[]{:S(2)}) collective-permute-start(bf16[512,128]{1,0:T(8,128)(2,1)S(1)} %copy-done.8), channel_id=1, source_target_pairs={{0,8},{4,12},{8,0},{12,4},{16,24},{20,28},{24,16},{28,20},{1,9},{5... | collective-permute-start | bytes 393224 | tf_op jit(solution)/shard_map/ppermute | solution.py:52
  60.0 12.3 %collective-permute-start.5 = (bf16[512,128]{1,0:T(8,128)(2,1)S(1)}, bf16[512,128]{1,0:T(8,128)(2,1)S(1)}, u32[]{:S(2)}, u32[]{:S(2)}) collective-permute-start(bf16[512,128]{1,0:T(8,128)(2,1)S(1)} %copy-done.7), channel_id=1, source_target_pairs={{0,12},{4,8},{8,4},{12,0},{16,28},{20,24},{24,20},{28,16},{1,13},{... | collective-permute-start | bytes 393224 | tf_op jit(solution)/shard_map/ppermute | solution.py:52
  63.6 14.7 %collective-permute-start.15 = (bf16[128,256]{1,0:T(8,128)(2,1)S(1)}, bf16[128,256]{1,0:T(8,128)(2,1)S(1)}, u32[]{:S(2)}, u32[]{:S(2)}) collective-permute-start(bf16[128,256]{1,0:T(8,128)(2,1)S(1)} %get-tuple-element.73), channel_id=1, source_target_pairs={{0,16},{4,20},{8,24},{12,28},{16,0},{20,4},{24,8},{28,12},{1,17},{... | collective-permute-start | bytes 196616 | tf_op jit(solution)/shard_map/ppermute | solution.py:52
  66.6 13.3 %collective-permute-start.12 = (bf16[128,256]{1,0:T(8,128)(2,1)S(1)}, bf16[128,256]{1,0:T(8,128)(2,1)S(1)}, u32[]{:S(2)}, u32[]{:S(2)}) collective-permute-start(bf16[128,256]{1,0:T(8,128)(2,1)S(1)} %get-tuple-element.70), channel_id=1, source_target_pairs={{0,4},{4,0},{8,12},{12,8},{16,20},{20,16},{24,28},{28,24},{1,5},{5... | collective-permute-start | bytes 196616 | tf_op jit(solution)/shard_map/ppermute | solution.py:52
  68.0 11.9 %collective-permute-start.13 = (bf16[128,256]{1,0:T(8,128)(2,1)S(1)}, bf16[128,256]{1,0:T(8,128)(2,1)S(1)}, u32[]{:S(2)}, u32[]{:S(2)}) collective-permute-start(bf16[128,256]{1,0:T(8,128)(2,1)S(1)} %get-tuple-element.71), channel_id=1, source_target_pairs={{0,20},{4,16},{8,28},{12,24},{16,4},{20,0},{24,12},{28,8},{1,21},{... | collective-permute-start | bytes 196616 | tf_op jit(solution)/shard_map/ppermute | solution.py:52
  78.3 4.5 %collective-permute-start.16 = (bf16[128,256]{1,0:T(8,128)(2,1)S(1)}, bf16[128,256]{1,0:T(8,128)(2,1)S(1)}, u32[]{:S(2)}, u32[]{:S(2)}) collective-permute-start(bf16[128,256]{1,0:T(8,128)(2,1)S(1)} %weight_scale.3.refs_0_), channel_id=1, source_target_pairs={{0,2},{1,3},{2,0},{3,1},{4,6},{5,7},{6,4},{7,5},{8,10},{9,11},{10,... | collective-permute-start | bytes 196616 | tf_op jit(solution)/shard_map/ppermute | solution.py:52
  79.9 4.3 %collective-permute-start.14 = (bf16[128,256]{1,0:T(8,128)(2,1)S(1)}, bf16[128,256]{1,0:T(8,128)(2,1)S(1)}, u32[]{:S(2)}, u32[]{:S(2)}) collective-permute-start(bf16[128,256]{1,0:T(8,128)(2,1)S(1)} %weight_scale.2.refs_4_), channel_id=1, source_target_pairs={{0,2},{1,3},{2,0},{3,1},{4,6},{5,7},{6,4},{7,5},{8,10},{9,11},{10,... | collective-permute-start | bytes 196616 | tf_op jit(solution)/shard_map/ppermute | solution.py:52
  81.3 3.5 %collective-permute-start.19 = (bf16[128,256]{1,0:T(8,128)(2,1)S(1)}, bf16[128,256]{1,0:T(8,128)(2,1)S(1)}, u32[]{:S(2)}, u32[]{:S(2)}) collective-permute-start(bf16[128,256]{1,0:T(8,128)(2,1)S(1)} %weight_scale.2.refs_4_), channel_id=1, source_target_pairs={{0,1},{1,0},{2,3},{3,2},{4,5},{5,4},{6,7},{7,6},{8,9},{9,8},{10,11... | collective-permute-start | bytes 196616 | tf_op jit(solution)/shard_map/ppermute | solution.py:52
  81.3 3.5 %collective-permute-start.17 = (bf16[128,256]{1,0:T(8,128)(2,1)S(1)}, bf16[128,256]{1,0:T(8,128)(2,1)S(1)}, u32[]{:S(2)}, u32[]{:S(2)}) collective-permute-start(bf16[128,256]{1,0:T(8,128)(2,1)S(1)} %weight_scale.3.refs_0_), channel_id=1, source_target_pairs={{0,1},{1,0},{2,3},{3,2},{4,5},{5,4},{6,7},{7,6},{8,9},{9,8},{10,11... | collective-permute-start | bytes 196616 | tf_op jit(solution)/shard_map/ppermute | solution.py:52
  84.2 1.3 %collective-permute-start.20 = (bf16[128,256]{1,0:T(8,128)(2,1)S(1)}, bf16[128,256]{1,0:T(8,128)(2,1)S(1)}, u32[]{:S(2)}, u32[]{:S(2)}) collective-permute-start(bf16[128,256]{1,0:T(8,128)(2,1)S(1)} %collective-permute-done.14.refs_6_), channel_id=1, source_target_pairs={{0,1},{1,0},{2,3},{3,2},{4,5},{5,4},{6,7},{7,6},{8,9},{9,8},{10,11... | collective-permute-start | bytes 196616 | tf_op jit(solution)/shard_map/ppermute | solution.py:52
  84.3 1.4 %collective-permute-start.18 = (bf16[128,256]{1,0:T(8,128)(2,1)S(1)}, bf16[128,256]{1,0:T(8,128)(2,1)S(1)}, u32[]{:S(2)}, u32[]{:S(2)}) collective-permute-start(bf16[128,256]{1,0:T(8,128)(2,1)S(1)} %collective-permute-done.16.refs_2_), channel_id=1, source_target_pairs={{0,1},{1,0},{2,3},{3,2},{4,5},{5,4},{6,7},{7,6},{8,9},{9,8},{10,11... | collective-permute-start | bytes 196616 | tf_op jit(solution)/shard_map/ppermute | solution.py:52
  (9 other events, 84.7 us)
